TPU v7x, 512 devices: a whole 4x4x16 slice. The times are simulated.
512 devices in a mesh: dp: 32 (over z_lo, x), mp: 16 (over z_hi, y, core).
Axes of the slice: x: 4, y: 4, z: 16 (z_hi: 2, z_lo: 8; z = z_hi * 8 + z_lo), core: 2. Of those that a mesh axis runs over, the one named last changes fastest.
Arguments:
- teacher_in: bfloat16 [2048, 16384], P('dp', 'mp'), may hold values from -6 to 6
- teacher_weight: bfloat16 [16384, 8192], P('mp', 'dp'), may hold values from -0.046875 to 0.046875
- student_in: bfloat16 [2048, 8192], P('dp', 'mp'), may hold values from -6 to 6
- projection: bfloat16 [8192, 8192], P('mp', 'dp'), may hold values from -0.0625 to 0.0625
- owner_order: int32 [2048], P('mp'), may hold values from 0 to 127, as said below
Outputs:
- projection_grad: float32 [8192, 8192], P('mp', 'dp')
- cosine: float32 [2048], P('mp')
Inputs may be any that keep to these rules, and one draw needn't show every extreme that they name: `owner_order`: each aligned block of 128 entries is a permutation of 0 to 127.
All inputs are finite; a program needn't handle non-finite values.
Results may differ from a plain program's by a relative error of at most 0.025.
Values may be sent and summed in bfloat16 or wider, within the bound.
No kernel may reach another device: no remote copies, remote signals or barrier semaphores. Data moves between devices by JAX's collectives and lax.ppermute only.
A program may use at most 64 MiB of HBM per device.

v0:
```python
import jax
import jax.numpy as jnp
from jax import lax
from jax.sharding import PartitionSpec as P


def shards(teacher_in, teacher_weight, student_in, projection, owner_order):
    teacher_all = lax.all_gather(teacher_in, "dp", axis=0, tiled=True)
    student_all = lax.all_gather(student_in, "dp", axis=0, tiled=True)
    groups = lax.axis_size("mp")
    total_rows = teacher_all.shape[0]
    block_len = total_rows // groups
    sub_len = block_len // groups
    slab = teacher_all
    owned = lax.psum_scatter(
        jnp.dot(slab, teacher_weight, preferred_element_type=jnp.float32).astype(jnp.bfloat16),
        "mp",
        scatter_dimension=0,
        tiled=True,
    )
    picked = owned[owner_order].reshape(groups, sub_len, owned.shape[1])
    arrived = lax.all_to_all(picked, "mp", split_axis=0, concat_axis=0, tiled=True)
    target = arrived.reshape(block_len, owned.shape[1])
    slab = student_all
    student_out = lax.psum_scatter(
        jnp.dot(slab, projection, preferred_element_type=jnp.float32).astype(jnp.bfloat16),
        "mp",
        scatter_dimension=0,
        tiled=True,
    ).astype(jnp.float32)
    target_f = target.astype(jnp.float32)
    inner, sq_student, sq_target = lax.psum(
        (
            jnp.sum(student_out * target_f, axis=1),
            jnp.sum(student_out * student_out, axis=1),
            jnp.sum(target_f * target_f, axis=1),
        ),
        "dp",
    )
    inv_student = lax.rsqrt(sq_student + 1e-06)
    inv_target = lax.rsqrt(sq_target + 1e-06)
    cosine = inner * inv_student * inv_target
    scale = -1.0 / total_rows
    grad_out = scale * (
        target_f * (inv_student * inv_target)[:, None]
        - (inner * inv_target * inv_student**3)[:, None] * student_out
    )
    grad_out = grad_out.astype(jnp.bfloat16)
    projection_grad = lax.dot_general(
        student_all,
        lax.all_gather(grad_out, "mp", axis=0, tiled=True),
        (((0,), (0,)), ((), ())),
        preferred_element_type=jnp.float32,
    )
    return (projection_grad, cosine)


def solution(mesh):
    return jax.shard_map(
        shards,
        mesh=mesh,
        in_specs=(P("dp", "mp"), P("mp", "dp"), P("dp", "mp"), P("mp", "dp"), P("mp")),
        out_specs=(P("mp", "dp"), P("mp")),
        check_vma=False,
    )
```

profile of v0, /device:TPU:1, one launch (start us, length us, event | category | flops | bytes accessed | tf_op | source)
XLA Modules:
  0.0 881.9 jit_solution(8804667251350406931)
XLA Ops:
  7.2 0.0 all-gather.4.cloned.1.call-start
  7.2 0.7 all-gather.4.cloned.1.call-update
  7.9 0.0 all-gather.6.cloned.1.call-start
  8.0 0.7 all-gather.6.cloned.1.call-update
  8.7 0.0 reduce-scatter.3.cloned.1.call-start
  8.7 214.9 %all-gather.4.cloned.1.call-done = bf16[2048,1024]{1,0:T(8,128)(2,1)} async-done(((bf16[64,1024]{1,0:T(8,128)(2,1)}), bf16[2048,1024]{1,0:T(8,128)(2,1)}) %all-gather.4.cloned.1.call-update) | async-done | bytes 4194320 | tf_op jit(solution)/shard_map/all_gather | solution.py:8
  223.6 4.4 convolution_convert_fusion.1
  228.1 0.0 reduce-scatter.5.cloned.1.call-start
  228.1 218.9 %all-gather.6.cloned.1.call-done = bf16[2048,512]{1,0:T(8,128)(2,1)} async-done(((bf16[64,512]{1,0:T(8,128)(2,1)}), bf16[2048,512]{1,0:T(8,128)(2,1)}) %all-gather.6.cloned.1.call-update) | async-done | bytes 2097168 | tf_op jit(solution)/shard_map/all_gather | solution.py:9
  447.0 3.3 convolution_convert_fusion
  450.3 0.0 all-gather.8.cloned.1.call-start
  450.4 126.4 %reduce-scatter.3.cloned.1.call-done = bf16[128,256]{1,0:T(8,128)(2,1)} async-done(((bf16[2048,256]{1,0:T(8,128)(2,1)}), bf16[128,256]{1,0:T(8,128)(2,1)}) %reduce-scatter.3.cloned.1.call-update) | async-done | bytes 65552 | tf_op jit(solution)/shard_map/reduce_scatter | solution.py:15
  576.8 1.6 gather_fusion
  578.4 20.2 %all_to_all.5 = bf16[16,8,256]{2,1,0:T(8,128)(2,1)S(1)} all-to-all(bf16[16,8,256]{2,1,0:T(8,128)(2,1)S(1)} %bitcast.23), channel_id=1, replica_groups=mesh['dp'=32,'mp'=16] {'mp'}, dimensions={0} | all-to-all | bytes 131072 | tf_op jit(solution)/shard_map/all_to_all | solution.py:22
  598.5 0.1 fusion.4
  598.6 0.1 reduce_sum.31
  598.7 81.6 %reduce-scatter.5.cloned.1.call-done = bf16[128,256]{1,0:T(8,128)(2,1)} async-done(((bf16[2048,256]{1,0:T(8,128)(2,1)}), bf16[128,256]{1,0:T(8,128)(2,1)}) %reduce-scatter.5.cloned.1.call-update) | async-done | bytes 65552 | tf_op jit(solution)/shard_map/reduce_scatter | solution.py:25
  680.3 0.9 fusion.5
  681.3 100.7 %all-reduce = (f32[128]{0:T(128)S(1)}, f32[128]{0:T(128)S(1)}, f32[128]{0:T(128)S(1)}) all-reduce(f32[128]{0:T(128)S(1)} %get-tuple-element.7, f32[128]{0:T(128)S(1)} %get-tuple-element.6, f32[128]{0:T(128)S(1)} %reduce_sum.31), channel_id=1, replica_groups=mesh['dp'=32,'mp'=16] {'dp'}, use_global_device_ids=true, to_apply=%region_7.0 | all-reduce | flops 384 | bytes 3072 | tf_op jit(solution)/shard_map/psum | solution.py:32
  782.0 0.5 multiply_multiply_fusion.1
  782.5 1.6 fusion.3
  784.1 88.3 %all-gather.8.cloned.1.call-done = bf16[2048,256]{1,0:T(8,128)(2,1)} async-done(((bf16[128,256]{1,0:T(8,128)(2,1)}), bf16[2048,256]{1,0:T(8,128)(2,1)}) %all-gather.8.cloned.1.call-update) | async-done | bytes 1048592 | tf_op jit(solution)/shard_map/all_gather | solution.py:51
  872.4 1.9 convolution_bitcast_fusion
  874.3 1.0 copy.8
  (13 shorter events, 0.1 us)
Async XLA Ops:
  7.2 216.4 %copy-start = (bf16[1024,256]{1,0:T(8,128)(2,1)S(1)}, bf16[1024,256]{1,0:T(8,128)(2,1)}, u32[]{:S(2)}) copy-start(bf16[1024,256]{1,0:T(8,128)(2,1)} %param.6) | copy-start | bytes 1572868
  7.2 216.4 %all-gather.4.cloned.1.call-start = ((), (), s32[]{:S(2)}) async-start(), calls=%async_computation.3 | async-start | bytes 4325376 | tf_op jit(solution)/shard_map/all_gather | solution.py:8
  7.9 439.1 %all-gather.6.cloned.1.call-start = ((), (), s32[]{:S(2)}) async-start(), calls=%async_computation.5 | async-start | bytes 2162688 | tf_op jit(solution)/shard_map/all_gather | solution.py:9
  8.7 438.3 %copy-start.2 = (bf16[512,256]{1,0:T(8,128)(2,1)S(1)}, bf16[512,256]{1,0:T(8,128)(2,1)}, u32[]{:S(2)}) copy-start(bf16[512,256]{1,0:T(8,128)(2,1)} %param.8) | copy-start | bytes 786436
  8.7 568.1 %reduce-scatter.3.cloned.1.call-start = ((), (), s32[]{:S(2)}) async-start(), calls=%async_computation.4 | async-start | bytes 1114112 | tf_op jit(solution)/shard_map/reduce_scatter | solution.py:15
  228.1 222.3 %copy-start.3 = (s32[128]{0:T(128)S(1)}, s32[128]{0:T(128)}, u32[]{:S(2)}) copy-start(s32[128]{0:T(128)} %param.9) | copy-start | bytes 1540
  228.1 452.2 %reduce-scatter.5.cloned.1.call-start = ((), (), s32[]{:S(2)}) async-start(), calls=%async_computation.6 | async-start | bytes 1114112 | tf_op jit(solution)/shard_map/reduce_scatter | solution.py:25
  450.3 422.1 %copy-start.1 = (bf16[2048,512]{1,0:T(8,128)(2,1)S(1)}, bf16[2048,512]{1,0:T(8,128)(2,1)}, u32[]{:S(2)}) copy-start(bf16[2048,512]{1,0:T(8,128)(2,1)} %all-gather.6.cloned.1.call-done) | copy-start | bytes 6291460
  450.3 422.1 %all-gather.8.cloned.1.call-start = ((), (), s32[]{:S(2)}) async-start(), calls=%async_computation.7 | async-start | bytes 1114112 | tf_op jit(solution)/shard_map/all_gather | solution.py:51
Sparse Core Ops, SparseCore 0:
  10.1 213.4 all-gather.3
  225.7 221.2 all-gather.5
  451.7 125.0 reduce-scatter.2
  582.0 98.2 reduce-scatter.4
  784.2 88.1 all-gather.7
where the time goes:
time: 882 us
  waiting for transfers between devices  731 us (83%)
  blocking collectives  121 us (14%)
  between operations  13.8 us (2%)
  matrix products  9.64 us (1%)
    all_gather x1, waiting for transfers between devices, shards(): student_all = lax.all_gather(student_in, 'dp', axis=0, tiled=True)  219 us
    all_gather x1, waiting for transfers between devices, shards(): teacher_all = lax.all_gather(teacher_in, 'dp', axis=0, tiled=True)  215 us
    reduce_scatter x1, waiting for transfers between devices, shards(): lax.psum_scatter(jnp.dot(slab, teacher_weight, preferred_element_type=jnp...  126 us
    psum x1, blocking collectives, shards(): lax.psum((jnp.sum(student_out * target_f, axis=1), jnp.sum(student_out *...  101 us
    all_gather x1, waiting for transfers between devices, shards(): lax.all_gather(grad_out, 'mp', axis=0, tiled=True)  88.3 us
    reduce_scatter x1, waiting for transfers between devices, shards(): lax.psum_scatter(jnp.dot(slab, projection, preferred_element_type=jnp.flo...  81.6 us
    all_to_all x1, blocking collectives, shards(): lax.all_to_all(picked, 'mp', split_axis=0, concat_axis=0, tiled=True)  20.2 us
  transfers between devices with their start and end apart: 5, of which 5 were waited for; matrix products, arithmetic and copies ran while one was open for 1% of the time, Pallas kernels for 0%

commit v1 on v0

v1 whole, which is shorter than its diff:
```python
import jax
import jax.numpy as jnp
from jax import lax
from jax.sharding import Mesh, PartitionSpec as P

F32 = jnp.float32
BF16 = jnp.bfloat16
DP = ("z2", "z1", "z0", "x1", "x0")
MP = ("zh", "y", "c")


def spread(value, axis):
    count = lax.axis_size(axis)
    copies = jnp.broadcast_to(value[None], (count,) + value.shape)
    return lax.all_to_all(copies, axis, split_axis=0, concat_axis=0, tiled=True)


def reduce_over(value, axis):
    pieces = lax.all_to_all(value, axis, split_axis=0, concat_axis=0, tiled=True)
    return jnp.sum(pieces.astype(F32), axis=0)


def shards(teacher_in, teacher_weight, student_in, projection, owner_order):
    rows, teacher_width = teacher_in.shape
    student_width = student_in.shape[1]
    out_width = projection.shape[1]
    groups = 16
    block = owner_order.shape[0]
    sub = block // groups
    total_rows = groups * block

    orders = lax.all_gather(
        jnp.broadcast_to(owner_order[:, None], (block, block)), MP, axis=0, tiled=False
    )
    pick = (orders == lax.broadcasted_iota(jnp.int32, orders.shape, 2)).astype(BF16)

    both = jnp.concatenate([teacher_in, student_in], axis=1)
    for axis in ("z2", "z1", "z0", ("x1", "x0")):
        both = spread(both, axis)
    both = both.reshape(total_rows, teacher_width + student_width)
    teacher_all = both[:, :teacher_width]
    student_all = both[:, teacher_width:]

    teacher_part = jnp.dot(teacher_all, teacher_weight, preferred_element_type=F32).astype(BF16)
    student_part = jnp.dot(student_all, projection, preferred_element_type=F32).astype(BF16)

    def by_block(part):
        part = part.reshape(2, 2, 2, 2, 2, rows, out_width)
        return part.transpose(4, 3, 2, 0, 1, 5, 6).reshape(groups, block, out_width)

    teacher_rows = jnp.einsum(
        "bqk,bkn->bqn", pick, by_block(teacher_part), preferred_element_type=F32
    ).astype(BF16)
    teacher_rows = teacher_rows.reshape(groups, groups, sub, out_width)
    teacher_rows = teacher_rows.transpose(1, 0, 2, 3).reshape(groups, block, out_width)
    sums = jnp.stack([teacher_rows, by_block(student_part)])
    sums = sums.reshape(2, 2, 4, 2, block, out_width).transpose(3, 2, 1, 0, 4, 5)
    sums = reduce_over(sums, "c").astype(BF16)
    sums = reduce_over(sums, "y").astype(BF16)
    sums = reduce_over(sums, "zh")
    target = sums[0].astype(BF16).astype(F32)
    student_out = sums[1]

    stats = jnp.stack(
        [
            jnp.sum(student_out * target, axis=1),
            jnp.sum(student_out * student_out, axis=1),
            jnp.sum(target * target, axis=1),
        ]
    )
    stats = jnp.sum(spread(stats, ("x1", "x0")), axis=0)
    stats = jnp.sum(spread(stats, ("z2", "z1", "z0")), axis=0)
    inner, sq_student, sq_target = stats[0], stats[1], stats[2]
    inv_student = lax.rsqrt(sq_student + 1e-06)
    inv_target = lax.rsqrt(sq_target + 1e-06)
    cosine = inner * inv_student * inv_target
    scale = -1.0 / total_rows
    grad_out = scale * (
        target * (inv_student * inv_target)[:, None]
        - (inner * inv_target * inv_student**3)[:, None] * student_out
    )
    grad_out = grad_out.astype(BF16)
    for axis in ("zh", "y", "c"):
        grad_out = spread(grad_out, axis)
    grad_out = grad_out.reshape(2, 2, 2, 2, 2, rows, out_width)
    grad_out = grad_out.transpose(0, 4, 2, 1, 3, 5, 6).reshape(total_rows, out_width)
    projection_grad = lax.dot_general(
        student_all, grad_out, (((0,), (0,)), ((), ())), preferred_element_type=F32
    )
    return (projection_grad, cosine)


def solution(mesh):
    fine = Mesh(mesh.devices.reshape(2, 2, 2, 2, 2, 2, 4, 2), DP + MP)
    return jax.shard_map(
        shards,
        mesh=fine,
        in_specs=(P(DP, MP), P(MP, DP), P(DP, MP), P(MP, DP), P(MP)),
        out_specs=(P(MP, DP), P(MP)),
        check_vma=False,
    )
```

time: 882 us -> 279 us (0.32)
  waiting for transfers between devices: 731 us -> 24.3 us
  blocking collectives: 121 us -> 228 us
  between operations: 13.8 us -> 0.81 us
    all_gather x3 -> x0, waiting for transfers between devices: 522 us -> none  [the longest x1 219 us: shards(): student_all = lax.all_gather(student_in, 'dp', axis=0, tiled=True)]
    reduce_scatter x2 -> x0, waiting for transfers between devices: 208 us -> none  [the longest x1 126 us: shards(): lax.psum_scatter(jnp.dot(slab, teacher_weight, preferred_element_type=jnp...]
    all_to_all x1 -> x11, blocking collectives: 20.2 us -> 183 us  [the longest x8 134 us: spread(): return lax.all_to_all(copies, axis, split_axis=0, concat_axis=0, tiled=True)]
    psum x1 -> x0, blocking collectives: 101 us -> none  [shards(): lax.psum((jnp.sum(student_out * target_f, axis=1), jnp.sum(student_out *...]
    all_gather x0 -> x1, blocking collectives: none -> 45.7 us  [shards(): lax.all_gather(jnp.broadcast_to(owner_order[:, None], (block, block)), MP...]
    all_to_all x0 -> x1, waiting for transfers between devices: none -> 24.3 us  [spread(): return lax.all_to_all(copies, axis, split_axis=0, concat_axis=0, tiled=True)]
  transfers between devices with their start and end apart: 5 -> 1, of which waited for: 5 -> 1; matrix products, arithmetic and copies ran while one was open for 1% -> 0% of each run, Pallas kernels for 0% -> 0%
where the time goes in v1:
time: 279 us; the launch traced here: 278 us
  blocking collectives  228 us (82%)
  waiting for transfers between devices  24.3 us (9%)
  matrix products  9.36 us (3%)
  local copies, waits for them, and re-layouts  5.96 us (2%)
  starting transfers between devices  5.37 us (2%)
  other arithmetic  3.96 us (1%)
    all_to_all x8, blocking collectives, spread(): return lax.all_to_all(copies, axis, split_axis=0, concat_axis=0, tiled=True)  134 us
    all_to_all x3, blocking collectives, reduce_over(): lax.all_to_all(value, axis, split_axis=0, concat_axis=0, tiled=True)  48.1 us
    all_gather x1, blocking collectives, shards(): lax.all_gather(jnp.broadcast_to(owner_order[:, None], (block, block)), MP...  45.7 us
    all_to_all x1, waiting for transfers between devices, spread(): return lax.all_to_all(copies, axis, split_axis=0, concat_axis=0, tiled=True)  24.3 us
  transfers between devices with their start and end apart: 1, of which 1 were waited for; matrix products, arithmetic and copies ran while one was open for 0% of the time, Pallas kernels for 0%

profile of v1, /device:TPU:1, one launch (start us, length us, event | category | flops | bytes accessed | tf_op | source)
XLA Modules:
  0.0 278.1 jit_solution(9311729291427595286)
XLA Ops:
  0.6 1.0 pad_maximum_fusion
  1.7 31.0 %all_to_all.60 = bf16[2,64,1536]{2,1,0:T(8,128)(2,1)S(1)} all-to-all(bf16[2,64,1536]{2,1,0:T(8,128)(2,1)S(1)} %broadcast_in_dim.20), channel_id=1, replica_groups=mesh['z2'=2,'z1'=2,'z0'=2,'x1'=2,'x0'=2,'zh'=2,'y'=4,'c'=2] {'z2'}, dimensions={0} | all-to-all | bytes 786432 | tf_op jit(solution)/shard_map/all_to_all | solution.py:15
  32.8 20.2 %all_to_all.61 = bf16[2,2,64,1536]{3,2,1,0:T(8,128)(2,1)S(1)} all-to-all(bf16[2,2,64,1536]{3,2,1,0:T(8,128)(2,1)S(1)} %broadcast_in_dim.21), channel_id=1, replica_groups=mesh['z2'=2,'z1'=2,'z0'=2,'x1'=2,'x0'=2,'zh'=2,'y'=4,'c'=2] {'z1'}, dimensions={0} | all-to-all | bytes 1572864 | tf_op jit(solution)/shard_map/all_to_all | solution.py:15
  53.2 21.3 %all_to_all.62 = bf16[2,2,2,64,1536]{4,3,2,1,0:T(8,128)(2,1)S(1)} all-to-all(bf16[2,2,2,64,1536]{4,3,2,1,0:T(8,128)(2,1)S(1)} %broadcast_in_dim.22), channel_id=1, replica_groups=mesh['z2'=2,'z1'=2,'z0'=2,'x1'=2,'x0'=2,'zh'=2,'y'=4,'c'=2] {'z0'}, dimensions={0} | all-to-all | bytes 3145728 | tf_op jit(solution)/shard_map/all_to_all | solution.py:15
  74.5 3.4 %broadcast_in_dim.23 = bf16[4,2,2,2,64,1536]{5,4,3,2,1,0:T(8,128)(2,1)} broadcast(bf16[2,2,2,64,1536]{4,3,2,1,0:T(8,128)(2,1)S(1)} %all_to_all.62), dimensions={1,2,3,4,5} | broadcast | bytes 7864320 | tf_op jit(solution)/shard_map/broadcast_in_dim | solution.py:14
  77.9 5.4 %all-to-all-start.3 = ((bf16[4,2,2,2,64,1536]{5,4,3,2,1,0:T(8,128)(2,1)}), bf16[4,2,2,2,64,1536]{5,4,3,2,1,0:T(8,128)(2,1)}, u32[]{:S(2)}, u32[]{:S(2)}) async-start(bf16[4,2,2,2,64,1536]{5,4,3,2,1,0:T(8,128)(2,1)} %broadcast_in_dim.23), calls=%async_computation.3 | async-start | bytes 12582912 | tf_op jit(solution)/shard_map/all_to_all | solution.py:15
  83.2 45.7 %all-gather.1 = s32[16,1,128]{2,1,0:T(1,128)S(1)} all-gather(s32[1,1,128]{2,1,0:T(1,128)S(1)} %bitcast.57), channel_id=3, replica_groups=mesh['z2'=2,'z1'=2,'z0'=2,'x1'=2,'x0'=2,'zh'=2,'y'=4,'c'=2] {'zh','y','c'}, dimensions={0}, use_global_device_ids=true | all-gather | bytes 8704 | tf_op jit(solution)/shard_map/all_gather | solution.py:32
  129.0 24.3 %all-to-all-done.3 = bf16[4,2,2,2,64,1536]{5,4,3,2,1,0:T(8,128)(2,1)} async-done(((bf16[4,2,2,2,64,1536]{5,4,3,2,1,0:T(8,128)(2,1)}), bf16[4,2,2,2,64,1536]{5,4,3,2,1,0:T(8,128)(2,1)}, u32[]{:S(2)}, u32[]{:S(2)}) %all-to-all-start.3) | async-done | bytes 6291488 | tf_op jit(solution)/shard_map/all_to_all | solution.py:15
  153.3 3.4 %fusion.2 = bf16[2048,256]{1,0:T(8,128)(2,1)S(1)} fusion(bf16[1024,256]{1,0:T(8,128)(2,1)S(1)} %copy-done, bf16[2048,1536]{1,0:T(8,128)(2,1)} %bitcast), kind=kOutput, calls=%fused_computation.3 | convolution fusion | flops 1074266112 | bytes 5767168 | tf_op jit(solution)/shard_map/dot_general | solution.py:44
  156.8 0.5 fusion.8
  157.4 0.3 copy-done.2
  157.7 2.3 convolution_convert_fusion
  160.5 7.3 %all_to_all.63 = bf16[2,4,2,2,128,256]{5,4,1,2,3,0:T(8,128)(2,1)S(1)} all-to-all(bf16[2,4,2,2,128,256]{5,4,1,2,3,0:T(8,128)(2,1)S(1)} %copy.50), channel_id=1, replica_groups=mesh['z2'=2,'z1'=2,'z0'=2,'x1'=2,'x0'=2,'zh'=2,'y'=4,'c'=2] {'c'}, dimensions={0} | all-to-all | bytes 4194304 | tf_op jit(solution)/shard_map/all_to_all | solution.py:19
  167.8 1.7 reduce_sum.78
  169.5 1.3 copy.52
  170.8 18.2 %all_to_all.64 = bf16[4,2,2,128,256]{4,3,1,2,0:T(8,128)(2,1)S(1)} all-to-all(bf16[4,2,2,128,256]{4,3,1,2,0:T(8,128)(2,1)S(1)} %copy.52), channel_id=1, replica_groups=mesh['z2'=2,'z1'=2,'z0'=2,'x1'=2,'x0'=2,'zh'=2,'y'=4,'c'=2] {'y'}, dimensions={0} | all-to-all | bytes 2097152 | tf_op jit(solution)/shard_map/all_to_all | solution.py:19
  189.3 22.6 %all_to_all.65 = bf16[2,2,128,256]{3,2,1,0:T(8,128)(2,1)S(1)} all-to-all(bf16[2,2,128,256]{3,2,1,0:T(8,128)(2,1)S(1)} %copy.54), channel_id=1, replica_groups=mesh['z2'=2,'z1'=2,'z0'=2,'x1'=2,'x0'=2,'zh'=2,'y'=4,'c'=2] {'zh'}, dimensions={0} | all-to-all | bytes 524288 | tf_op jit(solution)/shard_map/all_to_all | solution.py:19
  212.1 6.5 %all_to_all.66 = f32[4,3,128]{2,1,0:T(4,128)S(1)} all-to-all(f32[4,3,128]{2,1,0:T(4,128)S(1)} %broadcast_in_dim.24), channel_id=1, replica_groups=mesh['z2'=2,'z1'=2,'z0'=2,'x1'=2,'x0'=2,'zh'=2,'y'=4,'c'=2] {'x1','x0'}, dimensions={0} | all-to-all | bytes 12288 | tf_op jit(solution)/shard_map/all_to_all | solution.py:15
  218.6 21.5 %all_to_all.67 = f32[8,3,128]{2,1,0:T(4,128)S(1)} all-to-all(f32[8,3,128]{2,1,0:T(4,128)S(1)} %broadcast_in_dim.25), channel_id=1, replica_groups=mesh['z2'=2,'z1'=2,'z0'=2,'x1'=2,'x0'=2,'zh'=2,'y'=4,'c'=2] {'z2','z1','..., dimensions={0} | all-to-all | bytes 24576 | tf_op jit(solution)/shard_map/all_to_all | solution.py:15
  240.2 0.5 fusion.17
  240.8 14.4 %all_to_all.68 = bf16[2,128,256]{2,1,0:T(8,128)(2,1)S(1)} all-to-all(bf16[2,128,256]{2,1,0:T(8,128)(2,1)S(1)} %broadcast_in_dim.27), channel_id=1, replica_groups=mesh['z2'=2,'z1'=2,'z0'=2,'x1'=2,'x0'=2,'zh'=2,'y'=4,'c'=2] {'zh'}, dimensions={0} | all-to-all | bytes 262144 | tf_op jit(solution)/shard_map/all_to_all | solution.py:15
  255.3 9.3 %all_to_all.69 = bf16[4,2,128,256]{3,2,1,0:T(8,128)(2,1)S(1)} all-to-all(bf16[4,2,128,256]{3,2,1,0:T(8,128)(2,1)S(1)} %broadcast_in_dim.28), channel_id=1, replica_groups=mesh['z2'=2,'z1'=2,'z0'=2,'x1'=2,'x0'=2,'zh'=2,'y'=4,'c'=2] {'y'}, dimensions={0} | all-to-all | bytes 1048576 | tf_op jit(solution)/shard_map/all_to_all | solution.py:15
  264.7 10.1 %all_to_all.70 = bf16[2,4,2,128,256]{4,3,2,1,0:T(8,128)(2,1)S(1)} all-to-all(bf16[2,4,2,128,256]{4,3,2,1,0:T(8,128)(2,1)S(1)} %broadcast_in_dim.29), channel_id=1, replica_groups=mesh['z2'=2,'z1'=2,'z0'=2,'x1'=2,'x0'=2,'zh'=2,'y'=4,'c'=2] {'c'}, dimensions={0} | all-to-all | bytes 2097152 | tf_op jit(solution)/shard_map/all_to_all | solution.py:15
  274.9 3.1 %fusion.5 = f32[512,256]{1,0:T(8,128)} fusion(bf16[2048,256]{1,0:T(8,128)(2,1)S(1)} %bitcast.50, bf16[2048,1536]{1,0:T(8,128)(2,1)} %bitcast), kind=kOutput, calls=%fused_computation.5 | convolution fusion | flops 536870912 | bytes 3670016 | tf_op jit(solution)/shard_map/dot_general | solution.py:87
  (27 shorter events, 1.7 us)
Async XLA Ops:
  0.6 152.6 %copy-start = (bf16[1024,256]{1,0:T(8,128)(2,1)S(1)}, bf16[1024,256]{1,0:T(8,128)(2,1)}, u32[]{:S(2)}) copy-start(bf16[1024,256]{1,0:T(8,128)(2,1)} %param.6) | copy-start | bytes 1572868
  77.9 5.4 %copy-start.1 = (s32[128]{0:T(128)S(1)}, s32[128]{0:T(128)}, u32[]{:S(2)}) copy-start(s32[128]{0:T(128)} %param.9) | copy-start | bytes 1540
  77.9 75.4 %all-to-all-start.3 = ((bf16[4,2,2,2,64,1536]{5,4,3,2,1,0:T(8,128)(2,1)}), bf16[4,2,2,2,64,1536]{5,4,3,2,1,0:T(8,128)(2,1)}, u32[]{:S(2)}, u32[]{:S(2)}) async-start(bf16[4,2,2,2,64,1536]{5,4,3,2,1,0:T(8,128)(2,1)} %broadcast_in_dim.23), calls=%async_computation.3 | async-start | bytes 12582912 | tf_op jit(solution)/shard_map/all_to_all | solution.py:15
  156.8 1.0 copy-start.2

commit v2 on v1

v2 whole, which is shorter than its diff:
```python
import jax
import jax.numpy as jnp
from jax import lax
from jax.sharding import Mesh, PartitionSpec as P

F32 = jnp.float32
BF16 = jnp.bfloat16
DP = ("z2", "z1", "z0", "x")
MP = ("zh", "y1", "y0", "c")
SWAP = [(0, 1), (1, 0)]
UP = [(i, (i + 1) % 4) for i in range(4)]
DOWN = [(i, (i - 1) % 4) for i in range(4)]


def together(*values):
    return lax.optimization_barrier(values)


def swap_in(value, axis):
    other = lax.ppermute(value, axis, SWAP)
    first = lax.axis_index(axis) == 0
    both = jnp.stack([jnp.where(first, value, other), jnp.where(first, other, value)])
    return both.reshape((-1,) + value.shape[1:])


def spread(value, axis):
    count = lax.axis_size(axis)
    copies = jnp.broadcast_to(value[None], (count,) + value.shape)
    return lax.all_to_all(copies, axis, split_axis=0, concat_axis=0, tiled=True)


def neighbours(value):
    return lax.ppermute(value, "x", DOWN), lax.ppermute(value, "x", UP)


def opposite(after, before):
    half = after.shape[0] // 2
    return jnp.concatenate(
        [lax.ppermute(before[:half], "x", UP), lax.ppermute(after[half:], "x", DOWN)]
    )


def halve(value, axis):
    me = lax.axis_index(axis)
    other = lax.ppermute(
        lax.dynamic_index_in_dim(value, 1 - me, keepdims=False).astype(BF16), axis, SWAP
    )
    mine = lax.dynamic_index_in_dim(value, me, keepdims=False)
    return mine.astype(F32) + other.astype(F32)


def shards(teacher_in, teacher_weight, student_in, projection, owner_order):
    rows, teacher_width = teacher_in.shape
    out_width = projection.shape[1]
    groups = 16
    block = owner_order.shape[0]
    sub = block // groups
    total_rows = groups * block
    x = lax.axis_index("x")
    z0 = lax.axis_index("z0")
    part_width = teacher_width // 2

    def column_half(which):
        return lax.dynamic_slice_in_dim(teacher_in, which * part_width, part_width, 1)

    other = lax.ppermute(column_half(1 - z0), "z0", SWAP)
    mine = column_half(z0)
    orders = swap_in(owner_order[None], "c")
    other, orders = together(other, orders)
    teacher = jnp.concatenate([jnp.where(z0 == 0, mine, other), jnp.where(z0 == 0, other, mine)])
    teacher = swap_in(teacher, "z2")
    orders = swap_in(orders, "y0")
    teacher, orders = together(teacher, orders)
    teacher = swap_in(teacher, "z1")
    orders = swap_in(orders, "y1")

    teacher, student, orders, teacher_weight = together(
        teacher, student_in, orders, teacher_weight
    )
    after, before = neighbours(teacher)
    student = swap_in(student, "z2")
    orders = swap_in(orders, "zh")
    student = swap_in(student, "z1")
    weight_other = lax.ppermute(
        lax.dynamic_slice_in_dim(teacher_weight, (1 - z0) * part_width, part_width, 0), "z0", SWAP
    )
    weight_mine = lax.dynamic_slice_in_dim(teacher_weight, z0 * part_width, part_width, 0)
    after, before, student = together(after, before, student)
    far = opposite(after, before)
    teacher_blocks = (teacher, after, far, before)
    student = swap_in(student, "z0")
    student_after, student_before = neighbours(student)
    student_blocks = (student, student_after, opposite(student_after, student_before), student_before)

    pick = orders[:, :, None] == lax.broadcasted_iota(jnp.int32, (groups, block, block), 2)
    pick = pick.astype(BF16)

    def project(blocks, weight, order):
        width = weight.shape[1]
        part = jnp.zeros((4, total_rows // 4, width), BF16)
        for step, one in enumerate(blocks):
            product = jnp.dot(one, weight, preferred_element_type=F32).astype(BF16)
            part = lax.dynamic_update_slice_in_dim(part, product[None], (x + step) % 4, 0)
        part = part.reshape(2, 2, 2, 2, 2, rows, width)
        return part.transpose(order + (0, 1, 5, 6)).reshape(groups, block, width)

    def by_core(part):
        return part.reshape(2, 4, 2, block, -1).transpose(2, 1, 0, 3, 4)

    def reduced(part):
        part = lax.all_to_all(part, ("y1", "y0"), split_axis=0, concat_axis=0, tiled=True)
        part = jnp.sum(part.astype(F32), axis=0)
        other = lax.ppermute(part.astype(BF16), "zh", SWAP)
        return (part + other.astype(F32)).reshape(2 * block, out_width)

    weights = jnp.concatenate([weight_mine, weight_other], axis=1)
    teacher_rows = jnp.einsum(
        "bqk,bkn->bqn",
        pick,
        project(teacher_blocks, weights, (3, 2, 4)),
        preferred_element_type=F32,
    ).astype(BF16)
    teacher_rows = teacher_rows.reshape(groups, groups, sub, 2 * out_width)
    teacher_rows = teacher_rows.transpose(1, 0, 2, 3).reshape(groups, block, 2 * out_width)
    teacher_rows = halve(by_core(teacher_rows), "c")
    arrived = lax.ppermute(teacher_rows[..., out_width:].astype(BF16), "z0", SWAP)
    teacher_rows = teacher_rows[..., :out_width] + arrived.astype(F32)
    target = reduced(teacher_rows.astype(BF16)).astype(BF16).astype(F32)

    student_rows = by_core(project(student_blocks, projection, (4, 3, 2)))
    student_out = reduced(halve(student_rows, "c").astype(BF16))

    stats = jnp.stack(
        [
            jnp.sum(student_out * target, axis=1),
            jnp.sum(student_out * student_out, axis=1),
            jnp.sum(target * target, axis=1),
        ]
    )
    stats = jnp.sum(spread(stats, "x"), axis=0)
    stats = jnp.sum(spread(stats, ("z2", "z1", "z0")), axis=0)
    inner, sq_student, sq_target = stats[0], stats[1], stats[2]
    inv_student = lax.rsqrt(sq_student + 1e-06)
    inv_target = lax.rsqrt(sq_target + 1e-06)
    cosine = inner * inv_student * inv_target
    scale = -1.0 / total_rows
    grad_out = scale * (
        target * (inv_student * inv_target)[:, None]
        - (inner * inv_target * inv_student**3)[:, None] * student_out
    )
    grad_out = grad_out.astype(BF16)
    cosine = lax.dynamic_slice_in_dim(cosine, lax.axis_index("zh") * block, block)
    grad_out = spread(grad_out, ("y1", "y0"))
    grad_out = swap_in(grad_out[None], "c")
    grad_out = grad_out.reshape(2, 2, 2, 2, 2, rows, out_width)
    grad_out = grad_out.transpose(0, 4, 2, 1, 3, 5, 6).reshape(4, total_rows // 4, out_width)
    projection_grad = 0.0
    for step, one in enumerate(student_blocks):
        projection_grad += lax.dot_general(
            one,
            lax.dynamic_index_in_dim(grad_out, (x + step) % 4, keepdims=False),
            (((0,), (0,)), ((), ())),
            preferred_element_type=F32,
        )
    return (projection_grad, cosine)


def solution(mesh):
    fine = Mesh(mesh.devices.reshape(2, 2, 2, 4, 2, 2, 2, 2), DP + MP)
    return jax.shard_map(
        shards,
        mesh=fine,
        in_specs=(P(DP, MP), P(MP, DP), P(DP, MP), P(MP, DP), P(MP)),
        out_specs=(P(MP, DP), P(MP)),
        check_vma=False,
    )
```

time: 279 us -> 244 us (0.87)
  blocking collectives: 228 us -> 33.7 us
  starting transfers between devices: 5.37 us -> 118 us
  waiting for transfers between devices: 24.3 us -> 67.3 us
  local copies, waits for them, and re-layouts: 5.96 us -> 9.47 us
  matrix products: 9.36 us -> 6.11 us
    ppermute x0 -> x25, starting transfers between devices: none -> 111 us  [the longest x10 48.2 us: swap_in(): other = lax.ppermute(value, axis, SWAP)]
    all_to_all x8 -> x3, blocking collectives: 134 us -> 33.7 us  [spread(): return lax.all_to_all(copies, axis, split_axis=0, concat_axis=0, tiled=True)]
    ppermute x0 -> x25, waiting for transfers between devices: none -> 66.4 us  [the longest x10 33.8 us: swap_in(): other = lax.ppermute(value, axis, SWAP)]
    all_to_all x3 -> x0, blocking collectives: 48.1 us -> none  [reduce_over(): lax.all_to_all(value, axis, split_axis=0, concat_axis=0, tiled=True)]
    all_gather x1 -> x0, blocking collectives: 45.7 us -> none  [shards(): lax.all_gather(jnp.broadcast_to(owner_order[:, None], (block, block)), MP...]
    all_to_all x1 -> x2, waiting for transfers between devices: 24.3 us -> 0.84 us  [reduced(): lax.all_to_all(part, ('y1', 'y0'), split_axis=0, concat_axis=0, tiled=True)]
    broadcast_in_dim x9 -> x3, local copies, waits for them, and re-layouts: 3.74 us -> 0.05 us  [spread(): copies = jnp.broadcast_to(value[None], (count,) + value.shape)]
    dot_general x4 -> x13, matrix products: 9.36 us -> 6.11 us  [the longest x8 2.95 us: project(): product = jnp.dot(one, weight, preferred_element_type=F32).astype(BF16)]
  transfers between devices with their start and end apart: 1 -> 27, of which waited for: 1 -> 11; matrix products, arithmetic and copies ran while one was open for 0% -> 7% of each run, Pallas kernels for 0% -> 0%
where the time goes in v2:
time: 244 us; the launch traced here: 243 us
  starting transfers between devices  118 us (48%)
  waiting for transfers between devices  67.3 us (28%)
  blocking collectives  33.7 us (14%)
  local copies, waits for them, and re-layouts  9.47 us (4%)
  other arithmetic  6.6 us (3%)
  matrix products  6.11 us (3%)
    ppermute x10, starting transfers between devices, swap_in(): other = lax.ppermute(value, axis, SWAP)  48.2 us
    ppermute x10, waiting for transfers between devices, swap_in(): other = lax.ppermute(value, axis, SWAP)  33.8 us
    all_to_all x3, blocking collectives, spread(): return lax.all_to_all(copies, axis, split_axis=0, concat_axis=0, tiled=True)  33.7 us
    ppermute x2, waiting for transfers between devices, reduced(): other = lax.ppermute(part.astype(BF16), 'zh', SWAP)  22.4 us
    ppermute x2, starting transfers between devices, reduced(): other = lax.ppermute(part.astype(BF16), 'zh', SWAP)  14.3 us
    ppermute x2, starting transfers between devices, halve(): lax.ppermute(lax.dynamic_index_in_dim(value, 1 - me, keepdims=False).asty...  13.3 us
    ppermute x4, starting transfers between devices, neighbours(): return (lax.ppermute(value, 'x', DOWN), lax.ppermute(value, 'x', UP))  12.8 us
    ppermute x2, starting transfers between devices, opposite(): lax.ppermute(after[half:], 'x', DOWN)  7.46 us
  transfers between devices with their start and end apart: 27, of which 11 were waited for; matrix products, arithmetic and copies ran while one was open for 7% of the time, Pallas kernels for 0%

profile of v2, /device:TPU:1, one launch (start us, length us, event | category | flops | bytes accessed | tf_op | source)
XLA Modules:
  0.0 242.8 jit_solution(11118494240156866450)
XLA Ops:
  1.6 4.4 %collective-permute-start = (bf16[64,512]{1,0:T(8,128)(2,1)S(1)}, bf16[64,512]{1,0:T(8,128)(2,1)S(1)}, u32[]{:S(2)}, u32[]{:S(2)}) collective-permute-start(bf16[64,512]{1,0:T(8,128)(2,1)S(1)} %constant_dynamic-slice_fusion.2), channel_id=1, source_target_pairs={{0,64},{64,0},{1,65},{65,1},{2,66},{66,2},{3,67},{67,3},{4,68},{68... | collective-permute-start | bytes 196616 | tf_op jit(solution)/shard_map/ppermute | solution.py:66
  6.0 6.3 %collective-permute-start.1 = (s32[1,128]{1,0:T(1,128)}, s32[1,128]{1,0:T(1,128)S(1)}, u32[]{:S(2)}, u32[]{:S(2)}) collective-permute-start(s32[1,128]{1,0:T(1,128)} %bitcast.210), channel_id=1, source_target_pairs={{0,1},{1,0},{2,3},{3,2},{4,5},{5,4},{6,7},{7,6},{8,9},{9,8},{10,11... | collective-permute-start | bytes 1544 | tf_op jit(solution)/shard_map/ppermute | solution.py:20
  16.7 6.6 %collective-permute-start.2 = (bf16[128,512]{1,0:T(8,128)(2,1)S(1)}, bf16[128,512]{1,0:T(8,128)(2,1)S(1)}, u32[]{:S(2)}, u32[]{:S(2)}) collective-permute-start(bf16[128,512]{1,0:T(8,128)(2,1)S(1)} %pad_maximum_fusion.5), channel_id=1, source_target_pairs={{0,256},{256,0},{1,257},{257,1},{2,258},{258,2},{3,259},{259,3},{4... | collective-permute-start | bytes 393224 | tf_op jit(solution)/shard_map/ppermute | solution.py:20
  23.4 11.9 %collective-permute-done.2 = bf16[128,512]{1,0:T(8,128)(2,1)S(1)} collective-permute-done((bf16[128,512]{1,0:T(8,128)(2,1)S(1)}, bf16[128,512]{1,0:T(8,128)(2,1)S(1)}, u32[]{:S(2)}, u32[]{:S(2)}) %collective-permute-start.2) | collective-permute-done | bytes 131104 | tf_op jit(solution)/shard_map/ppermute | solution.py:20
  35.4 4.6 %collective-permute-start.5 = (s32[4,128]{1,0:T(4,128)S(1)}, s32[4,128]{1,0:T(4,128)S(1)}, u32[]{:S(2)}, u32[]{:S(2)}) collective-permute-start(s32[4,128]{1,0:T(4,128)S(1)} %bitcast.200), channel_id=1, source_target_pairs={{0,4},{4,0},{1,5},{5,1},{2,6},{6,2},{3,7},{7,3},{8,12},{12,8},{9,1... | collective-permute-start | bytes 6152 | tf_op jit(solution)/shard_map/ppermute | solution.py:20
  41.9 13.6 %collective-permute-done.4 = bf16[256,512]{1,0:T(8,128)(2,1)S(1)} collective-permute-done((bf16[256,512]{1,0:T(8,128)(2,1)S(1)}, bf16[256,512]{1,0:T(8,128)(2,1)S(1)}, u32[]{:S(2)}, u32[]{:S(2)}) %collective-permute-start.4) | collective-permute-done | bytes 262176 | tf_op jit(solution)/shard_map/ppermute | solution.py:20
  55.7 4.4 %collective-permute-start.6 = (bf16[512,512]{1,0:T(8,128)(2,1)S(1)}, bf16[512,512]{1,0:T(8,128)(2,1)S(1)}, u32[]{:S(2)}, u32[]{:S(2)}) collective-permute-start(bf16[512,512]{1,0:T(8,128)(2,1)S(1)} %bitcast.195), channel_id=1, source_target_pairs={{0,48},{16,0},{32,16},{48,32},{1,49},{17,1},{33,17},{49,33},{2,50}... | collective-permute-start | bytes 1572872 | tf_op jit(solution)/shard_map/ppermute | solution.py:33
  68.8 9.8 %collective-permute-start.11 = (s32[8,128]{1,0:T(8,128)S(1)}, s32[8,128]{1,0:T(8,128)S(1)}, u32[]{:S(2)}, u32[]{:S(2)}) collective-permute-start(s32[8,128]{1,0:T(8,128)S(1)} %bitcast.198), channel_id=1, source_target_pairs={{0,8},{8,0},{1,9},{9,1},{2,10},{10,2},{3,11},{11,3},{4,12},{12,4},... | collective-permute-start | bytes 12296 | tf_op jit(solution)/shard_map/ppermute | solution.py:20
  78.6 5.0 %collective-permute-start.9 = (bf16[128,512]{1,0:T(8,128)(2,1)S(1)}, bf16[128,512]{1,0:T(8,128)(2,1)S(1)}, u32[]{:S(2)}, u32[]{:S(2)}) collective-permute-start(bf16[128,512]{1,0:T(8,128)(2,1)S(1)} %bitcast.194), channel_id=1, source_target_pairs={{0,128},{128,0},{1,129},{129,1},{2,130},{130,2},{3,131},{131,3},{4... | collective-permute-start | bytes 393224 | tf_op jit(solution)/shard_map/ppermute | solution.py:20
  83.7 6.1 %collective-permute-done.9 = bf16[128,512]{1,0:T(8,128)(2,1)S(1)} collective-permute-done((bf16[128,512]{1,0:T(8,128)(2,1)S(1)}, bf16[128,512]{1,0:T(8,128)(2,1)S(1)}, u32[]{:S(2)}, u32[]{:S(2)}) %collective-permute-start.9) | collective-permute-done | bytes 131104 | tf_op jit(solution)/shard_map/ppermute | solution.py:20
  100.6 4.6 %collective-permute-start.18 = (bf16[512,512]{1,0:T(8,128)(2,1)S(1)}, bf16[512,512]{1,0:T(8,128)(2,1)S(1)}, u32[]{:S(2)}, u32[]{:S(2)}) collective-permute-start(bf16[512,512]{1,0:T(8,128)(2,1)S(1)} %bitcast.184), channel_id=1, source_target_pairs={{0,48},{16,0},{32,16},{48,32},{1,49},{17,1},{33,17},{49,33},{2,50}... | collective-permute-start | bytes 1572872 | tf_op jit(solution)/shard_map/ppermute | solution.py:33
  108.7 7.3 %collective-permute-start.15 = (bf16[4,2,128,512]{3,2,0,1:T(8,128)(2,1)}, bf16[4,2,128,512]{3,2,0,1:T(8,128)(2,1)}, u32[]{:S(2)}, u32[]{:S(2)}) collective-permute-start(bf16[4,2,128,512]{3,2,0,1:T(8,128)(2,1)} %dynamic-slice_bitcast_fusion), channel_id=1, source_target_pairs={{0,1},{1,0},{2,3},{3,2},{4,5},{5,4},{6,7},{7,6},{8,9},{9,8},{10,11... | collective-permute-start | bytes 3145736 | tf_op jit(solution)/shard_map/ppermute | solution.py:45
  118.4 4.6 %collective-permute-start.21 = (bf16[256,512]{1,0:T(8,128)(2,1)S(1)}, bf16[256,512]{1,0:T(8,128)(2,1)S(1)}, u32[]{:S(2)}, u32[]{:S(2)}) collective-permute-start(bf16[256,512]{1,0:T(8,128)(2,1)S(1)} %slice.40), channel_id=1, source_target_pairs={{0,48},{16,0},{32,16},{48,32},{1,49},{17,1},{33,17},{49,33},{2,50}... | collective-permute-start | bytes 786440 | tf_op jit(solution)/shard_map/ppermute | solution.py:39
  128.1 6.0 %collective-permute-start.22 = (bf16[4,2,128,256]{3,2,0,1:T(8,128)(2,1)}, bf16[4,2,128,256]{3,2,0,1:T(8,128)(2,1)}, u32[]{:S(2)}, u32[]{:S(2)}) collective-permute-start(bf16[4,2,128,256]{3,2,0,1:T(8,128)(2,1)} %dynamic-slice_bitcast_fusion.1), channel_id=1, source_target_pairs={{0,1},{1,0},{2,3},{3,2},{4,5},{5,4},{6,7},{7,6},{8,9},{9,8},{10,11... | collective-permute-start | bytes 1572872 | tf_op jit(solution)/shard_map/ppermute | solution.py:45
  143.0 3.5 %all-to-all-start.1 = ((bf16[4,2,128,256]{3,2,1,0:T(8,128)(2,1)}), bf16[4,2,128,256]{3,2,1,0:T(8,128)(2,1)S(1)}, u32[]{:S(2)}, u32[]{:S(2)}) async-start(bf16[4,2,128,256]{3,2,1,0:T(8,128)(2,1)} %copy.40), calls=%async_computation.1 | async-start | bytes 1048576 | tf_op jit(solution)/shard_map/all_to_all | solution.py:111
  146.5 7.2 %collective-permute-done.16 = bf16[4,2,128,256]{3,2,0,1:T(8,128)(2,1)} collective-permute-done((bf16[4,2,128,256]{3,2,0,1:T(8,128)(2,1)}, bf16[4,2,128,256]{3,2,0,1:T(8,128)(2,1)}, u32[]{:S(2)}, u32[]{:S(2)}) %collective-permute-start.16) | collective-permute-done | bytes 524320 | tf_op jit(solution)/shard_map/ppermute | solution.py:126
  155.8 3.5 %all-to-all-start = ((bf16[4,2,128,256]{3,2,1,0:T(8,128)(2,1)}), bf16[4,2,128,256]{3,2,1,0:T(8,128)(2,1)S(1)}, u32[]{:S(2)}, u32[]{:S(2)}) async-start(bf16[4,2,128,256]{3,2,1,0:T(8,128)(2,1)} %copy.37), calls=%async_computation | async-start | bytes 1048576 | tf_op jit(solution)/shard_map/all_to_all | solution.py:111
  159.3 7.1 %collective-permute-start.23 = (bf16[2,128,256]{2,1,0:T(8,128)(2,1)S(1)}, bf16[2,128,256]{2,1,0:T(8,128)(2,1)S(1)}, u32[]{:S(2)}, u32[]{:S(2)}) collective-permute-start(bf16[2,128,256]{2,1,0:T(8,128)(2,1)S(1)} %convert_element_type.138), channel_id=1, source_target_pairs={{0,8},{8,0},{1,9},{9,1},{2,10},{10,2},{3,11},{11,3},{4,12},{12,4},... | collective-permute-start | bytes 393224 | tf_op jit(solution)/shard_map/ppermute | solution.py:113
  167.4 7.1 %collective-permute-start.17 = (bf16[2,128,256]{2,1,0:T(8,128)(2,1)S(1)}, bf16[2,128,256]{2,1,0:T(8,128)(2,1)S(1)}, u32[]{:S(2)}, u32[]{:S(2)}) collective-permute-start(bf16[2,128,256]{2,1,0:T(8,128)(2,1)S(1)} %convert_element_type.123), channel_id=1, source_target_pairs={{0,8},{8,0},{1,9},{9,1},{2,10},{10,2},{3,11},{11,3},{4,12},{12,4},... | collective-permute-start | bytes 393224 | tf_op jit(solution)/shard_map/ppermute | solution.py:113
  174.6 22.4 %collective-permute-done.17 = bf16[2,128,256]{2,1,0:T(8,128)(2,1)S(1)} collective-permute-done((bf16[2,128,256]{2,1,0:T(8,128)(2,1)S(1)}, bf16[2,128,256]{2,1,0:T(8,128)(2,1)S(1)}, u32[]{:S(2)}, u32[]{:S(2)}) %collective-permute-start.17) | collective-permute-done | bytes 131104 | tf_op jit(solution)/shard_map/ppermute | solution.py:113
  197.2 8.7 %all_to_all.25 = f32[4,3,256]{2,1,0:T(4,128)S(1)} all-to-all(f32[4,3,256]{2,1,0:T(4,128)S(1)} %broadcast_in_dim.67), channel_id=1, replica_groups=mesh['z2'=2,'z1'=2,'z0'=2,'x'=4,'zh'=2,'y1'=2,'y0'=2,'c'=2] {'x'}, dimensions={0} | all-to-all | bytes 24576 | tf_op jit(solution)/shard_map/all_to_all | solution.py:29
  206.0 13.8 %all_to_all.26 = f32[8,3,256]{2,1,0:T(4,128)S(1)} all-to-all(f32[8,3,256]{2,1,0:T(4,128)S(1)} %broadcast_in_dim.68), channel_id=1, replica_groups=mesh['z2'=2,'z1'=2,'z0'=2,'x'=4,'zh'=2,'y1'=2,'y0'=2,'c'=2] {'z2','z1','..., dimensions={0} | all-to-all | bytes 49152 | tf_op jit(solution)/shard_map/all_to_all | solution.py:29
  220.0 11.2 %all_to_all.27 = bf16[4,256,256]{2,1,0:T(8,128)(2,1)S(1)} all-to-all(bf16[4,256,256]{2,1,0:T(8,128)(2,1)S(1)} %broadcast_in_dim.69), channel_id=1, replica_groups=mesh['z2'=2,'z1'=2,'z0'=2,'x'=4,'zh'=2,'y1'=2,'y0'=2,'c'=2] {'y1','y0'}, dimensions={0} | all-to-all | bytes 1048576 | tf_op jit(solution)/shard_map/all_to_all | solution.py:29
  231.2 6.7 %collective-permute-start.24 = (bf16[1,4,256,256]{3,2,1,0:T(8,128)(2,1)S(1)}, bf16[1,4,256,256]{3,2,1,0:T(8,128)(2,1)S(1)}, u32[]{:S(2)}, u32[]{:S(2)}) collective-permute-start(bf16[1,4,256,256]{3,2,1,0:T(8,128)(2,1)S(1)} %bitcast.187), channel_id=1, source_target_pairs={{0,1},{1,0},{2,3},{3,2},{4,5},{5,4},{6,7},{7,6},{8,9},{9,8},{10,11... | collective-permute-start | bytes 1572872 | tf_op jit(solution)/shard_map/ppermute | solution.py:20
  (131 shorter events, 54.8 us)
Async XLA Ops:
  1.6 12.3 %collective-permute-start = (bf16[64,512]{1,0:T(8,128)(2,1)S(1)}, bf16[64,512]{1,0:T(8,128)(2,1)S(1)}, u32[]{:S(2)}, u32[]{:S(2)}) collective-permute-start(bf16[64,512]{1,0:T(8,128)(2,1)S(1)} %constant_dynamic-slice_fusion.2), channel_id=1, source_target_pairs={{0,64},{64,0},{1,65},{65,1},{2,66},{66,2},{3,67},{67,3},{4,68},{68... | collective-permute-start | bytes 196616 | tf_op jit(solution)/shard_map/ppermute | solution.py:66
  13.9 9.5 %collective-permute-start.3 = (s32[2,128]{1,0:T(2,128)S(1)}, s32[2,128]{1,0:T(2,128)S(1)}, u32[]{:S(2)}, u32[]{:S(2)}) collective-permute-start(s32[2,128]{1,0:T(2,128)S(1)} %bitcast.202), channel_id=1, source_target_pairs={{0,2},{2,0},{1,3},{3,1},{4,6},{6,4},{5,7},{7,5},{8,10},{10,8},{9,1... | collective-permute-start | bytes 3080 | tf_op jit(solution)/shard_map/ppermute | solution.py:20
  16.7 18.5 %collective-permute-start.2 = (bf16[128,512]{1,0:T(8,128)(2,1)S(1)}, bf16[128,512]{1,0:T(8,128)(2,1)S(1)}, u32[]{:S(2)}, u32[]{:S(2)}) collective-permute-start(bf16[128,512]{1,0:T(8,128)(2,1)S(1)} %pad_maximum_fusion.5), channel_id=1, source_target_pairs={{0,256},{256,0},{1,257},{257,1},{2,258},{258,2},{3,259},{259,3},{4... | collective-permute-start | bytes 393224 | tf_op jit(solution)/shard_map/ppermute | solution.py:20
  40.0 15.6 %collective-permute-start.4 = (bf16[256,512]{1,0:T(8,128)(2,1)S(1)}, bf16[256,512]{1,0:T(8,128)(2,1)S(1)}, u32[]{:S(2)}, u32[]{:S(2)}) collective-permute-start(bf16[256,512]{1,0:T(8,128)(2,1)S(1)} %bitcast.190), channel_id=1, source_target_pairs={{0,128},{128,0},{1,129},{129,1},{2,130},{130,2},{3,131},{131,3},{4... | collective-permute-start | bytes 786440 | tf_op jit(solution)/shard_map/ppermute | solution.py:20
  55.7 34.2 %collective-permute-start.6 = (bf16[512,512]{1,0:T(8,128)(2,1)S(1)}, bf16[512,512]{1,0:T(8,128)(2,1)S(1)}, u32[]{:S(2)}, u32[]{:S(2)}) collective-permute-start(bf16[512,512]{1,0:T(8,128)(2,1)S(1)} %bitcast.195), channel_id=1, source_target_pairs={{0,48},{16,0},{32,16},{48,32},{1,49},{17,1},{33,17},{49,33},{2,50}... | collective-permute-start | bytes 1572872 | tf_op jit(solution)/shard_map/ppermute | solution.py:33
  60.1 29.8 %collective-permute-start.7 = (bf16[512,512]{1,0:T(8,128)(2,1)S(1)}, bf16[512,512]{1,0:T(8,128)(2,1)S(1)}, u32[]{:S(2)}, u32[]{:S(2)}) collective-permute-start(bf16[512,512]{1,0:T(8,128)(2,1)S(1)} %bitcast.196), channel_id=1, source_target_pairs={{0,16},{16,32},{32,48},{48,0},{1,17},{17,33},{33,49},{49,1},{2,18}... | collective-permute-start | bytes 1572872 | tf_op jit(solution)/shard_map/ppermute | solution.py:33
  62.0 16.6 %collective-permute-start.8 = (bf16[64,512]{1,0:T(8,128)(2,1)S(1)}, bf16[64,512]{1,0:T(8,128)(2,1)S(1)}, u32[]{:S(2)}, u32[]{:S(2)}) collective-permute-start(bf16[64,512]{1,0:T(8,128)(2,1)S(1)} %copy-done.12), channel_id=1, source_target_pairs={{0,256},{256,0},{1,257},{257,1},{2,258},{258,2},{3,259},{259,3},{4... | collective-permute-start | bytes 196616 | tf_op jit(solution)/shard_map/ppermute | solution.py:20
  65.5 26.3 %collective-permute-start.12 = (bf16[512,256]{1,0:T(8,128)(2,1)S(1)}, bf16[512,256]{1,0:T(8,128)(2,1)S(1)}, u32[]{:S(2)}, u32[]{:S(2)}) collective-permute-start(bf16[512,256]{1,0:T(8,128)(2,1)S(1)} %get-tuple-element.32), channel_id=1, source_target_pairs={{0,64},{64,0},{1,65},{65,1},{2,66},{66,2},{3,67},{67,3},{4,68},{68... | collective-permute-start | bytes 786440 | tf_op jit(solution)/shard_map/ppermute | solution.py:84
  68.8 14.8 %collective-permute-start.11 = (s32[8,128]{1,0:T(8,128)S(1)}, s32[8,128]{1,0:T(8,128)S(1)}, u32[]{:S(2)}, u32[]{:S(2)}) collective-permute-start(s32[8,128]{1,0:T(8,128)S(1)} %bitcast.198), channel_id=1, source_target_pairs={{0,8},{8,0},{1,9},{9,1},{2,10},{10,2},{3,11},{11,3},{4,12},{12,4},... | collective-permute-start | bytes 12296 | tf_op jit(solution)/shard_map/ppermute | solution.py:20
  78.6 11.2 %collective-permute-start.9 = (bf16[128,512]{1,0:T(8,128)(2,1)S(1)}, bf16[128,512]{1,0:T(8,128)(2,1)S(1)}, u32[]{:S(2)}, u32[]{:S(2)}) collective-permute-start(bf16[128,512]{1,0:T(8,128)(2,1)S(1)} %bitcast.194), channel_id=1, source_target_pairs={{0,128},{128,0},{1,129},{129,1},{2,130},{130,2},{3,131},{131,3},{4... | collective-permute-start | bytes 393224 | tf_op jit(solution)/shard_map/ppermute | solution.py:20
  89.9 8.7 %collective-permute-start.10 = (bf16[256,512]{1,0:T(8,128)(2,1)S(1)}, bf16[256,512]{1,0:T(8,128)(2,1)S(1)}, u32[]{:S(2)}, u32[]{:S(2)}) collective-permute-start(bf16[256,512]{1,0:T(8,128)(2,1)S(1)} %bitcast.192), channel_id=1, source_target_pairs={{0,64},{64,0},{1,65},{65,1},{2,66},{66,2},{3,67},{67,3},{4,68},{68... | collective-permute-start | bytes 786440 | tf_op jit(solution)/shard_map/ppermute | solution.py:20
  92.5 12.7 %collective-permute-start.14 = (bf16[256,512]{1,0:T(8,128)(2,1)S(1)}, bf16[256,512]{1,0:T(8,128)(2,1)S(1)}, u32[]{:S(2)}, u32[]{:S(2)}) collective-permute-start(bf16[256,512]{1,0:T(8,128)(2,1)S(1)} %slice.29), channel_id=1, source_target_pairs={{0,48},{16,0},{32,16},{48,32},{1,49},{17,1},{33,17},{49,33},{2,50}... | collective-permute-start | bytes 786440 | tf_op jit(solution)/shard_map/ppermute | solution.py:39
  95.4 9.8 %collective-permute-start.13 = (bf16[256,512]{1,0:T(8,128)(2,1)S(1)}, bf16[256,512]{1,0:T(8,128)(2,1)S(1)}, u32[]{:S(2)}, u32[]{:S(2)}) collective-permute-start(bf16[256,512]{1,0:T(8,128)(2,1)S(1)} %slice.28), channel_id=1, source_target_pairs={{0,16},{16,32},{32,48},{48,0},{1,17},{17,33},{33,49},{49,1},{2,18}... | collective-permute-start | bytes 786440 | tf_op jit(solution)/shard_map/ppermute | solution.py:39
  98.7 17.3 %collective-permute-start.19 = (bf16[512,512]{1,0:T(8,128)(2,1)S(1)}, bf16[512,512]{1,0:T(8,128)(2,1)S(1)}, u32[]{:S(2)}, u32[]{:S(2)}) collective-permute-start(bf16[512,512]{1,0:T(8,128)(2,1)S(1)} %bitcast.183), channel_id=1, source_target_pairs={{0,16},{16,32},{32,48},{48,0},{1,17},{17,33},{33,49},{49,1},{2,18}... | collective-permute-start | bytes 1572872 | tf_op jit(solution)/shard_map/ppermute | solution.py:33
  100.6 17.7 %collective-permute-start.18 = (bf16[512,512]{1,0:T(8,128)(2,1)S(1)}, bf16[512,512]{1,0:T(8,128)(2,1)S(1)}, u32[]{:S(2)}, u32[]{:S(2)}) collective-permute-start(bf16[512,512]{1,0:T(8,128)(2,1)S(1)} %bitcast.184), channel_id=1, source_target_pairs={{0,48},{16,0},{32,16},{48,32},{1,49},{17,1},{33,17},{49,33},{2,50}... | collective-permute-start | bytes 1572872 | tf_op jit(solution)/shard_map/ppermute | solution.py:33
  108.7 25.4 %collective-permute-start.15 = (bf16[4,2,128,512]{3,2,0,1:T(8,128)(2,1)}, bf16[4,2,128,512]{3,2,0,1:T(8,128)(2,1)}, u32[]{:S(2)}, u32[]{:S(2)}) collective-permute-start(bf16[4,2,128,512]{3,2,0,1:T(8,128)(2,1)} %dynamic-slice_bitcast_fusion), channel_id=1, source_target_pairs={{0,1},{1,0},{2,3},{3,2},{4,5},{5,4},{6,7},{7,6},{8,9},{9,8},{10,11... | collective-permute-start | bytes 3145736 | tf_op jit(solution)/shard_map/ppermute | solution.py:45
  116.0 8.3 %collective-permute-start.20 = (bf16[256,512]{1,0:T(8,128)(2,1)S(1)}, bf16[256,512]{1,0:T(8,128)(2,1)S(1)}, u32[]{:S(2)}, u32[]{:S(2)}) collective-permute-start(bf16[256,512]{1,0:T(8,128)(2,1)S(1)} %slice.39), channel_id=1, source_target_pairs={{0,16},{16,32},{32,48},{48,0},{1,17},{17,33},{33,49},{49,1},{2,18}... | collective-permute-start | bytes 786440 | tf_op jit(solution)/shard_map/ppermute | solution.py:39
  128.1 12.9 %collective-permute-start.22 = (bf16[4,2,128,256]{3,2,0,1:T(8,128)(2,1)}, bf16[4,2,128,256]{3,2,0,1:T(8,128)(2,1)}, u32[]{:S(2)}, u32[]{:S(2)}) collective-permute-start(bf16[4,2,128,256]{3,2,0,1:T(8,128)(2,1)} %dynamic-slice_bitcast_fusion.1), channel_id=1, source_target_pairs={{0,1},{1,0},{2,3},{3,2},{4,5},{5,4},{6,7},{7,6},{8,9},{9,8},{10,11... | collective-permute-start | bytes 1572872 | tf_op jit(solution)/shard_map/ppermute | solution.py:45
  137.8 15.9 %collective-permute-start.16 = (bf16[4,2,128,256]{3,2,0,1:T(8,128)(2,1)}, bf16[4,2,128,256]{3,2,0,1:T(8,128)(2,1)}, u32[]{:S(2)}, u32[]{:S(2)}) collective-permute-start(bf16[4,2,128,256]{3,2,0,1:T(8,128)(2,1)} %slice.54), channel_id=1, source_target_pairs={{0,64},{64,0},{1,65},{65,1},{2,66},{66,2},{3,67},{67,3},{4,68},{68... | collective-permute-start | bytes 1572872 | tf_op jit(solution)/shard_map/ppermute | solution.py:126
  143.0 12.8 %all-to-all-start.1 = ((bf16[4,2,128,256]{3,2,1,0:T(8,128)(2,1)}), bf16[4,2,128,256]{3,2,1,0:T(8,128)(2,1)S(1)}, u32[]{:S(2)}, u32[]{:S(2)}) async-start(bf16[4,2,128,256]{3,2,1,0:T(8,128)(2,1)} %copy.40), calls=%async_computation.1 | async-start | bytes 1048576 | tf_op jit(solution)/shard_map/all_to_all | solution.py:111
  155.8 11.5 %all-to-all-start = ((bf16[4,2,128,256]{3,2,1,0:T(8,128)(2,1)}), bf16[4,2,128,256]{3,2,1,0:T(8,128)(2,1)S(1)}, u32[]{:S(2)}, u32[]{:S(2)}) async-start(bf16[4,2,128,256]{3,2,1,0:T(8,128)(2,1)} %copy.37), calls=%async_computation | async-start | bytes 1048576 | tf_op jit(solution)/shard_map/all_to_all | solution.py:111
  159.3 15.2 %collective-permute-start.23 = (bf16[2,128,256]{2,1,0:T(8,128)(2,1)S(1)}, bf16[2,128,256]{2,1,0:T(8,128)(2,1)S(1)}, u32[]{:S(2)}, u32[]{:S(2)}) collective-permute-start(bf16[2,128,256]{2,1,0:T(8,128)(2,1)S(1)} %convert_element_type.138), channel_id=1, source_target_pairs={{0,8},{8,0},{1,9},{9,1},{2,10},{10,2},{3,11},{11,3},{4,12},{12,4},... | collective-permute-start | bytes 393224 | tf_op jit(solution)/shard_map/ppermute | solution.py:113
  167.4 29.6 %collective-permute-start.17 = (bf16[2,128,256]{2,1,0:T(8,128)(2,1)S(1)}, bf16[2,128,256]{2,1,0:T(8,128)(2,1)S(1)}, u32[]{:S(2)}, u32[]{:S(2)}) collective-permute-start(bf16[2,128,256]{2,1,0:T(8,128)(2,1)S(1)} %convert_element_type.123), channel_id=1, source_target_pairs={{0,8},{8,0},{1,9},{9,1},{2,10},{10,2},{3,11},{11,3},{4,12},{12,4},... | collective-permute-start | bytes 393224 | tf_op jit(solution)/shard_map/ppermute | solution.py:113
  231.2 8.2 %collective-permute-start.24 = (bf16[1,4,256,256]{3,2,1,0:T(8,128)(2,1)S(1)}, bf16[1,4,256,256]{3,2,1,0:T(8,128)(2,1)S(1)}, u32[]{:S(2)}, u32[]{:S(2)}) collective-permute-start(bf16[1,4,256,256]{3,2,1,0:T(8,128)(2,1)S(1)} %bitcast.187), channel_id=1, source_target_pairs={{0,1},{1,0},{2,3},{3,2},{4,5},{5,4},{6,7},{7,6},{8,9},{9,8},{10,11... | collective-permute-start | bytes 1572872 | tf_op jit(solution)/shard_map/ppermute | solution.py:20
  (16 other events, 326.9 us)

commit v3 on v1

v3 whole, which is shorter than its diff:
```python
import jax
import jax.numpy as jnp
from jax import lax
from jax.sharding import Mesh, PartitionSpec as P

F32 = jnp.float32
BF16 = jnp.bfloat16
YC = ("y1", "y0", "c")
DP = ("z2", "z1", "z0", "x")
MP = ("zh", "y1", "y0", "c")
SWAP = [(0, 1), (1, 0)]


def together(*values):
    return lax.optimization_barrier(values)


def in_order(value, other, axis):
    first = lax.axis_index(axis) == 0
    both = jnp.stack([jnp.where(first, value, other), jnp.where(first, other, value)])
    return both.reshape((-1,) + value.shape[1:])


def swap_in(value, axis):
    return in_order(value, lax.ppermute(value, axis, SWAP), axis)


def spread(value, axis):
    count = lax.axis_size(axis)
    copies = jnp.broadcast_to(value[None], (count,) + value.shape)
    return lax.all_to_all(copies, axis, split_axis=0, concat_axis=0, tiled=True)


def summed(pieces, axis):
    part = lax.all_to_all(pieces, axis, split_axis=0, concat_axis=0, tiled=True)
    return jnp.sum(part.astype(F32), axis=0)


def halve(value, axis):
    me = lax.axis_index(axis)
    other = lax.dynamic_index_in_dim(value, 1 - me, keepdims=False)
    other = lax.ppermute(other.astype(BF16), axis, SWAP)
    return lax.dynamic_index_in_dim(value, me, keepdims=False).astype(F32) + other.astype(F32)


def both_owners(part):
    other = lax.ppermute(part.astype(BF16), "zh", SWAP)
    return (part + other.astype(F32)).reshape(-1, part.shape[-1])


def shards(teacher_in, teacher_weight, student_in, projection, owner_order):
    rows, out_width = teacher_in.shape[0], projection.shape[1]
    groups = 16
    block = owner_order.shape[0]
    sub = block // groups
    total_rows = groups * block
    core = lax.axis_index("c")
    z0 = lax.axis_index("z0")
    part_width = teacher_in.shape[1] // 4
    student_width = student_in.shape[1]

    quarters = jnp.concatenate(
        [
            teacher_in.reshape(rows, 4, part_width).transpose(1, 0, 2),
            teacher_weight.reshape(4, part_width, out_width),
        ],
        axis=1,
    )
    quarters = lax.all_to_all(quarters, "x", split_axis=0, concat_axis=0, tiled=True)
    student, quarters = together(swap_in(student_in, "z2"), quarters)
    teacher = quarters[:, :rows].reshape(4 * rows, part_width)
    weights = quarters[:, rows:]
    student, teacher, orders = together(
        swap_in(student, "z1"), swap_in(teacher, "z2"), spread(owner_order, YC)
    )
    student, teacher, orders = together(swap_in(student, "z0"), swap_in(teacher, "z1"), orders)
    student_all, teacher, orders = together(
        spread(student, "x"), swap_in(teacher, "z0"), swap_in(orders, "zh")
    )
    student_all = student_all.reshape(total_rows, student_width)
    student_part = jnp.dot(student_all, projection, preferred_element_type=F32).astype(BF16)
    student_part = student_part.reshape(2, 2, 2, 2, 2, rows, out_width)
    student_part = student_part.transpose(3, 2, 0, 4, 1, 5, 6).reshape(8, 2, block, out_width)
    student_part, teacher = together(student_part, teacher)
    student_part = summed(student_part, YC)
    pick = orders[:, :, None] == lax.broadcasted_iota(jnp.int32, (groups, block, block), 2)
    pick = pick.astype(BF16)

    teacher = teacher.reshape(2, 2, 2, 2, 2, rows, part_width)
    teacher = teacher.transpose(2, 1, 0, 3, 4, 5, 6).reshape(groups, block, part_width)
    teacher = jnp.einsum("bqk,bkn->bqn", pick, teacher, preferred_element_type=F32).astype(BF16)
    teacher = teacher.reshape(groups, 2, 4, 2, sub, part_width)
    teacher = teacher.transpose(3, 2, 1, 0, 4, 5).reshape(2, total_rows // 2, part_width)

    def product(which):
        one = lax.dynamic_index_in_dim(teacher, which, keepdims=False)
        return [
            jnp.dot(one, weights[place], preferred_element_type=F32).astype(BF16)
            for place in range(4)
        ]

    arrived = lax.ppermute(jnp.stack(product(1 - core)), "c", SWAP)
    own = together(*product(core))
    part = jnp.stack(
        [(own[place].astype(F32) + arrived[place].astype(F32)).astype(BF16) for place in range(4)]
    )
    part = part.reshape(16, 2, block, out_width)
    part, student_part = together(part, student_part)
    part = summed(part, ("x", "y1", "y0"))
    student_out = both_owners(student_part)
    part, student_out = together(part, student_out)
    target = both_owners(part).astype(BF16)
    target = target.astype(F32)

    stats = jnp.stack(
        [
            jnp.sum(student_out * target, axis=1),
            jnp.sum(student_out * student_out, axis=1),
            jnp.sum(target * target, axis=1),
        ]
    )
    stats = jnp.sum(spread(stats, "x"), axis=0)
    stats = jnp.sum(spread(stats, ("z2", "z1", "z0")), axis=0)
    inner, sq_student, sq_target = stats[0], stats[1], stats[2]
    inv_student = lax.rsqrt(sq_student + 1e-06)
    inv_target = lax.rsqrt(sq_target + 1e-06)
    cosine = inner * inv_student * inv_target
    scale = -1.0 / total_rows
    grad_out = scale * (
        target * (inv_student * inv_target)[:, None]
        - (inner * inv_target * inv_student**3)[:, None] * student_out
    )
    grad_out = grad_out.astype(BF16)
    cosine = lax.dynamic_slice_in_dim(cosine, lax.axis_index("zh") * block, block)
    grad_out = spread(grad_out, ("y1", "y0"))
    grad_out = swap_in(grad_out[None], "c")
    grad_out = grad_out.reshape(2, 2, 2, 2, 2, rows, out_width)
    grad_out = grad_out.transpose(0, 4, 2, 1, 3, 5, 6).reshape(total_rows, out_width)
    projection_grad = lax.dot_general(
        student_all, grad_out, (((0,), (0,)), ((), ())), preferred_element_type=F32
    )
    return (projection_grad, cosine)


def solution(mesh):
    fine = Mesh(mesh.devices.reshape(2, 2, 2, 4, 2, 2, 2, 2), DP + MP)
    return jax.shard_map(
        shards,
        mesh=fine,
        in_specs=(P(DP, MP), P(MP, DP), P(DP, MP), P(MP, DP), P(MP)),
        out_specs=(P(MP, DP), P(MP)),
        check_vma=False,
    )
```

time: 279 us -> 231 us (0.83)
  blocking collectives: 228 us -> 37.7 us
  starting transfers between devices: 5.37 us -> 104 us
  waiting for transfers between devices: 24.3 us -> 57.3 us
  other arithmetic: 3.96 us -> 12.3 us
    all_to_all x8 -> x3, blocking collectives: 134 us -> 37.7 us  [spread(): return lax.all_to_all(copies, axis, split_axis=0, concat_axis=0, tiled=True)]
    ppermute x0 -> x11, starting transfers between devices: none -> 79.5 us  [the longest x8 50.7 us: swap_in(): return in_order(value, lax.ppermute(value, axis, SWAP), axis)]
    all_to_all x3 -> x0, blocking collectives: 48.1 us -> none  [reduce_over(): lax.all_to_all(value, axis, split_axis=0, concat_axis=0, tiled=True)]
    all_gather x1 -> x0, blocking collectives: 45.7 us -> none  [shards(): lax.all_gather(jnp.broadcast_to(owner_order[:, None], (block, block)), MP...]
    ppermute x0 -> x11, waiting for transfers between devices: none -> 35 us  [the longest x8 29.8 us: swap_in(): return in_order(value, lax.ppermute(value, axis, SWAP), axis)]
    all_to_all x1 -> x2, waiting for transfers between devices: 24.3 us -> 1.93 us  [spread(): return lax.all_to_all(copies, axis, split_axis=0, concat_axis=0, tiled=True)]
    all_to_all x0 -> x3, waiting for transfers between devices: none -> 20.4 us  [the longest x2 20.4 us: summed(): part = lax.all_to_all(pieces, axis, split_axis=0, concat_axis=0, tiled=True)]
    all_to_all x0 -> x3, starting transfers between devices: none -> 13.8 us  [the longest x2 8.95 us: summed(): part = lax.all_to_all(pieces, axis, split_axis=0, concat_axis=0, tiled=True)]
  transfers between devices with their start and end apart: 1 -> 16, of which waited for: 1 -> 11; matrix products, arithmetic and copies ran while one was open for 0% -> 5% of each run, Pallas kernels for 0% -> 0%
where the time goes in v3:
time: 231 us; the launch traced here: 230 us
  starting transfers between devices  104 us (45%)
  waiting for transfers between devices  57.3 us (25%)
  blocking collectives  37.7 us (16%)
  other arithmetic  12.3 us (5%)
  matrix products  11.9 us (5%)
  local copies, waits for them, and re-layouts  5.52 us (2%)
    ppermute x8, starting transfers between devices, swap_in(): return in_order(value, lax.ppermute(value, axis, SWAP), axis)  50.7 us
    all_to_all x3, blocking collectives, spread(): return lax.all_to_all(copies, axis, split_axis=0, concat_axis=0, tiled=True)  37.7 us
    ppermute x8, waiting for transfers between devices, swap_in(): return in_order(value, lax.ppermute(value, axis, SWAP), axis)  29.8 us
    ppermute x2, starting transfers between devices, both_owners(): other = lax.ppermute(part.astype(BF16), 'zh', SWAP)  24.4 us
    all_to_all x2, waiting for transfers between devices, summed(): part = lax.all_to_all(pieces, axis, split_axis=0, concat_axis=0, tiled=True)  20.4 us
    all_to_all x2, starting transfers between devices, spread(): return lax.all_to_all(copies, axis, split_axis=0, concat_axis=0, tiled=True)  10.8 us
    dot_general x8, matrix products, product(): jnp.dot(one, weights[place], preferred_element_type=F32).astype(BF16)  9.18 us
    all_to_all x2, starting transfers between devices, summed(): part = lax.all_to_all(pieces, axis, split_axis=0, concat_axis=0, tiled=True)  8.95 us
  transfers between devices with their start and end apart: 16, of which 11 were waited for; matrix products, arithmetic and copies ran while one was open for 5% of the time, Pallas kernels for 0%

profile of v3, /device:TPU:1, one launch (start us, length us, event | category | flops | bytes accessed | tf_op | source)
XLA Modules:
  0.0 230.0 jit_solution(17026255458091846818)
XLA Ops:
  3.6 4.8 %all-to-all-start = ((bf16[4,320,256]{2,1,0:T(8,128)(2,1)}), bf16[4,320,256]{2,1,0:T(8,128)(2,1)S(1)}, u32[]{:S(2)}, u32[]{:S(2)}) async-start(bf16[4,320,256]{2,1,0:T(8,128)(2,1)} %pad_maximum_fusion.3), calls=%async_computation | async-start | bytes 1310720 | tf_op jit(solution)/shard_map/all_to_all | solution.py:69
  8.4 8.8 %collective-permute-start = (bf16[64,512]{1,0:T(8,128)(2,1)S(1)}, bf16[64,512]{1,0:T(8,128)(2,1)S(1)}, u32[]{:S(2)}, u32[]{:S(2)}) collective-permute-start(bf16[64,512]{1,0:T(8,128)(2,1)S(1)} %copy-done.3), channel_id=1, source_target_pairs={{0,256},{256,0},{1,257},{257,1},{2,258},{258,2},{3,259},{259,3},{4... | collective-permute-start | bytes 196616 | tf_op jit(solution)/shard_map/ppermute | solution.py:25
  18.9 8.3 %collective-permute-start.2 = (bf16[256,256]{1,0:T(8,128)(2,1)S(1)}, bf16[256,256]{1,0:T(8,128)(2,1)S(1)}, u32[]{:S(2)}, u32[]{:S(2)}) collective-permute-start(bf16[256,256]{1,0:T(8,128)(2,1)S(1)} %bitcast.198), channel_id=1, source_target_pairs={{0,256},{256,0},{1,257},{257,1},{2,258},{258,2},{3,259},{259,3},{4... | collective-permute-start | bytes 393224 | tf_op jit(solution)/shard_map/ppermute | solution.py:25
  27.8 6.6 %all-to-all-start.1 = ((s32[8,1,128]{2,1,0:T(1,128)}), s32[8,1,128]{2,1,0:T(1,128)S(1)}, u32[]{:S(2)}, u32[]{:S(2)}) async-start(s32[8,1,128]{2,1,0:T(1,128)} %broadcast_in_dim.12), calls=%async_computation.1 | async-start | bytes 8192 | tf_op jit(solution)/shard_map/all_to_all | solution.py:31
  34.4 5.4 %collective-permute-start.1 = (bf16[128,512]{1,0:T(8,128)(2,1)S(1)}, bf16[128,512]{1,0:T(8,128)(2,1)S(1)}, u32[]{:S(2)}, u32[]{:S(2)}) collective-permute-start(bf16[128,512]{1,0:T(8,128)(2,1)S(1)} %bitcast.196), channel_id=1, source_target_pairs={{0,128},{128,0},{1,129},{129,1},{2,130},{130,2},{3,131},{131,3},{4... | collective-permute-start | bytes 393224 | tf_op jit(solution)/shard_map/ppermute | solution.py:25
  39.9 7.1 %collective-permute-done.1 = bf16[128,512]{1,0:T(8,128)(2,1)S(1)} collective-permute-done((bf16[128,512]{1,0:T(8,128)(2,1)S(1)}, bf16[128,512]{1,0:T(8,128)(2,1)S(1)}, u32[]{:S(2)}, u32[]{:S(2)}) %collective-permute-start.1) | collective-permute-done | bytes 131104 | tf_op jit(solution)/shard_map/ppermute | solution.py:25
  49.1 5.0 %collective-permute-start.4 = (bf16[512,256]{1,0:T(8,128)(2,1)S(1)}, bf16[512,256]{1,0:T(8,128)(2,1)S(1)}, u32[]{:S(2)}, u32[]{:S(2)}) collective-permute-start(bf16[512,256]{1,0:T(8,128)(2,1)S(1)} %bitcast.192), channel_id=1, source_target_pairs={{0,128},{128,0},{1,129},{129,1},{2,130},{130,2},{3,131},{131,3},{4... | collective-permute-start | bytes 786440 | tf_op jit(solution)/shard_map/ppermute | solution.py:25
  54.1 5.8 %collective-permute-done.3 = bf16[256,512]{1,0:T(8,128)(2,1)S(1)} collective-permute-done((bf16[256,512]{1,0:T(8,128)(2,1)S(1)}, bf16[256,512]{1,0:T(8,128)(2,1)S(1)}, u32[]{:S(2)}, u32[]{:S(2)}) %collective-permute-start.3) | collective-permute-done | bytes 262176 | tf_op jit(solution)/shard_map/ppermute | solution.py:25
  60.0 5.7 %collective-permute-done.4 = bf16[512,256]{1,0:T(8,128)(2,1)S(1)} collective-permute-done((bf16[512,256]{1,0:T(8,128)(2,1)S(1)}, bf16[512,256]{1,0:T(8,128)(2,1)S(1)}, u32[]{:S(2)}, u32[]{:S(2)}) %collective-permute-start.4) | collective-permute-done | bytes 262176 | tf_op jit(solution)/shard_map/ppermute | solution.py:25
  67.4 4.2 %all-to-all-start.2 = ((bf16[4,512,512]{2,1,0:T(8,128)(2,1)}), bf16[4,512,512]{2,1,0:T(8,128)(2,1)S(1)}, u32[]{:S(2)}, u32[]{:S(2)}) async-start(bf16[4,512,512]{2,1,0:T(8,128)(2,1)} %broadcast_in_dim.13), calls=%async_computation.2 | async-start | bytes 4194304 | tf_op jit(solution)/shard_map/all_to_all | solution.py:31
  73.5 12.1 %collective-permute-start.6 = (s32[8,128]{1,0:T(8,128)S(1)}, s32[8,128]{1,0:T(8,128)S(1)}, u32[]{:S(2)}, u32[]{:S(2)}) collective-permute-start(s32[8,128]{1,0:T(8,128)S(1)} %bitcast.202), channel_id=1, source_target_pairs={{0,8},{8,0},{1,9},{9,1},{2,10},{10,2},{3,11},{11,3},{4,12},{12,4},... | collective-permute-start | bytes 12296 | tf_op jit(solution)/shard_map/ppermute | solution.py:25
  85.7 8.6 %collective-permute-done.6 = s32[8,128]{1,0:T(8,128)S(1)} collective-permute-done((s32[8,128]{1,0:T(8,128)S(1)}, s32[8,128]{1,0:T(8,128)S(1)}, u32[]{:S(2)}, u32[]{:S(2)}) %collective-permute-start.6) | collective-permute-done | bytes 4128 | tf_op jit(solution)/shard_map/ppermute | solution.py:25
  102.1 4.4 %collective-permute-start.7 = (bf16[4,1024,256]{2,1,0:T(8,128)(2,1)}, bf16[4,1024,256]{2,1,0:T(8,128)(2,1)}, u32[]{:S(2)}, u32[]{:S(2)}) collective-permute-start(bf16[4,1024,256]{2,1,0:T(8,128)(2,1)} %pad_maximum_fusion), channel_id=1, source_target_pairs={{0,1},{1,0},{2,3},{3,2},{4,5},{5,4},{6,7},{7,6},{8,9},{9,8},{10,11... | collective-permute-start | bytes 6291464 | tf_op jit(solution)/shard_map/ppermute | solution.py:102
  106.5 4.5 %all-to-all-start.3 = ((bf16[8,2,128,256]{3,2,1,0:T(8,128)(2,1)}), bf16[8,2,128,256]{3,2,1,0:T(8,128)(2,1)}, u32[]{:S(2)}, u32[]{:S(2)}) async-start(bf16[8,2,128,256]{3,2,1,0:T(8,128)(2,1)} %bitcast.179), calls=%async_computation.3 | async-start | bytes 2097152 | tf_op jit(solution)/shard_map/all_to_all | solution.py:35
  119.0 7.2 %all-to-all-done.3 = bf16[8,2,128,256]{3,2,1,0:T(8,128)(2,1)} async-done(((bf16[8,2,128,256]{3,2,1,0:T(8,128)(2,1)}), bf16[8,2,128,256]{3,2,1,0:T(8,128)(2,1)}, u32[]{:S(2)}, u32[]{:S(2)}) %all-to-all-start.3) | async-done | bytes 1048608 | tf_op jit(solution)/shard_map/all_to_all | solution.py:35
  131.8 4.4 %all-to-all-start.4 = ((bf16[16,2,128,256]{3,2,1,0:T(8,128)(2,1)}), bf16[16,2,128,256]{3,2,1,0:T(8,128)(2,1)}, u32[]{:S(2)}, u32[]{:S(2)}) async-start(bf16[16,2,128,256]{3,2,1,0:T(8,128)(2,1)} %bitcast.177), calls=%async_computation.4 | async-start | bytes 4194304 | tf_op jit(solution)/shard_map/all_to_all | solution.py:35
  136.3 12.2 %collective-permute-start.8 = (bf16[2,128,256]{2,1,0:T(8,128)(2,1)S(1)}, bf16[2,128,256]{2,1,0:T(8,128)(2,1)S(1)}, u32[]{:S(2)}, u32[]{:S(2)}) collective-permute-start(bf16[2,128,256]{2,1,0:T(8,128)(2,1)S(1)} %convert_element_type.142), channel_id=1, source_target_pairs={{0,8},{8,0},{1,9},{9,1},{2,10},{10,2},{3,11},{11,3},{4,12},{12,4},... | collective-permute-start | bytes 393224 | tf_op jit(solution)/shard_map/ppermute | solution.py:47
  148.5 2.8 %collective-permute-done.8 = bf16[2,128,256]{2,1,0:T(8,128)(2,1)S(1)} collective-permute-done((bf16[2,128,256]{2,1,0:T(8,128)(2,1)S(1)}, bf16[2,128,256]{2,1,0:T(8,128)(2,1)S(1)}, u32[]{:S(2)}, u32[]{:S(2)}) %collective-permute-start.8) | collective-permute-done | bytes 131104 | tf_op jit(solution)/shard_map/ppermute | solution.py:47
  151.3 13.3 %all-to-all-done.4 = bf16[16,2,128,256]{3,2,1,0:T(8,128)(2,1)} async-done(((bf16[16,2,128,256]{3,2,1,0:T(8,128)(2,1)}), bf16[16,2,128,256]{3,2,1,0:T(8,128)(2,1)}, u32[]{:S(2)}, u32[]{:S(2)}) %all-to-all-start.4) | async-done | bytes 2097184 | tf_op jit(solution)/shard_map/all_to_all | solution.py:35
  166.5 12.2 %collective-permute-start.9 = (bf16[2,128,256]{2,1,0:T(8,128)(2,1)S(1)}, bf16[2,128,256]{2,1,0:T(8,128)(2,1)S(1)}, u32[]{:S(2)}, u32[]{:S(2)}) collective-permute-start(bf16[2,128,256]{2,1,0:T(8,128)(2,1)S(1)} %convert_element_type.144), channel_id=1, source_target_pairs={{0,8},{8,0},{1,9},{9,1},{2,10},{10,2},{3,11},{11,3},{4,12},{12,4},... | collective-permute-start | bytes 393224 | tf_op jit(solution)/shard_map/ppermute | solution.py:47
  181.5 6.6 %all_to_all.44 = f32[4,3,256]{2,1,0:T(4,128)S(1)} all-to-all(f32[4,3,256]{2,1,0:T(4,128)S(1)} %broadcast_in_dim.14), channel_id=1, replica_groups=mesh['z2'=2,'z1'=2,'z0'=2,'x'=4,'zh'=2,'y1'=2,'y0'=2,'c'=2] {'x'}, dimensions={0} | all-to-all | bytes 24576 | tf_op jit(solution)/shard_map/all_to_all | solution.py:31
  188.1 19.7 %all_to_all.45 = f32[8,3,256]{2,1,0:T(4,128)S(1)} all-to-all(f32[8,3,256]{2,1,0:T(4,128)S(1)} %broadcast_in_dim.15), channel_id=1, replica_groups=mesh['z2'=2,'z1'=2,'z0'=2,'x'=4,'zh'=2,'y1'=2,'y0'=2,'c'=2] {'z2','z1','..., dimensions={0} | all-to-all | bytes 49152 | tf_op jit(solution)/shard_map/all_to_all | solution.py:31
  208.0 11.4 %all_to_all.46 = bf16[4,256,256]{2,1,0:T(8,128)(2,1)S(1)} all-to-all(bf16[4,256,256]{2,1,0:T(8,128)(2,1)S(1)} %broadcast_in_dim.16), channel_id=1, replica_groups=mesh['z2'=2,'z1'=2,'z0'=2,'x'=4,'zh'=2,'y1'=2,'y0'=2,'c'=2] {'y1','y0'}, dimensions={0} | all-to-all | bytes 1048576 | tf_op jit(solution)/shard_map/all_to_all | solution.py:31
  219.4 7.2 %collective-permute-start.10 = (bf16[1,4,256,256]{3,2,1,0:T(8,128)(2,1)S(1)}, bf16[1,4,256,256]{3,2,1,0:T(8,128)(2,1)S(1)}, u32[]{:S(2)}, u32[]{:S(2)}) collective-permute-start(bf16[1,4,256,256]{3,2,1,0:T(8,128)(2,1)S(1)} %bitcast.187), channel_id=1, source_target_pairs={{0,1},{1,0},{2,3},{3,2},{4,5},{5,4},{6,7},{7,6},{8,9},{9,8},{10,11... | collective-permute-start | bytes 1572872 | tf_op jit(solution)/shard_map/ppermute | solution.py:25
  (77 shorter events, 40.6 us)
Async XLA Ops:
  0.6 95.8 %copy-start = (bf16[512,256]{1,0:T(8,128)(2,1)S(1)}, bf16[512,256]{1,0:T(8,128)(2,1)}, u32[]{:S(2)}) copy-start(bf16[512,256]{1,0:T(8,128)(2,1)} %param.8) | copy-start | bytes 786436
  0.6 7.8 %copy-start.3 = (bf16[64,512]{1,0:T(8,128)(2,1)S(1)}, bf16[64,512]{1,0:T(8,128)(2,1)}, u32[]{:S(2)}) copy-start(bf16[64,512]{1,0:T(8,128)(2,1)} %param.7) | copy-start | bytes 196612
  0.7 26.6 %copy-start.4 = (s32[128]{0:T(128)S(1)}, s32[128]{0:T(128)}, u32[]{:S(2)}) copy-start(s32[128]{0:T(128)} %param.9) | copy-start | bytes 1540
  3.6 15.3 %all-to-all-start = ((bf16[4,320,256]{2,1,0:T(8,128)(2,1)}), bf16[4,320,256]{2,1,0:T(8,128)(2,1)S(1)}, u32[]{:S(2)}, u32[]{:S(2)}) async-start(bf16[4,320,256]{2,1,0:T(8,128)(2,1)} %pad_maximum_fusion.3), calls=%async_computation | async-start | bytes 1310720 | tf_op jit(solution)/shard_map/all_to_all | solution.py:69
  8.4 10.5 %collective-permute-start = (bf16[64,512]{1,0:T(8,128)(2,1)S(1)}, bf16[64,512]{1,0:T(8,128)(2,1)S(1)}, u32[]{:S(2)}, u32[]{:S(2)}) collective-permute-start(bf16[64,512]{1,0:T(8,128)(2,1)S(1)} %copy-done.3), channel_id=1, source_target_pairs={{0,256},{256,0},{1,257},{257,1},{2,258},{258,2},{3,259},{259,3},{4... | collective-permute-start | bytes 196616 | tf_op jit(solution)/shard_map/ppermute | solution.py:25
  18.9 41.1 %copy-start.1 = (bf16[4,320,256]{2,1,0:T(8,128)(2,1)}, bf16[4,320,256]{2,1,0:T(8,128)(2,1)S(1)}, u32[]{:S(2)}) copy-start(bf16[4,320,256]{2,1,0:T(8,128)(2,1)S(1)} %all-to-all-done) | copy-start | bytes 1966084
  18.9 20.9 %collective-permute-start.2 = (bf16[256,256]{1,0:T(8,128)(2,1)S(1)}, bf16[256,256]{1,0:T(8,128)(2,1)S(1)}, u32[]{:S(2)}, u32[]{:S(2)}) collective-permute-start(bf16[256,256]{1,0:T(8,128)(2,1)S(1)} %bitcast.198), channel_id=1, source_target_pairs={{0,256},{256,0},{1,257},{257,1},{2,258},{258,2},{3,259},{259,3},{4... | collective-permute-start | bytes 393224 | tf_op jit(solution)/shard_map/ppermute | solution.py:25
  27.8 19.3 %all-to-all-start.1 = ((s32[8,1,128]{2,1,0:T(1,128)}), s32[8,1,128]{2,1,0:T(1,128)S(1)}, u32[]{:S(2)}, u32[]{:S(2)}) async-start(s32[8,1,128]{2,1,0:T(1,128)} %broadcast_in_dim.12), calls=%async_computation.1 | async-start | bytes 8192 | tf_op jit(solution)/shard_map/all_to_all | solution.py:31
  34.4 12.6 %collective-permute-start.1 = (bf16[128,512]{1,0:T(8,128)(2,1)S(1)}, bf16[128,512]{1,0:T(8,128)(2,1)S(1)}, u32[]{:S(2)}, u32[]{:S(2)}) collective-permute-start(bf16[128,512]{1,0:T(8,128)(2,1)S(1)} %bitcast.196), channel_id=1, source_target_pairs={{0,128},{128,0},{1,129},{129,1},{2,130},{130,2},{3,131},{131,3},{4... | collective-permute-start | bytes 393224 | tf_op jit(solution)/shard_map/ppermute | solution.py:25
  47.1 12.8 %collective-permute-start.3 = (bf16[256,512]{1,0:T(8,128)(2,1)S(1)}, bf16[256,512]{1,0:T(8,128)(2,1)S(1)}, u32[]{:S(2)}, u32[]{:S(2)}) collective-permute-start(bf16[256,512]{1,0:T(8,128)(2,1)S(1)} %bitcast.194), channel_id=1, source_target_pairs={{0,64},{64,0},{1,65},{65,1},{2,66},{66,2},{3,67},{67,3},{4,68},{68... | collective-permute-start | bytes 786440 | tf_op jit(solution)/shard_map/ppermute | solution.py:25
  49.1 16.6 %collective-permute-start.4 = (bf16[512,256]{1,0:T(8,128)(2,1)S(1)}, bf16[512,256]{1,0:T(8,128)(2,1)S(1)}, u32[]{:S(2)}, u32[]{:S(2)}) collective-permute-start(bf16[512,256]{1,0:T(8,128)(2,1)S(1)} %bitcast.192), channel_id=1, source_target_pairs={{0,128},{128,0},{1,129},{129,1},{2,130},{130,2},{3,131},{131,3},{4... | collective-permute-start | bytes 786440 | tf_op jit(solution)/shard_map/ppermute | solution.py:25
  67.4 29.0 %all-to-all-start.2 = ((bf16[4,512,512]{2,1,0:T(8,128)(2,1)}), bf16[4,512,512]{2,1,0:T(8,128)(2,1)S(1)}, u32[]{:S(2)}, u32[]{:S(2)}) async-start(bf16[4,512,512]{2,1,0:T(8,128)(2,1)} %broadcast_in_dim.13), calls=%async_computation.2 | async-start | bytes 4194304 | tf_op jit(solution)/shard_map/all_to_all | solution.py:31
  71.6 22.7 %collective-permute-start.5 = (bf16[1024,256]{1,0:T(8,128)(2,1)S(1)}, bf16[1024,256]{1,0:T(8,128)(2,1)S(1)}, u32[]{:S(2)}, u32[]{:S(2)}) collective-permute-start(bf16[1024,256]{1,0:T(8,128)(2,1)S(1)} %bitcast.185), channel_id=1, source_target_pairs={{0,64},{64,0},{1,65},{65,1},{2,66},{66,2},{3,67},{67,3},{4,68},{68... | collective-permute-start | bytes 1572872 | tf_op jit(solution)/shard_map/ppermute | solution.py:25
  73.5 20.8 %collective-permute-start.6 = (s32[8,128]{1,0:T(8,128)S(1)}, s32[8,128]{1,0:T(8,128)S(1)}, u32[]{:S(2)}, u32[]{:S(2)}) collective-permute-start(s32[8,128]{1,0:T(8,128)S(1)} %bitcast.202), channel_id=1, source_target_pairs={{0,8},{8,0},{1,9},{9,1},{2,10},{10,2},{3,11},{11,3},{4,12},{12,4},... | collective-permute-start | bytes 12296 | tf_op jit(solution)/shard_map/ppermute | solution.py:25
  98.2 1.1 copy-start.2
  102.1 25.5 %collective-permute-start.7 = (bf16[4,1024,256]{2,1,0:T(8,128)(2,1)}, bf16[4,1024,256]{2,1,0:T(8,128)(2,1)}, u32[]{:S(2)}, u32[]{:S(2)}) collective-permute-start(bf16[4,1024,256]{2,1,0:T(8,128)(2,1)} %pad_maximum_fusion), channel_id=1, source_target_pairs={{0,1},{1,0},{2,3},{3,2},{4,5},{5,4},{6,7},{7,6},{8,9},{9,8},{10,11... | collective-permute-start | bytes 6291464 | tf_op jit(solution)/shard_map/ppermute | solution.py:102
  106.5 19.7 %all-to-all-start.3 = ((bf16[8,2,128,256]{3,2,1,0:T(8,128)(2,1)}), bf16[8,2,128,256]{3,2,1,0:T(8,128)(2,1)}, u32[]{:S(2)}, u32[]{:S(2)}) async-start(bf16[8,2,128,256]{3,2,1,0:T(8,128)(2,1)} %bitcast.179), calls=%async_computation.3 | async-start | bytes 2097152 | tf_op jit(solution)/shard_map/all_to_all | solution.py:35
  131.8 32.8 %all-to-all-start.4 = ((bf16[16,2,128,256]{3,2,1,0:T(8,128)(2,1)}), bf16[16,2,128,256]{3,2,1,0:T(8,128)(2,1)}, u32[]{:S(2)}, u32[]{:S(2)}) async-start(bf16[16,2,128,256]{3,2,1,0:T(8,128)(2,1)} %bitcast.177), calls=%async_computation.4 | async-start | bytes 4194304 | tf_op jit(solution)/shard_map/all_to_all | solution.py:35
  136.3 15.0 %collective-permute-start.8 = (bf16[2,128,256]{2,1,0:T(8,128)(2,1)S(1)}, bf16[2,128,256]{2,1,0:T(8,128)(2,1)S(1)}, u32[]{:S(2)}, u32[]{:S(2)}) collective-permute-start(bf16[2,128,256]{2,1,0:T(8,128)(2,1)S(1)} %convert_element_type.142), channel_id=1, source_target_pairs={{0,8},{8,0},{1,9},{9,1},{2,10},{10,2},{3,11},{11,3},{4,12},{12,4},... | collective-permute-start | bytes 393224 | tf_op jit(solution)/shard_map/ppermute | solution.py:47
  166.5 14.6 %collective-permute-start.9 = (bf16[2,128,256]{2,1,0:T(8,128)(2,1)S(1)}, bf16[2,128,256]{2,1,0:T(8,128)(2,1)S(1)}, u32[]{:S(2)}, u32[]{:S(2)}) collective-permute-start(bf16[2,128,256]{2,1,0:T(8,128)(2,1)S(1)} %convert_element_type.144), channel_id=1, source_target_pairs={{0,8},{8,0},{1,9},{9,1},{2,10},{10,2},{3,11},{11,3},{4,12},{12,4},... | collective-permute-start | bytes 393224 | tf_op jit(solution)/shard_map/ppermute | solution.py:47
  219.4 8.7 %collective-permute-start.10 = (bf16[1,4,256,256]{3,2,1,0:T(8,128)(2,1)S(1)}, bf16[1,4,256,256]{3,2,1,0:T(8,128)(2,1)S(1)}, u32[]{:S(2)}, u32[]{:S(2)}) collective-permute-start(bf16[1,4,256,256]{3,2,1,0:T(8,128)(2,1)S(1)} %bitcast.187), channel_id=1, source_target_pairs={{0,1},{1,0},{2,3},{3,2},{4,5},{5,4},{6,7},{7,6},{8,9},{9,8},{10,11... | collective-permute-start | bytes 1572872 | tf_op jit(solution)/shard_map/ppermute | solution.py:25

commit v4 on v3

--- a/solution.py
+++ b/solution.py
@@ -71,18 +71,18 @@
     teacher = quarters[:, :rows].reshape(4 * rows, part_width)
     weights = quarters[:, rows:]
     student, teacher, orders = together(
-        swap_in(student, "z1"), swap_in(teacher, "z2"), spread(owner_order, YC)
+        swap_in(student, "z1"), swap_in(teacher, "z2"), owner_order
     )
-    student, teacher, orders = together(swap_in(student, "z0"), swap_in(teacher, "z1"), orders)
+    student, orders = together(swap_in(student, "z0"), spread(orders, YC))
     student_all, teacher, orders = together(
-        spread(student, "x"), swap_in(teacher, "z0"), swap_in(orders, "zh")
+        spread(student, "x"), swap_in(swap_in(teacher, "z1"), "z0"), swap_in(orders, "zh")
     )
     student_all = student_all.reshape(total_rows, student_width)
     student_part = jnp.dot(student_all, projection, preferred_element_type=F32).astype(BF16)
     student_part = student_part.reshape(2, 2, 2, 2, 2, rows, out_width)
     student_part = student_part.transpose(3, 2, 0, 4, 1, 5, 6).reshape(8, 2, block, out_width)
     student_part, teacher = together(student_part, teacher)
-    student_part = summed(student_part, YC)
+    student_part = lax.all_to_all(student_part, YC, split_axis=0, concat_axis=0, tiled=True)
     pick = orders[:, :, None] == lax.broadcasted_iota(jnp.int32, (groups, block, block), 2)
     pick = pick.astype(BF16)
 
@@ -107,7 +107,7 @@
     part = part.reshape(16, 2, block, out_width)
     part, student_part = together(part, student_part)
     part = summed(part, ("x", "y1", "y0"))
-    student_out = both_owners(student_part)
+    student_out = both_owners(jnp.sum(student_part.astype(F32), axis=0))
     part, student_out = together(part, student_out)
     target = both_owners(part).astype(BF16)
     target = target.astype(F32)

time: 231 us -> 222 us (0.961)
  starting transfers between devices: 104 us -> 100 us
  matrix products: 11.9 us -> 8.7 us
  waiting for transfers between devices: 57.3 us -> 54.4 us
    all_to_all x2 -> x1, waiting for transfers between devices: 20.4 us -> 1.3 us  [summed(): part = lax.all_to_all(pieces, axis, split_axis=0, concat_axis=0, tiled=True)]
    ppermute x2, waiting for transfers between devices: 5.2 us -> 22.7 us  [both_owners(): other = lax.ppermute(part.astype(BF16), 'zh', SWAP)]
    ppermute x2, starting transfers between devices: 24.4 us -> 15.6 us  [both_owners(): other = lax.ppermute(part.astype(BF16), 'zh', SWAP)]
    ppermute x8, waiting for transfers between devices: 29.8 us -> 22 us  [swap_in(): return in_order(value, lax.ppermute(value, axis, SWAP), axis)]
    all_to_all x0 -> x1, waiting for transfers between devices: none -> 6.62 us  [shards(): lax.all_to_all(student_part, YC, split_axis=0, concat_axis=0, tiled=True)]
    ppermute x8, starting transfers between devices: 50.7 us -> 56.9 us  [swap_in(): return in_order(value, lax.ppermute(value, axis, SWAP), axis)]
    all_to_all x0 -> x1, starting transfers between devices: none -> 4.21 us  [shards(): lax.all_to_all(student_part, YC, split_axis=0, concat_axis=0, tiled=True)]
    all_to_all x2 -> x1, starting transfers between devices: 8.95 us -> 5.4 us  [summed(): part = lax.all_to_all(pieces, axis, split_axis=0, concat_axis=0, tiled=True)]
  transfers between devices with their start and end apart: 16 -> 16, of which waited for: 11 -> 10; matrix products, arithmetic and copies ran while one was open for 5% -> 6% of each run, Pallas kernels for 0% -> 0%
where the time goes in v4:
time: 222 us; the launch traced here: 221 us
  starting transfers between devices  100 us (45%)
  waiting for transfers between devices  54.4 us (25%)
  blocking collectives  39.4 us (18%)
  other arithmetic  11.8 us (5%)
  matrix products  8.7 us (4%)
  local copies, waits for them, and re-layouts  5.54 us (2%)
    ppermute x8, starting transfers between devices, swap_in(): return in_order(value, lax.ppermute(value, axis, SWAP), axis)  56.9 us
    all_to_all x3, blocking collectives, spread(): return lax.all_to_all(copies, axis, split_axis=0, concat_axis=0, tiled=True)  39.4 us
    ppermute x2, waiting for transfers between devices, both_owners(): other = lax.ppermute(part.astype(BF16), 'zh', SWAP)  22.7 us
    ppermute x8, waiting for transfers between devices, swap_in(): return in_order(value, lax.ppermute(value, axis, SWAP), axis)  22 us
    ppermute x2, starting transfers between devices, both_owners(): other = lax.ppermute(part.astype(BF16), 'zh', SWAP)  15.6 us
    all_to_all x2, starting transfers between devices, spread(): return lax.all_to_all(copies, axis, split_axis=0, concat_axis=0, tiled=True)  9.32 us
    all_to_all x1, waiting for transfers between devices, shards(): lax.all_to_all(student_part, YC, split_axis=0, concat_axis=0, tiled=True)  6.62 us
    dot_general x8, matrix products, product(): jnp.dot(one, weights[place], preferred_element_type=F32).astype(BF16)  5.96 us
  transfers between devices with their start and end apart: 16, of which 10 were waited for; matrix products, arithmetic and copies ran while one was open for 6% of the time, Pallas kernels for 0%

profile of v4, /device:TPU:1, one launch (start us, length us, event | category | flops | bytes accessed | tf_op | source)
XLA Modules:
  0.0 221.0 jit_solution(2720451170230556566)
XLA Ops:
  3.6 5.0 %all-to-all-start = ((bf16[4,320,256]{2,1,0:T(8,128)(2,1)}), bf16[4,320,256]{2,1,0:T(8,128)(2,1)S(1)}, u32[]{:S(2)}, u32[]{:S(2)}) async-start(bf16[4,320,256]{2,1,0:T(8,128)(2,1)} %pad_maximum_fusion.3), calls=%async_computation | async-start | bytes 1310720 | tf_op jit(solution)/shard_map/all_to_all | solution.py:69
  8.5 8.8 %collective-permute-start = (bf16[64,512]{1,0:T(8,128)(2,1)S(1)}, bf16[64,512]{1,0:T(8,128)(2,1)S(1)}, u32[]{:S(2)}, u32[]{:S(2)}) collective-permute-start(bf16[64,512]{1,0:T(8,128)(2,1)S(1)} %copy-done.3), channel_id=1, source_target_pairs={{0,256},{256,0},{1,257},{257,1},{2,258},{258,2},{3,259},{259,3},{4... | collective-permute-start | bytes 196616 | tf_op jit(solution)/shard_map/ppermute | solution.py:25
  19.1 8.3 %collective-permute-start.2 = (bf16[256,256]{1,0:T(8,128)(2,1)S(1)}, bf16[256,256]{1,0:T(8,128)(2,1)S(1)}, u32[]{:S(2)}, u32[]{:S(2)}) collective-permute-start(bf16[256,256]{1,0:T(8,128)(2,1)S(1)} %bitcast.199), channel_id=1, source_target_pairs={{0,256},{256,0},{1,257},{257,1},{2,258},{258,2},{3,259},{259,3},{4... | collective-permute-start | bytes 393224 | tf_op jit(solution)/shard_map/ppermute | solution.py:25
  27.4 6.7 %collective-permute-start.1 = (bf16[128,512]{1,0:T(8,128)(2,1)S(1)}, bf16[128,512]{1,0:T(8,128)(2,1)S(1)}, u32[]{:S(2)}, u32[]{:S(2)}) collective-permute-start(bf16[128,512]{1,0:T(8,128)(2,1)S(1)} %bitcast.197), channel_id=1, source_target_pairs={{0,128},{128,0},{1,129},{129,1},{2,130},{130,2},{3,131},{131,3},{4... | collective-permute-start | bytes 393224 | tf_op jit(solution)/shard_map/ppermute | solution.py:25
  34.2 3.2 %collective-permute-done.1 = bf16[128,512]{1,0:T(8,128)(2,1)S(1)} collective-permute-done((bf16[128,512]{1,0:T(8,128)(2,1)S(1)}, bf16[128,512]{1,0:T(8,128)(2,1)S(1)}, u32[]{:S(2)}, u32[]{:S(2)}) %collective-permute-start.1) | collective-permute-done | bytes 131104 | tf_op jit(solution)/shard_map/ppermute | solution.py:25
  37.5 7.8 %collective-permute-start.3 = (bf16[256,512]{1,0:T(8,128)(2,1)S(1)}, bf16[256,512]{1,0:T(8,128)(2,1)S(1)}, u32[]{:S(2)}, u32[]{:S(2)}) collective-permute-start(bf16[256,512]{1,0:T(8,128)(2,1)S(1)} %bitcast.195), channel_id=1, source_target_pairs={{0,64},{64,0},{1,65},{65,1},{2,66},{66,2},{3,67},{67,3},{4,68},{68... | collective-permute-start | bytes 786440 | tf_op jit(solution)/shard_map/ppermute | solution.py:25
  45.9 5.7 %all-to-all-start.1 = ((s32[8,1,128]{2,1,0:T(1,128)}), s32[8,1,128]{2,1,0:T(1,128)S(1)}, u32[]{:S(2)}, u32[]{:S(2)}) async-start(s32[8,1,128]{2,1,0:T(1,128)} %broadcast_in_dim.12), calls=%async_computation.1 | async-start | bytes 8192 | tf_op jit(solution)/shard_map/all_to_all | solution.py:31
  51.6 2.5 %collective-permute-start.4 = (bf16[512,256]{1,0:T(8,128)(2,1)S(1)}, bf16[512,256]{1,0:T(8,128)(2,1)S(1)}, u32[]{:S(2)}, u32[]{:S(2)}) collective-permute-start(bf16[512,256]{1,0:T(8,128)(2,1)S(1)} %bitcast.193), channel_id=1, source_target_pairs={{0,128},{128,0},{1,129},{129,1},{2,130},{130,2},{3,131},{131,3},{4... | collective-permute-start | bytes 786440 | tf_op jit(solution)/shard_map/ppermute | solution.py:25
  57.6 3.6 %all-to-all-start.2 = ((bf16[4,512,512]{2,1,0:T(8,128)(2,1)}), bf16[4,512,512]{2,1,0:T(8,128)(2,1)S(1)}, u32[]{:S(2)}, u32[]{:S(2)}) async-start(bf16[4,512,512]{2,1,0:T(8,128)(2,1)} %broadcast_in_dim.13), calls=%async_computation.2 | async-start | bytes 4194304 | tf_op jit(solution)/shard_map/all_to_all | solution.py:31
  61.3 6.7 %collective-permute-done.4 = bf16[512,256]{1,0:T(8,128)(2,1)S(1)} collective-permute-done((bf16[512,256]{1,0:T(8,128)(2,1)S(1)}, bf16[512,256]{1,0:T(8,128)(2,1)S(1)}, u32[]{:S(2)}, u32[]{:S(2)}) %collective-permute-start.4) | collective-permute-done | bytes 262176 | tf_op jit(solution)/shard_map/ppermute | solution.py:25
  70.0 12.6 %collective-permute-start.6 = (s32[8,128]{1,0:T(8,128)S(1)}, s32[8,128]{1,0:T(8,128)S(1)}, u32[]{:S(2)}, u32[]{:S(2)}) collective-permute-start(s32[8,128]{1,0:T(8,128)S(1)} %bitcast.203), channel_id=1, source_target_pairs={{0,8},{8,0},{1,9},{9,1},{2,10},{10,2},{3,11},{11,3},{4,12},{12,4},... | collective-permute-start | bytes 12296 | tf_op jit(solution)/shard_map/ppermute | solution.py:25
  82.6 9.5 %collective-permute-done.6 = s32[8,128]{1,0:T(8,128)S(1)} collective-permute-done((s32[8,128]{1,0:T(8,128)S(1)}, s32[8,128]{1,0:T(8,128)S(1)}, u32[]{:S(2)}, u32[]{:S(2)}) %collective-permute-start.6) | collective-permute-done | bytes 4128 | tf_op jit(solution)/shard_map/ppermute | solution.py:25
  98.1 3.6 %collective-permute-start.7 = (bf16[4,1024,256]{2,1,0:T(8,128)(2,1)}, bf16[4,1024,256]{2,1,0:T(8,128)(2,1)}, u32[]{:S(2)}, u32[]{:S(2)}) collective-permute-start(bf16[4,1024,256]{2,1,0:T(8,128)(2,1)} %pad_maximum_fusion), channel_id=1, source_target_pairs={{0,1},{1,0},{2,3},{3,2},{4,5},{5,4},{6,7},{7,6},{8,9},{9,8},{10,11... | collective-permute-start | bytes 6291464 | tf_op jit(solution)/shard_map/ppermute | solution.py:102
  101.7 4.2 %all-to-all-start.3 = ((bf16[8,2,128,256]{3,2,1,0:T(8,128)(2,1)}), bf16[8,2,128,256]{3,2,1,0:T(8,128)(2,1)}, u32[]{:S(2)}, u32[]{:S(2)}) async-start(bf16[8,2,128,256]{3,2,1,0:T(8,128)(2,1)} %bitcast.181), calls=%async_computation.3 | async-start | bytes 2097152 | tf_op jit(solution)/shard_map/all_to_all | solution.py:85
  114.5 6.6 %all-to-all-done.3 = bf16[8,2,128,256]{3,2,1,0:T(8,128)(2,1)} async-done(((bf16[8,2,128,256]{3,2,1,0:T(8,128)(2,1)}), bf16[8,2,128,256]{3,2,1,0:T(8,128)(2,1)}, u32[]{:S(2)}, u32[]{:S(2)}) %all-to-all-start.3) | async-done | bytes 1048608 | tf_op jit(solution)/shard_map/all_to_all | solution.py:85
  121.1 5.4 %all-to-all-start.4 = ((bf16[16,2,128,256]{3,2,1,0:T(8,128)(2,1)}), bf16[16,2,128,256]{3,2,1,0:T(8,128)(2,1)}, u32[]{:S(2)}, u32[]{:S(2)}) async-start(bf16[16,2,128,256]{3,2,1,0:T(8,128)(2,1)} %bitcast.179), calls=%async_computation.4 | async-start | bytes 4194304 | tf_op jit(solution)/shard_map/all_to_all | solution.py:35
  127.9 6.9 %collective-permute-start.8 = (bf16[2,128,256]{2,1,0:T(8,128)(2,1)S(1)}, bf16[2,128,256]{2,1,0:T(8,128)(2,1)S(1)}, u32[]{:S(2)}, u32[]{:S(2)}) collective-permute-start(bf16[2,128,256]{2,1,0:T(8,128)(2,1)S(1)} %convert_element_type.142), channel_id=1, source_target_pairs={{0,8},{8,0},{1,9},{9,1},{2,10},{10,2},{3,11},{11,3},{4,12},{12,4},... | collective-permute-start | bytes 393224 | tf_op jit(solution)/shard_map/ppermute | solution.py:47
  134.8 16.9 %collective-permute-done.8 = bf16[2,128,256]{2,1,0:T(8,128)(2,1)S(1)} collective-permute-done((bf16[2,128,256]{2,1,0:T(8,128)(2,1)S(1)}, bf16[2,128,256]{2,1,0:T(8,128)(2,1)S(1)}, u32[]{:S(2)}, u32[]{:S(2)}) %collective-permute-start.8) | collective-permute-done | bytes 131104 | tf_op jit(solution)/shard_map/ppermute | solution.py:47
  154.9 8.7 %collective-permute-start.9 = (bf16[2,128,256]{2,1,0:T(8,128)(2,1)S(1)}, bf16[2,128,256]{2,1,0:T(8,128)(2,1)S(1)}, u32[]{:S(2)}, u32[]{:S(2)}) collective-permute-start(bf16[2,128,256]{2,1,0:T(8,128)(2,1)S(1)} %convert_element_type.144), channel_id=1, source_target_pairs={{0,8},{8,0},{1,9},{9,1},{2,10},{10,2},{3,11},{11,3},{4,12},{12,4},... | collective-permute-start | bytes 393224 | tf_op jit(solution)/shard_map/ppermute | solution.py:47
  163.6 5.8 %collective-permute-done.9 = bf16[2,128,256]{2,1,0:T(8,128)(2,1)S(1)} collective-permute-done((bf16[2,128,256]{2,1,0:T(8,128)(2,1)S(1)}, bf16[2,128,256]{2,1,0:T(8,128)(2,1)S(1)}, u32[]{:S(2)}, u32[]{:S(2)}) %collective-permute-start.9) | collective-permute-done | bytes 131104 | tf_op jit(solution)/shard_map/ppermute | solution.py:47
  169.8 15.7 %all_to_all.44 = f32[4,3,256]{2,1,0:T(4,128)S(1)} all-to-all(f32[4,3,256]{2,1,0:T(4,128)S(1)} %broadcast_in_dim.14), channel_id=1, replica_groups=mesh['z2'=2,'z1'=2,'z0'=2,'x'=4,'zh'=2,'y1'=2,'y0'=2,'c'=2] {'x'}, dimensions={0} | all-to-all | bytes 24576 | tf_op jit(solution)/shard_map/all_to_all | solution.py:31
  185.5 11.9 %all_to_all.45 = f32[8,3,256]{2,1,0:T(4,128)S(1)} all-to-all(f32[8,3,256]{2,1,0:T(4,128)S(1)} %broadcast_in_dim.15), channel_id=1, replica_groups=mesh['z2'=2,'z1'=2,'z0'=2,'x'=4,'zh'=2,'y1'=2,'y0'=2,'c'=2] {'z2','z1','..., dimensions={0} | all-to-all | bytes 49152 | tf_op jit(solution)/shard_map/all_to_all | solution.py:31
  197.6 11.8 %all_to_all.46 = bf16[4,256,256]{2,1,0:T(8,128)(2,1)S(1)} all-to-all(bf16[4,256,256]{2,1,0:T(8,128)(2,1)S(1)} %broadcast_in_dim.16), channel_id=1, replica_groups=mesh['z2'=2,'z1'=2,'z0'=2,'x'=4,'zh'=2,'y1'=2,'y0'=2,'c'=2] {'y1','y0'}, dimensions={0} | all-to-all | bytes 1048576 | tf_op jit(solution)/shard_map/all_to_all | solution.py:31
  209.4 8.2 %collective-permute-start.10 = (bf16[1,4,256,256]{3,2,1,0:T(8,128)(2,1)S(1)}, bf16[1,4,256,256]{3,2,1,0:T(8,128)(2,1)S(1)}, u32[]{:S(2)}, u32[]{:S(2)}) collective-permute-start(bf16[1,4,256,256]{3,2,1,0:T(8,128)(2,1)S(1)} %bitcast.188), channel_id=1, source_target_pairs={{0,1},{1,0},{2,3},{3,2},{4,5},{5,4},{6,7},{7,6},{8,9},{9,8},{10,11... | collective-permute-start | bytes 1572872 | tf_op jit(solution)/shard_map/ppermute | solution.py:25
  (77 shorter events, 33.7 us)
Async XLA Ops:
  0.6 91.7 %copy-start = (bf16[512,256]{1,0:T(8,128)(2,1)S(1)}, bf16[512,256]{1,0:T(8,128)(2,1)}, u32[]{:S(2)}) copy-start(bf16[512,256]{1,0:T(8,128)(2,1)} %param.8) | copy-start | bytes 786436
  0.6 7.9 %copy-start.3 = (bf16[64,512]{1,0:T(8,128)(2,1)S(1)}, bf16[64,512]{1,0:T(8,128)(2,1)}, u32[]{:S(2)}) copy-start(bf16[64,512]{1,0:T(8,128)(2,1)} %param.7) | copy-start | bytes 196612
  3.6 41.7 %copy-start.4 = (s32[128]{0:T(128)S(1)}, s32[128]{0:T(128)}, u32[]{:S(2)}) copy-start(s32[128]{0:T(128)} %param.9) | copy-start | bytes 1540
  3.6 15.5 %all-to-all-start = ((bf16[4,320,256]{2,1,0:T(8,128)(2,1)}), bf16[4,320,256]{2,1,0:T(8,128)(2,1)S(1)}, u32[]{:S(2)}, u32[]{:S(2)}) async-start(bf16[4,320,256]{2,1,0:T(8,128)(2,1)} %pad_maximum_fusion.3), calls=%async_computation | async-start | bytes 1310720 | tf_op jit(solution)/shard_map/all_to_all | solution.py:69
  8.5 10.5 %collective-permute-start = (bf16[64,512]{1,0:T(8,128)(2,1)S(1)}, bf16[64,512]{1,0:T(8,128)(2,1)S(1)}, u32[]{:S(2)}, u32[]{:S(2)}) collective-permute-start(bf16[64,512]{1,0:T(8,128)(2,1)S(1)} %copy-done.3), channel_id=1, source_target_pairs={{0,256},{256,0},{1,257},{257,1},{2,258},{258,2},{3,259},{259,3},{4... | collective-permute-start | bytes 196616 | tf_op jit(solution)/shard_map/ppermute | solution.py:25
  19.1 35.2 %copy-start.1 = (bf16[4,320,256]{2,1,0:T(8,128)(2,1)}, bf16[4,320,256]{2,1,0:T(8,128)(2,1)S(1)}, u32[]{:S(2)}) copy-start(bf16[4,320,256]{2,1,0:T(8,128)(2,1)S(1)} %all-to-all-done) | copy-start | bytes 1966084
  19.1 15.0 %collective-permute-start.2 = (bf16[256,256]{1,0:T(8,128)(2,1)S(1)}, bf16[256,256]{1,0:T(8,128)(2,1)S(1)}, u32[]{:S(2)}, u32[]{:S(2)}) collective-permute-start(bf16[256,256]{1,0:T(8,128)(2,1)S(1)} %bitcast.199), channel_id=1, source_target_pairs={{0,256},{256,0},{1,257},{257,1},{2,258},{258,2},{3,259},{259,3},{4... | collective-permute-start | bytes 393224 | tf_op jit(solution)/shard_map/ppermute | solution.py:25
  27.4 10.0 %collective-permute-start.1 = (bf16[128,512]{1,0:T(8,128)(2,1)S(1)}, bf16[128,512]{1,0:T(8,128)(2,1)S(1)}, u32[]{:S(2)}, u32[]{:S(2)}) collective-permute-start(bf16[128,512]{1,0:T(8,128)(2,1)S(1)} %bitcast.197), channel_id=1, source_target_pairs={{0,128},{128,0},{1,129},{129,1},{2,130},{130,2},{3,131},{131,3},{4... | collective-permute-start | bytes 393224 | tf_op jit(solution)/shard_map/ppermute | solution.py:25
  37.5 16.7 %collective-permute-start.3 = (bf16[256,512]{1,0:T(8,128)(2,1)S(1)}, bf16[256,512]{1,0:T(8,128)(2,1)S(1)}, u32[]{:S(2)}, u32[]{:S(2)}) collective-permute-start(bf16[256,512]{1,0:T(8,128)(2,1)S(1)} %bitcast.195), channel_id=1, source_target_pairs={{0,64},{64,0},{1,65},{65,1},{2,66},{66,2},{3,67},{67,3},{4,68},{68... | collective-permute-start | bytes 786440 | tf_op jit(solution)/shard_map/ppermute | solution.py:25
  45.9 10.2 %all-to-all-start.1 = ((s32[8,1,128]{2,1,0:T(1,128)}), s32[8,1,128]{2,1,0:T(1,128)S(1)}, u32[]{:S(2)}, u32[]{:S(2)}) async-start(s32[8,1,128]{2,1,0:T(1,128)} %broadcast_in_dim.12), calls=%async_computation.1 | async-start | bytes 8192 | tf_op jit(solution)/shard_map/all_to_all | solution.py:31
  51.6 16.3 %collective-permute-start.4 = (bf16[512,256]{1,0:T(8,128)(2,1)S(1)}, bf16[512,256]{1,0:T(8,128)(2,1)S(1)}, u32[]{:S(2)}, u32[]{:S(2)}) collective-permute-start(bf16[512,256]{1,0:T(8,128)(2,1)S(1)} %bitcast.193), channel_id=1, source_target_pairs={{0,128},{128,0},{1,129},{129,1},{2,130},{130,2},{3,131},{131,3},{4... | collective-permute-start | bytes 786440 | tf_op jit(solution)/shard_map/ppermute | solution.py:25
  57.6 34.7 %all-to-all-start.2 = ((bf16[4,512,512]{2,1,0:T(8,128)(2,1)}), bf16[4,512,512]{2,1,0:T(8,128)(2,1)S(1)}, u32[]{:S(2)}, u32[]{:S(2)}) async-start(bf16[4,512,512]{2,1,0:T(8,128)(2,1)} %broadcast_in_dim.13), calls=%async_computation.2 | async-start | bytes 4194304 | tf_op jit(solution)/shard_map/all_to_all | solution.py:31
  68.0 24.1 %collective-permute-start.5 = (bf16[1024,256]{1,0:T(8,128)(2,1)S(1)}, bf16[1024,256]{1,0:T(8,128)(2,1)S(1)}, u32[]{:S(2)}, u32[]{:S(2)}) collective-permute-start(bf16[1024,256]{1,0:T(8,128)(2,1)S(1)} %bitcast.187), channel_id=1, source_target_pairs={{0,64},{64,0},{1,65},{65,1},{2,66},{66,2},{3,67},{67,3},{4,68},{68... | collective-permute-start | bytes 1572872 | tf_op jit(solution)/shard_map/ppermute | solution.py:25
  70.0 22.1 %collective-permute-start.6 = (s32[8,128]{1,0:T(8,128)S(1)}, s32[8,128]{1,0:T(8,128)S(1)}, u32[]{:S(2)}, u32[]{:S(2)}) collective-permute-start(s32[8,128]{1,0:T(8,128)S(1)} %bitcast.203), channel_id=1, source_target_pairs={{0,8},{8,0},{1,9},{9,1},{2,10},{10,2},{3,11},{11,3},{4,12},{12,4},... | collective-permute-start | bytes 12296 | tf_op jit(solution)/shard_map/ppermute | solution.py:25
  94.2 1.1 copy-start.2
  98.1 12.7 %collective-permute-start.7 = (bf16[4,1024,256]{2,1,0:T(8,128)(2,1)}, bf16[4,1024,256]{2,1,0:T(8,128)(2,1)}, u32[]{:S(2)}, u32[]{:S(2)}) collective-permute-start(bf16[4,1024,256]{2,1,0:T(8,128)(2,1)} %pad_maximum_fusion), channel_id=1, source_target_pairs={{0,1},{1,0},{2,3},{3,2},{4,5},{5,4},{6,7},{7,6},{8,9},{9,8},{10,11... | collective-permute-start | bytes 6291464 | tf_op jit(solution)/shard_map/ppermute | solution.py:102
  101.7 19.4 %all-to-all-start.3 = ((bf16[8,2,128,256]{3,2,1,0:T(8,128)(2,1)}), bf16[8,2,128,256]{3,2,1,0:T(8,128)(2,1)}, u32[]{:S(2)}, u32[]{:S(2)}) async-start(bf16[8,2,128,256]{3,2,1,0:T(8,128)(2,1)} %bitcast.181), calls=%async_computation.3 | async-start | bytes 2097152 | tf_op jit(solution)/shard_map/all_to_all | solution.py:85
  121.1 31.9 %all-to-all-start.4 = ((bf16[16,2,128,256]{3,2,1,0:T(8,128)(2,1)}), bf16[16,2,128,256]{3,2,1,0:T(8,128)(2,1)}, u32[]{:S(2)}, u32[]{:S(2)}) async-start(bf16[16,2,128,256]{3,2,1,0:T(8,128)(2,1)} %bitcast.179), calls=%async_computation.4 | async-start | bytes 4194304 | tf_op jit(solution)/shard_map/all_to_all | solution.py:35
  127.9 23.8 %collective-permute-start.8 = (bf16[2,128,256]{2,1,0:T(8,128)(2,1)S(1)}, bf16[2,128,256]{2,1,0:T(8,128)(2,1)S(1)}, u32[]{:S(2)}, u32[]{:S(2)}) collective-permute-start(bf16[2,128,256]{2,1,0:T(8,128)(2,1)S(1)} %convert_element_type.142), channel_id=1, source_target_pairs={{0,8},{8,0},{1,9},{9,1},{2,10},{10,2},{3,11},{11,3},{4,12},{12,4},... | collective-permute-start | bytes 393224 | tf_op jit(solution)/shard_map/ppermute | solution.py:47
  154.9 14.5 %collective-permute-start.9 = (bf16[2,128,256]{2,1,0:T(8,128)(2,1)S(1)}, bf16[2,128,256]{2,1,0:T(8,128)(2,1)S(1)}, u32[]{:S(2)}, u32[]{:S(2)}) collective-permute-start(bf16[2,128,256]{2,1,0:T(8,128)(2,1)S(1)} %convert_element_type.144), channel_id=1, source_target_pairs={{0,8},{8,0},{1,9},{9,1},{2,10},{10,2},{3,11},{11,3},{4,12},{12,4},... | collective-permute-start | bytes 393224 | tf_op jit(solution)/shard_map/ppermute | solution.py:47
  209.4 9.7 %collective-permute-start.10 = (bf16[1,4,256,256]{3,2,1,0:T(8,128)(2,1)S(1)}, bf16[1,4,256,256]{3,2,1,0:T(8,128)(2,1)S(1)}, u32[]{:S(2)}, u32[]{:S(2)}) collective-permute-start(bf16[1,4,256,256]{3,2,1,0:T(8,128)(2,1)S(1)} %bitcast.188), channel_id=1, source_target_pairs={{0,1},{1,0},{2,3},{3,2},{4,5},{5,4},{6,7},{7,6},{8,9},{9,8},{10,11... | collective-permute-start | bytes 1572872 | tf_op jit(solution)/shard_map/ppermute | solution.py:25

commit v5 on v4

--- a/solution.py
+++ b/solution.py
@@ -119,8 +119,7 @@
             jnp.sum(target * target, axis=1),
         ]
     )
-    stats = jnp.sum(spread(stats, "x"), axis=0)
-    stats = jnp.sum(spread(stats, ("z2", "z1", "z0")), axis=0)
+    stats = jnp.sum(spread(stats, DP), axis=0)
     inner, sq_student, sq_target = stats[0], stats[1], stats[2]
     inv_student = lax.rsqrt(sq_student + 1e-06)
     inv_target = lax.rsqrt(sq_target + 1e-06)

time: 222 us -> 218 us (0.982)
  blocking collectives: 39.4 us -> 36 us
    all_to_all x3 -> x2, blocking collectives: 39.4 us -> 36 us  [spread(): return lax.all_to_all(copies, axis, split_axis=0, concat_axis=0, tiled=True)]
where the time goes in v5:
time: 218 us; the launch traced here: 217 us
  starting transfers between devices  99.3 us (46%)
  waiting for transfers between devices  54.5 us (25%)
  blocking collectives  36 us (17%)
  other arithmetic  11.8 us (5%)
  matrix products  8.73 us (4%)
  local copies, waits for them, and re-layouts  5.55 us (3%)
    ppermute x8, starting transfers between devices, swap_in(): return in_order(value, lax.ppermute(value, axis, SWAP), axis)  56.2 us
    all_to_all x2, blocking collectives, spread(): return lax.all_to_all(copies, axis, split_axis=0, concat_axis=0, tiled=True)  36 us
    ppermute x2, waiting for transfers between devices, both_owners(): other = lax.ppermute(part.astype(BF16), 'zh', SWAP)  23 us
    ppermute x8, waiting for transfers between devices, swap_in(): return in_order(value, lax.ppermute(value, axis, SWAP), axis)  22 us
    ppermute x2, starting transfers between devices, both_owners(): other = lax.ppermute(part.astype(BF16), 'zh', SWAP)  15.5 us
    all_to_all x2, starting transfers between devices, spread(): return lax.all_to_all(copies, axis, split_axis=0, concat_axis=0, tiled=True)  9.32 us
    all_to_all x1, waiting for transfers between devices, shards(): lax.all_to_all(student_part, YC, split_axis=0, concat_axis=0, tiled=True)  6.6 us
    dot_general x8, matrix products, product(): jnp.dot(one, weights[place], preferred_element_type=F32).astype(BF16)  6 us
  transfers between devices with their start and end apart: 16, of which 10 were waited for; matrix products, arithmetic and copies ran while one was open for 6% of the time, Pallas kernels for 0%

profile of v5, /device:TPU:1, one launch (start us, length us, event | category | flops | bytes accessed | tf_op | source)
XLA Modules:
  0.0 217.0 jit_solution(3768582265677880694)
XLA Ops:
  3.6 5.0 %all-to-all-start = ((bf16[4,320,256]{2,1,0:T(8,128)(2,1)}), bf16[4,320,256]{2,1,0:T(8,128)(2,1)S(1)}, u32[]{:S(2)}, u32[]{:S(2)}) async-start(bf16[4,320,256]{2,1,0:T(8,128)(2,1)} %pad_maximum_fusion.3), calls=%async_computation | async-start | bytes 1310720 | tf_op jit(solution)/shard_map/all_to_all | solution.py:69
  8.5 8.8 %collective-permute-start = (bf16[64,512]{1,0:T(8,128)(2,1)S(1)}, bf16[64,512]{1,0:T(8,128)(2,1)S(1)}, u32[]{:S(2)}, u32[]{:S(2)}) collective-permute-start(bf16[64,512]{1,0:T(8,128)(2,1)S(1)} %copy-done.3), channel_id=1, source_target_pairs={{0,256},{256,0},{1,257},{257,1},{2,258},{258,2},{3,259},{259,3},{4... | collective-permute-start | bytes 196616 | tf_op jit(solution)/shard_map/ppermute | solution.py:25
  19.1 8.3 %collective-permute-start.2 = (bf16[256,256]{1,0:T(8,128)(2,1)S(1)}, bf16[256,256]{1,0:T(8,128)(2,1)S(1)}, u32[]{:S(2)}, u32[]{:S(2)}) collective-permute-start(bf16[256,256]{1,0:T(8,128)(2,1)S(1)} %bitcast.199), channel_id=1, source_target_pairs={{0,256},{256,0},{1,257},{257,1},{2,258},{258,2},{3,259},{259,3},{4... | collective-permute-start | bytes 393224 | tf_op jit(solution)/shard_map/ppermute | solution.py:25
  27.4 6.7 %collective-permute-start.1 = (bf16[128,512]{1,0:T(8,128)(2,1)S(1)}, bf16[128,512]{1,0:T(8,128)(2,1)S(1)}, u32[]{:S(2)}, u32[]{:S(2)}) collective-permute-start(bf16[128,512]{1,0:T(8,128)(2,1)S(1)} %bitcast.197), channel_id=1, source_target_pairs={{0,128},{128,0},{1,129},{129,1},{2,130},{130,2},{3,131},{131,3},{4... | collective-permute-start | bytes 393224 | tf_op jit(solution)/shard_map/ppermute | solution.py:25
  34.2 3.2 %collective-permute-done.1 = bf16[128,512]{1,0:T(8,128)(2,1)S(1)} collective-permute-done((bf16[128,512]{1,0:T(8,128)(2,1)S(1)}, bf16[128,512]{1,0:T(8,128)(2,1)S(1)}, u32[]{:S(2)}, u32[]{:S(2)}) %collective-permute-start.1) | collective-permute-done | bytes 131104 | tf_op jit(solution)/shard_map/ppermute | solution.py:25
  37.5 7.8 %collective-permute-start.3 = (bf16[256,512]{1,0:T(8,128)(2,1)S(1)}, bf16[256,512]{1,0:T(8,128)(2,1)S(1)}, u32[]{:S(2)}, u32[]{:S(2)}) collective-permute-start(bf16[256,512]{1,0:T(8,128)(2,1)S(1)} %bitcast.195), channel_id=1, source_target_pairs={{0,64},{64,0},{1,65},{65,1},{2,66},{66,2},{3,67},{67,3},{4,68},{68... | collective-permute-start | bytes 786440 | tf_op jit(solution)/shard_map/ppermute | solution.py:25
  45.9 5.7 %all-to-all-start.1 = ((s32[8,1,128]{2,1,0:T(1,128)}), s32[8,1,128]{2,1,0:T(1,128)S(1)}, u32[]{:S(2)}, u32[]{:S(2)}) async-start(s32[8,1,128]{2,1,0:T(1,128)} %broadcast_in_dim.10), calls=%async_computation.1 | async-start | bytes 8192 | tf_op jit(solution)/shard_map/all_to_all | solution.py:31
  51.6 2.5 %collective-permute-start.4 = (bf16[512,256]{1,0:T(8,128)(2,1)S(1)}, bf16[512,256]{1,0:T(8,128)(2,1)S(1)}, u32[]{:S(2)}, u32[]{:S(2)}) collective-permute-start(bf16[512,256]{1,0:T(8,128)(2,1)S(1)} %bitcast.193), channel_id=1, source_target_pairs={{0,128},{128,0},{1,129},{129,1},{2,130},{130,2},{3,131},{131,3},{4... | collective-permute-start | bytes 786440 | tf_op jit(solution)/shard_map/ppermute | solution.py:25
  57.6 3.6 %all-to-all-start.2 = ((bf16[4,512,512]{2,1,0:T(8,128)(2,1)}), bf16[4,512,512]{2,1,0:T(8,128)(2,1)S(1)}, u32[]{:S(2)}, u32[]{:S(2)}) async-start(bf16[4,512,512]{2,1,0:T(8,128)(2,1)} %broadcast_in_dim.11), calls=%async_computation.2 | async-start | bytes 4194304 | tf_op jit(solution)/shard_map/all_to_all | solution.py:31
  61.3 6.7 %collective-permute-done.4 = bf16[512,256]{1,0:T(8,128)(2,1)S(1)} collective-permute-done((bf16[512,256]{1,0:T(8,128)(2,1)S(1)}, bf16[512,256]{1,0:T(8,128)(2,1)S(1)}, u32[]{:S(2)}, u32[]{:S(2)}) %collective-permute-start.4) | collective-permute-done | bytes 262176 | tf_op jit(solution)/shard_map/ppermute | solution.py:25
  70.0 12.6 %collective-permute-start.6 = (s32[8,128]{1,0:T(8,128)S(1)}, s32[8,128]{1,0:T(8,128)S(1)}, u32[]{:S(2)}, u32[]{:S(2)}) collective-permute-start(s32[8,128]{1,0:T(8,128)S(1)} %bitcast.203), channel_id=1, source_target_pairs={{0,8},{8,0},{1,9},{9,1},{2,10},{10,2},{3,11},{11,3},{4,12},{12,4},... | collective-permute-start | bytes 12296 | tf_op jit(solution)/shard_map/ppermute | solution.py:25
  82.6 9.5 %collective-permute-done.6 = s32[8,128]{1,0:T(8,128)S(1)} collective-permute-done((s32[8,128]{1,0:T(8,128)S(1)}, s32[8,128]{1,0:T(8,128)S(1)}, u32[]{:S(2)}, u32[]{:S(2)}) %collective-permute-start.6) | collective-permute-done | bytes 4128 | tf_op jit(solution)/shard_map/ppermute | solution.py:25
  98.1 3.6 %collective-permute-start.7 = (bf16[4,1024,256]{2,1,0:T(8,128)(2,1)}, bf16[4,1024,256]{2,1,0:T(8,128)(2,1)}, u32[]{:S(2)}, u32[]{:S(2)}) collective-permute-start(bf16[4,1024,256]{2,1,0:T(8,128)(2,1)} %pad_maximum_fusion), channel_id=1, source_target_pairs={{0,1},{1,0},{2,3},{3,2},{4,5},{5,4},{6,7},{7,6},{8,9},{9,8},{10,11... | collective-permute-start | bytes 6291464 | tf_op jit(solution)/shard_map/ppermute | solution.py:102
  101.7 4.2 %all-to-all-start.3 = ((bf16[8,2,128,256]{3,2,1,0:T(8,128)(2,1)}), bf16[8,2,128,256]{3,2,1,0:T(8,128)(2,1)}, u32[]{:S(2)}, u32[]{:S(2)}) async-start(bf16[8,2,128,256]{3,2,1,0:T(8,128)(2,1)} %bitcast.181), calls=%async_computation.3 | async-start | bytes 2097152 | tf_op jit(solution)/shard_map/all_to_all | solution.py:85
  110.8 2.1 fusion.8
  114.5 6.6 %all-to-all-done.3 = bf16[8,2,128,256]{3,2,1,0:T(8,128)(2,1)} async-done(((bf16[8,2,128,256]{3,2,1,0:T(8,128)(2,1)}), bf16[8,2,128,256]{3,2,1,0:T(8,128)(2,1)}, u32[]{:S(2)}, u32[]{:S(2)}) %all-to-all-start.3) | async-done | bytes 1048608 | tf_op jit(solution)/shard_map/all_to_all | solution.py:85
  121.1 5.4 %all-to-all-start.4 = ((bf16[16,2,128,256]{3,2,1,0:T(8,128)(2,1)}), bf16[16,2,128,256]{3,2,1,0:T(8,128)(2,1)}, u32[]{:S(2)}, u32[]{:S(2)}) async-start(bf16[16,2,128,256]{3,2,1,0:T(8,128)(2,1)} %bitcast.179), calls=%async_computation.4 | async-start | bytes 4194304 | tf_op jit(solution)/shard_map/all_to_all | solution.py:35
  127.9 6.9 %collective-permute-start.8 = (bf16[2,128,256]{2,1,0:T(8,128)(2,1)S(1)}, bf16[2,128,256]{2,1,0:T(8,128)(2,1)S(1)}, u32[]{:S(2)}, u32[]{:S(2)}) collective-permute-start(bf16[2,128,256]{2,1,0:T(8,128)(2,1)S(1)} %convert_element_type.142), channel_id=1, source_target_pairs={{0,8},{8,0},{1,9},{9,1},{2,10},{10,2},{3,11},{11,3},{4,12},{12,4},... | collective-permute-start | bytes 393224 | tf_op jit(solution)/shard_map/ppermute | solution.py:47
  134.8 17.1 %collective-permute-done.8 = bf16[2,128,256]{2,1,0:T(8,128)(2,1)S(1)} collective-permute-done((bf16[2,128,256]{2,1,0:T(8,128)(2,1)S(1)}, bf16[2,128,256]{2,1,0:T(8,128)(2,1)S(1)}, u32[]{:S(2)}, u32[]{:S(2)}) %collective-permute-start.8) | collective-permute-done | bytes 131104 | tf_op jit(solution)/shard_map/ppermute | solution.py:47
  155.0 8.7 %collective-permute-start.9 = (bf16[2,128,256]{2,1,0:T(8,128)(2,1)S(1)}, bf16[2,128,256]{2,1,0:T(8,128)(2,1)S(1)}, u32[]{:S(2)}, u32[]{:S(2)}) collective-permute-start(bf16[2,128,256]{2,1,0:T(8,128)(2,1)S(1)} %convert_element_type.144), channel_id=1, source_target_pairs={{0,8},{8,0},{1,9},{9,1},{2,10},{10,2},{3,11},{11,3},{4,12},{12,4},... | collective-permute-start | bytes 393224 | tf_op jit(solution)/shard_map/ppermute | solution.py:47
  163.7 5.8 %collective-permute-done.9 = bf16[2,128,256]{2,1,0:T(8,128)(2,1)S(1)} collective-permute-done((bf16[2,128,256]{2,1,0:T(8,128)(2,1)S(1)}, bf16[2,128,256]{2,1,0:T(8,128)(2,1)S(1)}, u32[]{:S(2)}, u32[]{:S(2)}) %collective-permute-start.9) | collective-permute-done | bytes 131104 | tf_op jit(solution)/shard_map/ppermute | solution.py:47
  169.8 24.5 %all_to_all.39 = f32[32,3,256]{2,1,0:T(4,128)S(1)} all-to-all(f32[32,3,256]{2,1,0:T(4,128)S(1)} %broadcast_in_dim.12), channel_id=1, replica_groups=mesh['z2'=2,'z1'=2,'z0'=2,'x'=4,'zh'=2,'y1'=2,'y0'=2,'c'=2] {'z2','z1','..., dimensions={0} | all-to-all | bytes 196608 | tf_op jit(solution)/shard_map/all_to_all | solution.py:31
  194.6 11.5 %all_to_all.40 = bf16[4,256,256]{2,1,0:T(8,128)(2,1)S(1)} all-to-all(bf16[4,256,256]{2,1,0:T(8,128)(2,1)S(1)} %broadcast_in_dim.13), channel_id=1, replica_groups=mesh['z2'=2,'z1'=2,'z0'=2,'x'=4,'zh'=2,'y1'=2,'y0'=2,'c'=2] {'y1','y0'}, dimensions={0} | all-to-all | bytes 1048576 | tf_op jit(solution)/shard_map/all_to_all | solution.py:31
  206.1 7.6 %collective-permute-start.10 = (bf16[1,4,256,256]{3,2,1,0:T(8,128)(2,1)S(1)}, bf16[1,4,256,256]{3,2,1,0:T(8,128)(2,1)S(1)}, u32[]{:S(2)}, u32[]{:S(2)}) collective-permute-start(bf16[1,4,256,256]{3,2,1,0:T(8,128)(2,1)S(1)} %bitcast.188), channel_id=1, source_target_pairs={{0,1},{1,0},{2,3},{3,2},{4,5},{5,4},{6,7},{7,6},{8,9},{9,8},{10,11... | collective-permute-start | bytes 1572872 | tf_op jit(solution)/shard_map/ppermute | solution.py:25
  (74 shorter events, 31.4 us)
Async XLA Ops:
  0.6 91.7 %copy-start = (bf16[512,256]{1,0:T(8,128)(2,1)S(1)}, bf16[512,256]{1,0:T(8,128)(2,1)}, u32[]{:S(2)}) copy-start(bf16[512,256]{1,0:T(8,128)(2,1)} %param.8) | copy-start | bytes 786436
  0.6 7.9 %copy-start.3 = (bf16[64,512]{1,0:T(8,128)(2,1)S(1)}, bf16[64,512]{1,0:T(8,128)(2,1)}, u32[]{:S(2)}) copy-start(bf16[64,512]{1,0:T(8,128)(2,1)} %param.7) | copy-start | bytes 196612
  3.6 41.7 %copy-start.4 = (s32[128]{0:T(128)S(1)}, s32[128]{0:T(128)}, u32[]{:S(2)}) copy-start(s32[128]{0:T(128)} %param.9) | copy-start | bytes 1540
  3.6 15.5 %all-to-all-start = ((bf16[4,320,256]{2,1,0:T(8,128)(2,1)}), bf16[4,320,256]{2,1,0:T(8,128)(2,1)S(1)}, u32[]{:S(2)}, u32[]{:S(2)}) async-start(bf16[4,320,256]{2,1,0:T(8,128)(2,1)} %pad_maximum_fusion.3), calls=%async_computation | async-start | bytes 1310720 | tf_op jit(solution)/shard_map/all_to_all | solution.py:69
  8.5 10.5 %collective-permute-start = (bf16[64,512]{1,0:T(8,128)(2,1)S(1)}, bf16[64,512]{1,0:T(8,128)(2,1)S(1)}, u32[]{:S(2)}, u32[]{:S(2)}) collective-permute-start(bf16[64,512]{1,0:T(8,128)(2,1)S(1)} %copy-done.3), channel_id=1, source_target_pairs={{0,256},{256,0},{1,257},{257,1},{2,258},{258,2},{3,259},{259,3},{4... | collective-permute-start | bytes 196616 | tf_op jit(solution)/shard_map/ppermute | solution.py:25
  19.1 35.2 %copy-start.1 = (bf16[4,320,256]{2,1,0:T(8,128)(2,1)}, bf16[4,320,256]{2,1,0:T(8,128)(2,1)S(1)}, u32[]{:S(2)}) copy-start(bf16[4,320,256]{2,1,0:T(8,128)(2,1)S(1)} %all-to-all-done) | copy-start | bytes 1966084
  19.1 15.0 %collective-permute-start.2 = (bf16[256,256]{1,0:T(8,128)(2,1)S(1)}, bf16[256,256]{1,0:T(8,128)(2,1)S(1)}, u32[]{:S(2)}, u32[]{:S(2)}) collective-permute-start(bf16[256,256]{1,0:T(8,128)(2,1)S(1)} %bitcast.199), channel_id=1, source_target_pairs={{0,256},{256,0},{1,257},{257,1},{2,258},{258,2},{3,259},{259,3},{4... | collective-permute-start | bytes 393224 | tf_op jit(solution)/shard_map/ppermute | solution.py:25
  27.4 10.0 %collective-permute-start.1 = (bf16[128,512]{1,0:T(8,128)(2,1)S(1)}, bf16[128,512]{1,0:T(8,128)(2,1)S(1)}, u32[]{:S(2)}, u32[]{:S(2)}) collective-permute-start(bf16[128,512]{1,0:T(8,128)(2,1)S(1)} %bitcast.197), channel_id=1, source_target_pairs={{0,128},{128,0},{1,129},{129,1},{2,130},{130,2},{3,131},{131,3},{4... | collective-permute-start | bytes 393224 | tf_op jit(solution)/shard_map/ppermute | solution.py:25
  37.5 16.7 %collective-permute-start.3 = (bf16[256,512]{1,0:T(8,128)(2,1)S(1)}, bf16[256,512]{1,0:T(8,128)(2,1)S(1)}, u32[]{:S(2)}, u32[]{:S(2)}) collective-permute-start(bf16[256,512]{1,0:T(8,128)(2,1)S(1)} %bitcast.195), channel_id=1, source_target_pairs={{0,64},{64,0},{1,65},{65,1},{2,66},{66,2},{3,67},{67,3},{4,68},{68... | collective-permute-start | bytes 786440 | tf_op jit(solution)/shard_map/ppermute | solution.py:25
  45.9 10.2 %all-to-all-start.1 = ((s32[8,1,128]{2,1,0:T(1,128)}), s32[8,1,128]{2,1,0:T(1,128)S(1)}, u32[]{:S(2)}, u32[]{:S(2)}) async-start(s32[8,1,128]{2,1,0:T(1,128)} %broadcast_in_dim.10), calls=%async_computation.1 | async-start | bytes 8192 | tf_op jit(solution)/shard_map/all_to_all | solution.py:31
  51.6 16.3 %collective-permute-start.4 = (bf16[512,256]{1,0:T(8,128)(2,1)S(1)}, bf16[512,256]{1,0:T(8,128)(2,1)S(1)}, u32[]{:S(2)}, u32[]{:S(2)}) collective-permute-start(bf16[512,256]{1,0:T(8,128)(2,1)S(1)} %bitcast.193), channel_id=1, source_target_pairs={{0,128},{128,0},{1,129},{129,1},{2,130},{130,2},{3,131},{131,3},{4... | collective-permute-start | bytes 786440 | tf_op jit(solution)/shard_map/ppermute | solution.py:25
  57.6 34.7 %all-to-all-start.2 = ((bf16[4,512,512]{2,1,0:T(8,128)(2,1)}), bf16[4,512,512]{2,1,0:T(8,128)(2,1)S(1)}, u32[]{:S(2)}, u32[]{:S(2)}) async-start(bf16[4,512,512]{2,1,0:T(8,128)(2,1)} %broadcast_in_dim.11), calls=%async_computation.2 | async-start | bytes 4194304 | tf_op jit(solution)/shard_map/all_to_all | solution.py:31
  68.0 24.1 %collective-permute-start.5 = (bf16[1024,256]{1,0:T(8,128)(2,1)S(1)}, bf16[1024,256]{1,0:T(8,128)(2,1)S(1)}, u32[]{:S(2)}, u32[]{:S(2)}) collective-permute-start(bf16[1024,256]{1,0:T(8,128)(2,1)S(1)} %bitcast.187), channel_id=1, source_target_pairs={{0,64},{64,0},{1,65},{65,1},{2,66},{66,2},{3,67},{67,3},{4,68},{68... | collective-permute-start | bytes 1572872 | tf_op jit(solution)/shard_map/ppermute | solution.py:25
  70.0 22.1 %collective-permute-start.6 = (s32[8,128]{1,0:T(8,128)S(1)}, s32[8,128]{1,0:T(8,128)S(1)}, u32[]{:S(2)}, u32[]{:S(2)}) collective-permute-start(s32[8,128]{1,0:T(8,128)S(1)} %bitcast.203), channel_id=1, source_target_pairs={{0,8},{8,0},{1,9},{9,1},{2,10},{10,2},{3,11},{11,3},{4,12},{12,4},... | collective-permute-start | bytes 12296 | tf_op jit(solution)/shard_map/ppermute | solution.py:25
  94.2 1.1 copy-start.2
  98.1 12.7 %collective-permute-start.7 = (bf16[4,1024,256]{2,1,0:T(8,128)(2,1)}, bf16[4,1024,256]{2,1,0:T(8,128)(2,1)}, u32[]{:S(2)}, u32[]{:S(2)}) collective-permute-start(bf16[4,1024,256]{2,1,0:T(8,128)(2,1)} %pad_maximum_fusion), channel_id=1, source_target_pairs={{0,1},{1,0},{2,3},{3,2},{4,5},{5,4},{6,7},{7,6},{8,9},{9,8},{10,11... | collective-permute-start | bytes 6291464 | tf_op jit(solution)/shard_map/ppermute | solution.py:102
  101.7 19.4 %all-to-all-start.3 = ((bf16[8,2,128,256]{3,2,1,0:T(8,128)(2,1)}), bf16[8,2,128,256]{3,2,1,0:T(8,128)(2,1)}, u32[]{:S(2)}, u32[]{:S(2)}) async-start(bf16[8,2,128,256]{3,2,1,0:T(8,128)(2,1)} %bitcast.181), calls=%async_computation.3 | async-start | bytes 2097152 | tf_op jit(solution)/shard_map/all_to_all | solution.py:85
  121.1 32.0 %all-to-all-start.4 = ((bf16[16,2,128,256]{3,2,1,0:T(8,128)(2,1)}), bf16[16,2,128,256]{3,2,1,0:T(8,128)(2,1)}, u32[]{:S(2)}, u32[]{:S(2)}) async-start(bf16[16,2,128,256]{3,2,1,0:T(8,128)(2,1)} %bitcast.179), calls=%async_computation.4 | async-start | bytes 4194304 | tf_op jit(solution)/shard_map/all_to_all | solution.py:35
  127.9 24.0 %collective-permute-start.8 = (bf16[2,128,256]{2,1,0:T(8,128)(2,1)S(1)}, bf16[2,128,256]{2,1,0:T(8,128)(2,1)S(1)}, u32[]{:S(2)}, u32[]{:S(2)}) collective-permute-start(bf16[2,128,256]{2,1,0:T(8,128)(2,1)S(1)} %convert_element_type.142), channel_id=1, source_target_pairs={{0,8},{8,0},{1,9},{9,1},{2,10},{10,2},{3,11},{11,3},{4,12},{12,4},... | collective-permute-start | bytes 393224 | tf_op jit(solution)/shard_map/ppermute | solution.py:47
  155.0 14.5 %collective-permute-start.9 = (bf16[2,128,256]{2,1,0:T(8,128)(2,1)S(1)}, bf16[2,128,256]{2,1,0:T(8,128)(2,1)S(1)}, u32[]{:S(2)}, u32[]{:S(2)}) collective-permute-start(bf16[2,128,256]{2,1,0:T(8,128)(2,1)S(1)} %convert_element_type.144), channel_id=1, source_target_pairs={{0,8},{8,0},{1,9},{9,1},{2,10},{10,2},{3,11},{11,3},{4,12},{12,4},... | collective-permute-start | bytes 393224 | tf_op jit(solution)/shard_map/ppermute | solution.py:47
  206.1 9.1 %collective-permute-start.10 = (bf16[1,4,256,256]{3,2,1,0:T(8,128)(2,1)S(1)}, bf16[1,4,256,256]{3,2,1,0:T(8,128)(2,1)S(1)}, u32[]{:S(2)}, u32[]{:S(2)}) collective-permute-start(bf16[1,4,256,256]{3,2,1,0:T(8,128)(2,1)S(1)} %bitcast.188), channel_id=1, source_target_pairs={{0,1},{1,0},{2,3},{3,2},{4,5},{5,4},{6,7},{7,6},{8,9},{9,8},{10,11... | collective-permute-start | bytes 1572872 | tf_op jit(solution)/shard_map/ppermute | solution.py:25

commit v6 on v5

--- a/solution.py
+++ b/solution.py
@@ -131,10 +131,9 @@
     )
     grad_out = grad_out.astype(BF16)
     cosine = lax.dynamic_slice_in_dim(cosine, lax.axis_index("zh") * block, block)
-    grad_out = spread(grad_out, ("y1", "y0"))
-    grad_out = swap_in(grad_out[None], "c")
+    grad_out = spread(grad_out, YC)
     grad_out = grad_out.reshape(2, 2, 2, 2, 2, rows, out_width)
-    grad_out = grad_out.transpose(0, 4, 2, 1, 3, 5, 6).reshape(total_rows, out_width)
+    grad_out = grad_out.transpose(2, 4, 1, 0, 3, 5, 6).reshape(total_rows, out_width)
     projection_grad = lax.dot_general(
         student_all, grad_out, (((0,), (0,)), ((), ())), preferred_element_type=F32
     )

time: 218 us -> 223 us (1.023)
  waiting for transfers between devices: 54.5 us -> 68.1 us
  blocking collectives: 36 us -> 24.5 us
    all_to_all x2 -> x3, waiting for transfers between devices: 1.87 us -> 16.4 us  [spread(): return lax.all_to_all(copies, axis, split_axis=0, concat_axis=0, tiled=True)]
    all_to_all x2 -> x1, blocking collectives: 36 us -> 24.5 us  [spread(): return lax.all_to_all(copies, axis, split_axis=0, concat_axis=0, tiled=True)]
    all_to_all x2 -> x3, starting transfers between devices: 9.32 us -> 18.6 us  [spread(): return lax.all_to_all(copies, axis, split_axis=0, concat_axis=0, tiled=True)]
    ppermute x8 -> x7, starting transfers between devices: 56.2 us -> 48.7 us  [swap_in(): return in_order(value, lax.ppermute(value, axis, SWAP), axis)]
    ppermute x8 -> x7, waiting for transfers between devices: 22 us -> 21.1 us  [swap_in(): return in_order(value, lax.ppermute(value, axis, SWAP), axis)]
where the time goes in v6:
time: 223 us; the launch traced here: 222 us
  starting transfers between devices  101 us (45%)
  waiting for transfers between devices  68.1 us (31%)
  blocking collectives  24.5 us (11%)
  other arithmetic  11.6 us (5%)
  matrix products  8.73 us (4%)
  local copies, waits for them, and re-layouts  6.57 us (3%)
    ppermute x7, starting transfers between devices, swap_in(): return in_order(value, lax.ppermute(value, axis, SWAP), axis)  48.7 us
    all_to_all x1, blocking collectives, spread(): return lax.all_to_all(copies, axis, split_axis=0, concat_axis=0, tiled=True)  24.5 us
    ppermute x2, waiting for transfers between devices, both_owners(): other = lax.ppermute(part.astype(BF16), 'zh', SWAP)  23 us
    ppermute x7, waiting for transfers between devices, swap_in(): return in_order(value, lax.ppermute(value, axis, SWAP), axis)  21.1 us
    all_to_all x3, starting transfers between devices, spread(): return lax.all_to_all(copies, axis, split_axis=0, concat_axis=0, tiled=True)  18.6 us
    all_to_all x3, waiting for transfers between devices, spread(): return lax.all_to_all(copies, axis, split_axis=0, concat_axis=0, tiled=True)  16.4 us
    ppermute x2, starting transfers between devices, both_owners(): other = lax.ppermute(part.astype(BF16), 'zh', SWAP)  15.5 us
    all_to_all x1, waiting for transfers between devices, shards(): lax.all_to_all(student_part, YC, split_axis=0, concat_axis=0, tiled=True)  6.6 us
  transfers between devices with their start and end apart: 16, of which 10 were waited for; matrix products, arithmetic and copies ran while one was open for 6% of the time, Pallas kernels for 0%

profile of v6, /device:TPU:1, one launch (start us, length us, event | category | flops | bytes accessed | tf_op | source)
XLA Modules:
  0.0 221.6 jit_solution(5335878912956027461)
XLA Ops:
  3.6 5.0 %all-to-all-start = ((bf16[4,320,256]{2,1,0:T(8,128)(2,1)}), bf16[4,320,256]{2,1,0:T(8,128)(2,1)S(1)}, u32[]{:S(2)}, u32[]{:S(2)}) async-start(bf16[4,320,256]{2,1,0:T(8,128)(2,1)} %pad_maximum_fusion.3), calls=%async_computation | async-start | bytes 1310720 | tf_op jit(solution)/shard_map/all_to_all | solution.py:69
  8.5 8.8 %collective-permute-start = (bf16[64,512]{1,0:T(8,128)(2,1)S(1)}, bf16[64,512]{1,0:T(8,128)(2,1)S(1)}, u32[]{:S(2)}, u32[]{:S(2)}) collective-permute-start(bf16[64,512]{1,0:T(8,128)(2,1)S(1)} %copy-done.3), channel_id=1, source_target_pairs={{0,256},{256,0},{1,257},{257,1},{2,258},{258,2},{3,259},{259,3},{4... | collective-permute-start | bytes 196616 | tf_op jit(solution)/shard_map/ppermute | solution.py:25
  19.1 8.3 %collective-permute-start.2 = (bf16[256,256]{1,0:T(8,128)(2,1)S(1)}, bf16[256,256]{1,0:T(8,128)(2,1)S(1)}, u32[]{:S(2)}, u32[]{:S(2)}) collective-permute-start(bf16[256,256]{1,0:T(8,128)(2,1)S(1)} %bitcast.193), channel_id=1, source_target_pairs={{0,256},{256,0},{1,257},{257,1},{2,258},{258,2},{3,259},{259,3},{4... | collective-permute-start | bytes 393224 | tf_op jit(solution)/shard_map/ppermute | solution.py:25
  27.4 6.7 %collective-permute-start.1 = (bf16[128,512]{1,0:T(8,128)(2,1)S(1)}, bf16[128,512]{1,0:T(8,128)(2,1)S(1)}, u32[]{:S(2)}, u32[]{:S(2)}) collective-permute-start(bf16[128,512]{1,0:T(8,128)(2,1)S(1)} %bitcast.191), channel_id=1, source_target_pairs={{0,128},{128,0},{1,129},{129,1},{2,130},{130,2},{3,131},{131,3},{4... | collective-permute-start | bytes 393224 | tf_op jit(solution)/shard_map/ppermute | solution.py:25
  34.2 3.2 %collective-permute-done.1 = bf16[128,512]{1,0:T(8,128)(2,1)S(1)} collective-permute-done((bf16[128,512]{1,0:T(8,128)(2,1)S(1)}, bf16[128,512]{1,0:T(8,128)(2,1)S(1)}, u32[]{:S(2)}, u32[]{:S(2)}) %collective-permute-start.1) | collective-permute-done | bytes 131104 | tf_op jit(solution)/shard_map/ppermute | solution.py:25
  37.5 7.8 %collective-permute-start.3 = (bf16[256,512]{1,0:T(8,128)(2,1)S(1)}, bf16[256,512]{1,0:T(8,128)(2,1)S(1)}, u32[]{:S(2)}, u32[]{:S(2)}) collective-permute-start(bf16[256,512]{1,0:T(8,128)(2,1)S(1)} %bitcast.189), channel_id=1, source_target_pairs={{0,64},{64,0},{1,65},{65,1},{2,66},{66,2},{3,67},{67,3},{4,68},{68... | collective-permute-start | bytes 786440 | tf_op jit(solution)/shard_map/ppermute | solution.py:25
  45.9 5.7 %all-to-all-start.1 = ((s32[8,1,128]{2,1,0:T(1,128)}), s32[8,1,128]{2,1,0:T(1,128)S(1)}, u32[]{:S(2)}, u32[]{:S(2)}) async-start(s32[8,1,128]{2,1,0:T(1,128)} %broadcast_in_dim.8), calls=%async_computation.1 | async-start | bytes 8192 | tf_op jit(solution)/shard_map/all_to_all | solution.py:31
  51.6 2.5 %collective-permute-start.4 = (bf16[512,256]{1,0:T(8,128)(2,1)S(1)}, bf16[512,256]{1,0:T(8,128)(2,1)S(1)}, u32[]{:S(2)}, u32[]{:S(2)}) collective-permute-start(bf16[512,256]{1,0:T(8,128)(2,1)S(1)} %bitcast.187), channel_id=1, source_target_pairs={{0,128},{128,0},{1,129},{129,1},{2,130},{130,2},{3,131},{131,3},{4... | collective-permute-start | bytes 786440 | tf_op jit(solution)/shard_map/ppermute | solution.py:25
  57.6 3.6 %all-to-all-start.2 = ((bf16[4,512,512]{2,1,0:T(8,128)(2,1)}), bf16[4,512,512]{2,1,0:T(8,128)(2,1)S(1)}, u32[]{:S(2)}, u32[]{:S(2)}) async-start(bf16[4,512,512]{2,1,0:T(8,128)(2,1)} %broadcast_in_dim.9), calls=%async_computation.2 | async-start | bytes 4194304 | tf_op jit(solution)/shard_map/all_to_all | solution.py:31
  61.3 6.7 %collective-permute-done.4 = bf16[512,256]{1,0:T(8,128)(2,1)S(1)} collective-permute-done((bf16[512,256]{1,0:T(8,128)(2,1)S(1)}, bf16[512,256]{1,0:T(8,128)(2,1)S(1)}, u32[]{:S(2)}, u32[]{:S(2)}) %collective-permute-start.4) | collective-permute-done | bytes 262176 | tf_op jit(solution)/shard_map/ppermute | solution.py:25
  70.0 12.6 %collective-permute-start.6 = (s32[8,128]{1,0:T(8,128)S(1)}, s32[8,128]{1,0:T(8,128)S(1)}, u32[]{:S(2)}, u32[]{:S(2)}) collective-permute-start(s32[8,128]{1,0:T(8,128)S(1)} %bitcast.197), channel_id=1, source_target_pairs={{0,8},{8,0},{1,9},{9,1},{2,10},{10,2},{3,11},{11,3},{4,12},{12,4},... | collective-permute-start | bytes 12296 | tf_op jit(solution)/shard_map/ppermute | solution.py:25
  82.6 9.5 %collective-permute-done.6 = s32[8,128]{1,0:T(8,128)S(1)} collective-permute-done((s32[8,128]{1,0:T(8,128)S(1)}, s32[8,128]{1,0:T(8,128)S(1)}, u32[]{:S(2)}, u32[]{:S(2)}) %collective-permute-start.6) | collective-permute-done | bytes 4128 | tf_op jit(solution)/shard_map/ppermute | solution.py:25
  98.1 3.6 %collective-permute-start.7 = (bf16[4,1024,256]{2,1,0:T(8,128)(2,1)}, bf16[4,1024,256]{2,1,0:T(8,128)(2,1)}, u32[]{:S(2)}, u32[]{:S(2)}) collective-permute-start(bf16[4,1024,256]{2,1,0:T(8,128)(2,1)} %pad_maximum_fusion), channel_id=1, source_target_pairs={{0,1},{1,0},{2,3},{3,2},{4,5},{5,4},{6,7},{7,6},{8,9},{9,8},{10,11... | collective-permute-start | bytes 6291464 | tf_op jit(solution)/shard_map/ppermute | solution.py:102
  101.7 4.2 %all-to-all-start.3 = ((bf16[8,2,128,256]{3,2,1,0:T(8,128)(2,1)}), bf16[8,2,128,256]{3,2,1,0:T(8,128)(2,1)}, u32[]{:S(2)}, u32[]{:S(2)}) async-start(bf16[8,2,128,256]{3,2,1,0:T(8,128)(2,1)} %bitcast.177), calls=%async_computation.3 | async-start | bytes 2097152 | tf_op jit(solution)/shard_map/all_to_all | solution.py:85
  110.8 2.1 fusion.8
  114.5 6.6 %all-to-all-done.3 = bf16[8,2,128,256]{3,2,1,0:T(8,128)(2,1)} async-done(((bf16[8,2,128,256]{3,2,1,0:T(8,128)(2,1)}), bf16[8,2,128,256]{3,2,1,0:T(8,128)(2,1)}, u32[]{:S(2)}, u32[]{:S(2)}) %all-to-all-start.3) | async-done | bytes 1048608 | tf_op jit(solution)/shard_map/all_to_all | solution.py:85
  121.1 5.4 %all-to-all-start.4 = ((bf16[16,2,128,256]{3,2,1,0:T(8,128)(2,1)}), bf16[16,2,128,256]{3,2,1,0:T(8,128)(2,1)}, u32[]{:S(2)}, u32[]{:S(2)}) async-start(bf16[16,2,128,256]{3,2,1,0:T(8,128)(2,1)} %bitcast.175), calls=%async_computation.4 | async-start | bytes 4194304 | tf_op jit(solution)/shard_map/all_to_all | solution.py:35
  127.9 6.9 %collective-permute-start.8 = (bf16[2,128,256]{2,1,0:T(8,128)(2,1)S(1)}, bf16[2,128,256]{2,1,0:T(8,128)(2,1)S(1)}, u32[]{:S(2)}, u32[]{:S(2)}) collective-permute-start(bf16[2,128,256]{2,1,0:T(8,128)(2,1)S(1)} %convert_element_type.142), channel_id=1, source_target_pairs={{0,8},{8,0},{1,9},{9,1},{2,10},{10,2},{3,11},{11,3},{4,12},{12,4},... | collective-permute-start | bytes 393224 | tf_op jit(solution)/shard_map/ppermute | solution.py:47
  134.8 17.1 %collective-permute-done.8 = bf16[2,128,256]{2,1,0:T(8,128)(2,1)S(1)} collective-permute-done((bf16[2,128,256]{2,1,0:T(8,128)(2,1)S(1)}, bf16[2,128,256]{2,1,0:T(8,128)(2,1)S(1)}, u32[]{:S(2)}, u32[]{:S(2)}) %collective-permute-start.8) | collective-permute-done | bytes 131104 | tf_op jit(solution)/shard_map/ppermute | solution.py:47
  155.0 8.7 %collective-permute-start.9 = (bf16[2,128,256]{2,1,0:T(8,128)(2,1)S(1)}, bf16[2,128,256]{2,1,0:T(8,128)(2,1)S(1)}, u32[]{:S(2)}, u32[]{:S(2)}) collective-permute-start(bf16[2,128,256]{2,1,0:T(8,128)(2,1)S(1)} %convert_element_type.144), channel_id=1, source_target_pairs={{0,8},{8,0},{1,9},{9,1},{2,10},{10,2},{3,11},{11,3},{4,12},{12,4},... | collective-permute-start | bytes 393224 | tf_op jit(solution)/shard_map/ppermute | solution.py:47
  163.7 5.8 %collective-permute-done.9 = bf16[2,128,256]{2,1,0:T(8,128)(2,1)S(1)} collective-permute-done((bf16[2,128,256]{2,1,0:T(8,128)(2,1)S(1)}, bf16[2,128,256]{2,1,0:T(8,128)(2,1)S(1)}, u32[]{:S(2)}, u32[]{:S(2)}) %collective-permute-start.9) | collective-permute-done | bytes 131104 | tf_op jit(solution)/shard_map/ppermute | solution.py:47
  169.8 24.5 %all_to_all.39 = f32[32,3,256]{2,1,0:T(4,128)S(1)} all-to-all(f32[32,3,256]{2,1,0:T(4,128)S(1)} %broadcast_in_dim.10), channel_id=1, replica_groups=mesh['z2'=2,'z1'=2,'z0'=2,'x'=4,'zh'=2,'y1'=2,'y0'=2,'c'=2] {'z2','z1','..., dimensions={0} | all-to-all | bytes 196608 | tf_op jit(solution)/shard_map/all_to_all | solution.py:31
  195.6 9.3 %all-to-all-start.6 = ((bf16[8,256,256]{2,1,0:T(8,128)(2,1)}), bf16[8,256,256]{2,1,0:T(8,128)(2,1)S(1)}, u32[]{:S(2)}, u32[]{:S(2)}) async-start(bf16[8,256,256]{2,1,0:T(8,128)(2,1)} %broadcast_in_dim.11), calls=%async_computation.6 | async-start | bytes 2097152 | tf_op jit(solution)/shard_map/all_to_all | solution.py:31
  205.5 14.5 %all-to-all-done.6 = bf16[8,256,256]{2,1,0:T(8,128)(2,1)S(1)} async-done(((bf16[8,256,256]{2,1,0:T(8,128)(2,1)}), bf16[8,256,256]{2,1,0:T(8,128)(2,1)S(1)}, u32[]{:S(2)}, u32[]{:S(2)}) %all-to-all-start.6) | async-done | bytes 1048608 | tf_op jit(solution)/shard_map/all_to_all | solution.py:31
  (71 shorter events, 31.3 us)
Async XLA Ops:
  0.6 91.7 %copy-start = (bf16[512,256]{1,0:T(8,128)(2,1)S(1)}, bf16[512,256]{1,0:T(8,128)(2,1)}, u32[]{:S(2)}) copy-start(bf16[512,256]{1,0:T(8,128)(2,1)} %param.8) | copy-start | bytes 786436
  0.6 7.9 %copy-start.3 = (bf16[64,512]{1,0:T(8,128)(2,1)S(1)}, bf16[64,512]{1,0:T(8,128)(2,1)}, u32[]{:S(2)}) copy-start(bf16[64,512]{1,0:T(8,128)(2,1)} %param.7) | copy-start | bytes 196612
  3.6 41.7 %copy-start.4 = (s32[128]{0:T(128)S(1)}, s32[128]{0:T(128)}, u32[]{:S(2)}) copy-start(s32[128]{0:T(128)} %param.9) | copy-start | bytes 1540
  3.6 15.5 %all-to-all-start = ((bf16[4,320,256]{2,1,0:T(8,128)(2,1)}), bf16[4,320,256]{2,1,0:T(8,128)(2,1)S(1)}, u32[]{:S(2)}, u32[]{:S(2)}) async-start(bf16[4,320,256]{2,1,0:T(8,128)(2,1)} %pad_maximum_fusion.3), calls=%async_computation | async-start | bytes 1310720 | tf_op jit(solution)/shard_map/all_to_all | solution.py:69
  8.5 10.5 %collective-permute-start = (bf16[64,512]{1,0:T(8,128)(2,1)S(1)}, bf16[64,512]{1,0:T(8,128)(2,1)S(1)}, u32[]{:S(2)}, u32[]{:S(2)}) collective-permute-start(bf16[64,512]{1,0:T(8,128)(2,1)S(1)} %copy-done.3), channel_id=1, source_target_pairs={{0,256},{256,0},{1,257},{257,1},{2,258},{258,2},{3,259},{259,3},{4... | collective-permute-start | bytes 196616 | tf_op jit(solution)/shard_map/ppermute | solution.py:25
  19.1 35.2 %copy-start.1 = (bf16[4,320,256]{2,1,0:T(8,128)(2,1)}, bf16[4,320,256]{2,1,0:T(8,128)(2,1)S(1)}, u32[]{:S(2)}) copy-start(bf16[4,320,256]{2,1,0:T(8,128)(2,1)S(1)} %all-to-all-done) | copy-start | bytes 1966084
  19.1 15.0 %collective-permute-start.2 = (bf16[256,256]{1,0:T(8,128)(2,1)S(1)}, bf16[256,256]{1,0:T(8,128)(2,1)S(1)}, u32[]{:S(2)}, u32[]{:S(2)}) collective-permute-start(bf16[256,256]{1,0:T(8,128)(2,1)S(1)} %bitcast.193), channel_id=1, source_target_pairs={{0,256},{256,0},{1,257},{257,1},{2,258},{258,2},{3,259},{259,3},{4... | collective-permute-start | bytes 393224 | tf_op jit(solution)/shard_map/ppermute | solution.py:25
  27.4 10.0 %collective-permute-start.1 = (bf16[128,512]{1,0:T(8,128)(2,1)S(1)}, bf16[128,512]{1,0:T(8,128)(2,1)S(1)}, u32[]{:S(2)}, u32[]{:S(2)}) collective-permute-start(bf16[128,512]{1,0:T(8,128)(2,1)S(1)} %bitcast.191), channel_id=1, source_target_pairs={{0,128},{128,0},{1,129},{129,1},{2,130},{130,2},{3,131},{131,3},{4... | collective-permute-start | bytes 393224 | tf_op jit(solution)/shard_map/ppermute | solution.py:25
  37.5 16.7 %collective-permute-start.3 = (bf16[256,512]{1,0:T(8,128)(2,1)S(1)}, bf16[256,512]{1,0:T(8,128)(2,1)S(1)}, u32[]{:S(2)}, u32[]{:S(2)}) collective-permute-start(bf16[256,512]{1,0:T(8,128)(2,1)S(1)} %bitcast.189), channel_id=1, source_target_pairs={{0,64},{64,0},{1,65},{65,1},{2,66},{66,2},{3,67},{67,3},{4,68},{68... | collective-permute-start | bytes 786440 | tf_op jit(solution)/shard_map/ppermute | solution.py:25
  45.9 10.2 %all-to-all-start.1 = ((s32[8,1,128]{2,1,0:T(1,128)}), s32[8,1,128]{2,1,0:T(1,128)S(1)}, u32[]{:S(2)}, u32[]{:S(2)}) async-start(s32[8,1,128]{2,1,0:T(1,128)} %broadcast_in_dim.8), calls=%async_computation.1 | async-start | bytes 8192 | tf_op jit(solution)/shard_map/all_to_all | solution.py:31
  51.6 16.3 %collective-permute-start.4 = (bf16[512,256]{1,0:T(8,128)(2,1)S(1)}, bf16[512,256]{1,0:T(8,128)(2,1)S(1)}, u32[]{:S(2)}, u32[]{:S(2)}) collective-permute-start(bf16[512,256]{1,0:T(8,128)(2,1)S(1)} %bitcast.187), channel_id=1, source_target_pairs={{0,128},{128,0},{1,129},{129,1},{2,130},{130,2},{3,131},{131,3},{4... | collective-permute-start | bytes 786440 | tf_op jit(solution)/shard_map/ppermute | solution.py:25
  57.6 34.7 %all-to-all-start.2 = ((bf16[4,512,512]{2,1,0:T(8,128)(2,1)}), bf16[4,512,512]{2,1,0:T(8,128)(2,1)S(1)}, u32[]{:S(2)}, u32[]{:S(2)}) async-start(bf16[4,512,512]{2,1,0:T(8,128)(2,1)} %broadcast_in_dim.9), calls=%async_computation.2 | async-start | bytes 4194304 | tf_op jit(solution)/shard_map/all_to_all | solution.py:31
  68.0 24.1 %collective-permute-start.5 = (bf16[1024,256]{1,0:T(8,128)(2,1)S(1)}, bf16[1024,256]{1,0:T(8,128)(2,1)S(1)}, u32[]{:S(2)}, u32[]{:S(2)}) collective-permute-start(bf16[1024,256]{1,0:T(8,128)(2,1)S(1)} %bitcast.184), channel_id=1, source_target_pairs={{0,64},{64,0},{1,65},{65,1},{2,66},{66,2},{3,67},{67,3},{4,68},{68... | collective-permute-start | bytes 1572872 | tf_op jit(solution)/shard_map/ppermute | solution.py:25
  70.0 22.1 %collective-permute-start.6 = (s32[8,128]{1,0:T(8,128)S(1)}, s32[8,128]{1,0:T(8,128)S(1)}, u32[]{:S(2)}, u32[]{:S(2)}) collective-permute-start(s32[8,128]{1,0:T(8,128)S(1)} %bitcast.197), channel_id=1, source_target_pairs={{0,8},{8,0},{1,9},{9,1},{2,10},{10,2},{3,11},{11,3},{4,12},{12,4},... | collective-permute-start | bytes 12296 | tf_op jit(solution)/shard_map/ppermute | solution.py:25
  94.2 1.1 copy-start.2
  98.1 12.7 %collective-permute-start.7 = (bf16[4,1024,256]{2,1,0:T(8,128)(2,1)}, bf16[4,1024,256]{2,1,0:T(8,128)(2,1)}, u32[]{:S(2)}, u32[]{:S(2)}) collective-permute-start(bf16[4,1024,256]{2,1,0:T(8,128)(2,1)} %pad_maximum_fusion), channel_id=1, source_target_pairs={{0,1},{1,0},{2,3},{3,2},{4,5},{5,4},{6,7},{7,6},{8,9},{9,8},{10,11... | collective-permute-start | bytes 6291464 | tf_op jit(solution)/shard_map/ppermute | solution.py:102
  101.7 19.4 %all-to-all-start.3 = ((bf16[8,2,128,256]{3,2,1,0:T(8,128)(2,1)}), bf16[8,2,128,256]{3,2,1,0:T(8,128)(2,1)}, u32[]{:S(2)}, u32[]{:S(2)}) async-start(bf16[8,2,128,256]{3,2,1,0:T(8,128)(2,1)} %bitcast.177), calls=%async_computation.3 | async-start | bytes 2097152 | tf_op jit(solution)/shard_map/all_to_all | solution.py:85
  121.1 32.0 %all-to-all-start.4 = ((bf16[16,2,128,256]{3,2,1,0:T(8,128)(2,1)}), bf16[16,2,128,256]{3,2,1,0:T(8,128)(2,1)}, u32[]{:S(2)}, u32[]{:S(2)}) async-start(bf16[16,2,128,256]{3,2,1,0:T(8,128)(2,1)} %bitcast.175), calls=%async_computation.4 | async-start | bytes 4194304 | tf_op jit(solution)/shard_map/all_to_all | solution.py:35
  127.9 24.0 %collective-permute-start.8 = (bf16[2,128,256]{2,1,0:T(8,128)(2,1)S(1)}, bf16[2,128,256]{2,1,0:T(8,128)(2,1)S(1)}, u32[]{:S(2)}, u32[]{:S(2)}) collective-permute-start(bf16[2,128,256]{2,1,0:T(8,128)(2,1)S(1)} %convert_element_type.142), channel_id=1, source_target_pairs={{0,8},{8,0},{1,9},{9,1},{2,10},{10,2},{3,11},{11,3},{4,12},{12,4},... | collective-permute-start | bytes 393224 | tf_op jit(solution)/shard_map/ppermute | solution.py:47
  155.0 14.5 %collective-permute-start.9 = (bf16[2,128,256]{2,1,0:T(8,128)(2,1)S(1)}, bf16[2,128,256]{2,1,0:T(8,128)(2,1)S(1)}, u32[]{:S(2)}, u32[]{:S(2)}) collective-permute-start(bf16[2,128,256]{2,1,0:T(8,128)(2,1)S(1)} %convert_element_type.144), channel_id=1, source_target_pairs={{0,8},{8,0},{1,9},{9,1},{2,10},{10,2},{3,11},{11,3},{4,12},{12,4},... | collective-permute-start | bytes 393224 | tf_op jit(solution)/shard_map/ppermute | solution.py:47
  195.6 24.4 %all-to-all-start.6 = ((bf16[8,256,256]{2,1,0:T(8,128)(2,1)}), bf16[8,256,256]{2,1,0:T(8,128)(2,1)S(1)}, u32[]{:S(2)}, u32[]{:S(2)}) async-start(bf16[8,256,256]{2,1,0:T(8,128)(2,1)} %broadcast_in_dim.11), calls=%async_computation.6 | async-start | bytes 2097152 | tf_op jit(solution)/shard_map/all_to_all | solution.py:31

commit v7 on v5

--- a/solution.py
+++ b/solution.py
@@ -71,12 +71,13 @@
     teacher = quarters[:, :rows].reshape(4 * rows, part_width)
     weights = quarters[:, rows:]
     student, teacher, orders = together(
-        swap_in(student, "z1"), swap_in(teacher, "z2"), owner_order
+        swap_in(student, "z1"), swap_in(teacher, "z2"), swap_in(owner_order[None], "zh")
     )
     student, orders = together(swap_in(student, "z0"), spread(orders, YC))
     student_all, teacher, orders = together(
-        spread(student, "x"), swap_in(swap_in(teacher, "z1"), "z0"), swap_in(orders, "zh")
+        spread(student, "x"), swap_in(swap_in(teacher, "z1"), "z0"), orders
     )
+    orders = orders.transpose(1, 0, 2).reshape(groups, block)
     student_all = student_all.reshape(total_rows, student_width)
     student_part = jnp.dot(student_all, projection, preferred_element_type=F32).astype(BF16)
     student_part = student_part.reshape(2, 2, 2, 2, 2, rows, out_width)

time: 218 us -> 221 us (1.014)
  waiting for transfers between devices: 54.5 us -> 71.2 us
  starting transfers between devices: 99.3 us -> 85.1 us
    ppermute x8, starting transfers between devices: 56.2 us -> 41.1 us  [swap_in(): return in_order(value, lax.ppermute(value, axis, SWAP), axis)]
    all_to_all x2, waiting for transfers between devices: 1.87 us -> 15.2 us  [spread(): return lax.all_to_all(copies, axis, split_axis=0, concat_axis=0, tiled=True)]
    all_to_all x1, waiting for transfers between devices: 1.05 us -> 12.1 us  [summed(): part = lax.all_to_all(pieces, axis, split_axis=0, concat_axis=0, tiled=True)]
    ppermute x2, waiting for transfers between devices: 23 us -> 13.2 us  [both_owners(): other = lax.ppermute(part.astype(BF16), 'zh', SWAP)]
  transfers between devices with their start and end apart: 16 -> 16, of which waited for: 10 -> 9; matrix products, arithmetic and copies ran while one was open for 6% -> 6% of each run, Pallas kernels for 0% -> 0%
where the time goes in v7:
time: 221 us; the launch traced here: 220 us
  starting transfers between devices  85.1 us (39%)
  waiting for transfers between devices  71.2 us (32%)
  blocking collectives  36.5 us (17%)
  other arithmetic  11.8 us (5%)
  matrix products  8.73 us (4%)
  local copies, waits for them, and re-layouts  5.53 us (3%)
    ppermute x8, starting transfers between devices, swap_in(): return in_order(value, lax.ppermute(value, axis, SWAP), axis)  41.1 us
    all_to_all x2, blocking collectives, spread(): return lax.all_to_all(copies, axis, split_axis=0, concat_axis=0, tiled=True)  36.5 us
    ppermute x8, waiting for transfers between devices, swap_in(): return in_order(value, lax.ppermute(value, axis, SWAP), axis)  24.1 us
    ppermute x2, starting transfers between devices, both_owners(): other = lax.ppermute(part.astype(BF16), 'zh', SWAP)  16.3 us
    all_to_all x2, waiting for transfers between devices, spread(): return lax.all_to_all(copies, axis, split_axis=0, concat_axis=0, tiled=True)  15.2 us
    ppermute x2, waiting for transfers between devices, both_owners(): other = lax.ppermute(part.astype(BF16), 'zh', SWAP)  13.2 us
    all_to_all x1, waiting for transfers between devices, summed(): part = lax.all_to_all(pieces, axis, split_axis=0, concat_axis=0, tiled=True)  12.1 us
    all_to_all x2, starting transfers between devices, spread(): return lax.all_to_all(copies, axis, split_axis=0, concat_axis=0, tiled=True)  10.4 us
  transfers between devices with their start and end apart: 16, of which 9 were waited for; matrix products, arithmetic and copies ran while one was open for 6% of the time, Pallas kernels for 0%

profile of v7, /device:TPU:1, one launch (start us, length us, event | category | flops | bytes accessed | tf_op | source)
XLA Modules:
  0.0 220.0 jit_solution(8656826303123880125)
XLA Ops:
  3.6 4.8 %all-to-all-start = ((bf16[4,320,256]{2,1,0:T(8,128)(2,1)}), bf16[4,320,256]{2,1,0:T(8,128)(2,1)S(1)}, u32[]{:S(2)}, u32[]{:S(2)}) async-start(bf16[4,320,256]{2,1,0:T(8,128)(2,1)} %pad_maximum_fusion.3), calls=%async_computation | async-start | bytes 1310720 | tf_op jit(solution)/shard_map/all_to_all | solution.py:69
  8.4 8.8 %collective-permute-start = (bf16[64,512]{1,0:T(8,128)(2,1)S(1)}, bf16[64,512]{1,0:T(8,128)(2,1)S(1)}, u32[]{:S(2)}, u32[]{:S(2)}) collective-permute-start(bf16[64,512]{1,0:T(8,128)(2,1)S(1)} %copy-done.3), channel_id=1, source_target_pairs={{0,256},{256,0},{1,257},{257,1},{2,258},{258,2},{3,259},{259,3},{4... | collective-permute-start | bytes 196616 | tf_op jit(solution)/shard_map/ppermute | solution.py:25
  17.2 10.6 %collective-permute-start.3 = (s32[1,128]{1,0:T(1,128)S(1)}, s32[1,128]{1,0:T(1,128)S(1)}, u32[]{:S(2)}, u32[]{:S(2)}) collective-permute-start(s32[1,128]{1,0:T(1,128)S(1)} %bitcast.217), channel_id=1, source_target_pairs={{0,8},{8,0},{1,9},{9,1},{2,10},{10,2},{3,11},{11,3},{4,12},{12,4},... | collective-permute-start | bytes 1544 | tf_op jit(solution)/shard_map/ppermute | solution.py:25
  28.0 5.2 %collective-permute-start.2 = (bf16[256,256]{1,0:T(8,128)(2,1)S(1)}, bf16[256,256]{1,0:T(8,128)(2,1)S(1)}, u32[]{:S(2)}, u32[]{:S(2)}) collective-permute-start(bf16[256,256]{1,0:T(8,128)(2,1)S(1)} %bitcast.205), channel_id=1, source_target_pairs={{0,256},{256,0},{1,257},{257,1},{2,258},{258,2},{3,259},{259,3},{4... | collective-permute-start | bytes 393224 | tf_op jit(solution)/shard_map/ppermute | solution.py:25
  33.2 3.1 %collective-permute-start.1 = (bf16[128,512]{1,0:T(8,128)(2,1)S(1)}, bf16[128,512]{1,0:T(8,128)(2,1)S(1)}, u32[]{:S(2)}, u32[]{:S(2)}) collective-permute-start(bf16[128,512]{1,0:T(8,128)(2,1)S(1)} %bitcast.203), channel_id=1, source_target_pairs={{0,128},{128,0},{1,129},{129,1},{2,130},{130,2},{3,131},{131,3},{4... | collective-permute-start | bytes 393224 | tf_op jit(solution)/shard_map/ppermute | solution.py:25
  36.3 10.9 %collective-permute-done.2 = bf16[256,256]{1,0:T(8,128)(2,1)S(1)} collective-permute-done((bf16[256,256]{1,0:T(8,128)(2,1)S(1)}, bf16[256,256]{1,0:T(8,128)(2,1)S(1)}, u32[]{:S(2)}, u32[]{:S(2)}) %collective-permute-start.2) | collective-permute-done | bytes 131104 | tf_op jit(solution)/shard_map/ppermute | solution.py:25
  49.3 2.8 %collective-permute-start.5 = (bf16[512,256]{1,0:T(8,128)(2,1)S(1)}, bf16[512,256]{1,0:T(8,128)(2,1)S(1)}, u32[]{:S(2)}, u32[]{:S(2)}) collective-permute-start(bf16[512,256]{1,0:T(8,128)(2,1)S(1)} %bitcast.199), channel_id=1, source_target_pairs={{0,128},{128,0},{1,129},{129,1},{2,130},{130,2},{3,131},{131,3},{4... | collective-permute-start | bytes 786440 | tf_op jit(solution)/shard_map/ppermute | solution.py:25
  52.7 6.3 %all-to-all-start.1 = ((s32[8,2,128]{2,1,0:T(2,128)}), s32[8,2,128]{2,1,0:T(2,128)S(1)}, u32[]{:S(2)}, u32[]{:S(2)}) async-start(s32[8,2,128]{2,1,0:T(2,128)} %broadcast_in_dim.13), calls=%async_computation.1 | async-start | bytes 16384 | tf_op jit(solution)/shard_map/all_to_all | solution.py:31
  59.2 4.5 %all-to-all-done.1 = s32[8,2,128]{2,1,0:T(2,128)S(1)} async-done(((s32[8,2,128]{2,1,0:T(2,128)}), s32[8,2,128]{2,1,0:T(2,128)S(1)}, u32[]{:S(2)}, u32[]{:S(2)}) %all-to-all-start.1) | async-done | bytes 8224 | tf_op jit(solution)/shard_map/all_to_all | solution.py:31
  65.2 4.0 %all-to-all-start.2 = ((bf16[4,512,512]{2,1,0:T(8,128)(2,1)}), bf16[4,512,512]{2,1,0:T(8,128)(2,1)S(1)}, u32[]{:S(2)}, u32[]{:S(2)}) async-start(bf16[4,512,512]{2,1,0:T(8,128)(2,1)} %broadcast_in_dim.14), calls=%async_computation.2 | async-start | bytes 4194304 | tf_op jit(solution)/shard_map/all_to_all | solution.py:31
  71.4 12.3 %collective-permute-done.6 = bf16[1024,256]{1,0:T(8,128)(2,1)S(1)} collective-permute-done((bf16[1024,256]{1,0:T(8,128)(2,1)S(1)}, bf16[1024,256]{1,0:T(8,128)(2,1)S(1)}, u32[]{:S(2)}, u32[]{:S(2)}) %collective-permute-start.6) | collective-permute-done | bytes 524320 | tf_op jit(solution)/shard_map/ppermute | solution.py:25
  83.9 10.7 %all-to-all-done.2 = bf16[4,512,512]{2,1,0:T(8,128)(2,1)S(1)} async-done(((bf16[4,512,512]{2,1,0:T(8,128)(2,1)}), bf16[4,512,512]{2,1,0:T(8,128)(2,1)S(1)}, u32[]{:S(2)}, u32[]{:S(2)}) %all-to-all-start.2) | async-done | bytes 2097184 | tf_op jit(solution)/shard_map/all_to_all | solution.py:31
  100.3 3.8 %collective-permute-start.7 = (bf16[4,1024,256]{2,1,0:T(8,128)(2,1)}, bf16[4,1024,256]{2,1,0:T(8,128)(2,1)}, u32[]{:S(2)}, u32[]{:S(2)}) collective-permute-start(bf16[4,1024,256]{2,1,0:T(8,128)(2,1)} %pad_maximum_fusion), channel_id=1, source_target_pairs={{0,1},{1,0},{2,3},{3,2},{4,5},{5,4},{6,7},{7,6},{8,9},{9,8},{10,11... | collective-permute-start | bytes 6291464 | tf_op jit(solution)/shard_map/ppermute | solution.py:103
  104.1 4.2 %all-to-all-start.3 = ((bf16[8,2,128,256]{3,2,1,0:T(8,128)(2,1)}), bf16[8,2,128,256]{3,2,1,0:T(8,128)(2,1)}, u32[]{:S(2)}, u32[]{:S(2)}) async-start(bf16[8,2,128,256]{3,2,1,0:T(8,128)(2,1)} %bitcast.187), calls=%async_computation.3 | async-start | bytes 2097152 | tf_op jit(solution)/shard_map/all_to_all | solution.py:86
  116.9 6.6 %all-to-all-done.3 = bf16[8,2,128,256]{3,2,1,0:T(8,128)(2,1)} async-done(((bf16[8,2,128,256]{3,2,1,0:T(8,128)(2,1)}), bf16[8,2,128,256]{3,2,1,0:T(8,128)(2,1)}, u32[]{:S(2)}, u32[]{:S(2)}) %all-to-all-start.3) | async-done | bytes 1048608 | tf_op jit(solution)/shard_map/all_to_all | solution.py:86
  123.5 4.4 %all-to-all-start.4 = ((bf16[16,2,128,256]{3,2,1,0:T(8,128)(2,1)}), bf16[16,2,128,256]{3,2,1,0:T(8,128)(2,1)}, u32[]{:S(2)}, u32[]{:S(2)}) async-start(bf16[16,2,128,256]{3,2,1,0:T(8,128)(2,1)} %bitcast.185), calls=%async_computation.4 | async-start | bytes 4194304 | tf_op jit(solution)/shard_map/all_to_all | solution.py:35
  129.4 8.2 %collective-permute-start.8 = (bf16[2,128,256]{2,1,0:T(8,128)(2,1)S(1)}, bf16[2,128,256]{2,1,0:T(8,128)(2,1)S(1)}, u32[]{:S(2)}, u32[]{:S(2)}) collective-permute-start(bf16[2,128,256]{2,1,0:T(8,128)(2,1)S(1)} %convert_element_type.142), channel_id=1, source_target_pairs={{0,8},{8,0},{1,9},{9,1},{2,10},{10,2},{3,11},{11,3},{4,12},{12,4},... | collective-permute-start | bytes 393224 | tf_op jit(solution)/shard_map/ppermute | solution.py:47
  137.5 6.6 %collective-permute-done.8 = bf16[2,128,256]{2,1,0:T(8,128)(2,1)S(1)} collective-permute-done((bf16[2,128,256]{2,1,0:T(8,128)(2,1)S(1)}, bf16[2,128,256]{2,1,0:T(8,128)(2,1)S(1)}, u32[]{:S(2)}, u32[]{:S(2)}) %collective-permute-start.8) | collective-permute-done | bytes 131104 | tf_op jit(solution)/shard_map/ppermute | solution.py:47
  144.2 12.1 %all-to-all-done.4 = bf16[16,2,128,256]{3,2,1,0:T(8,128)(2,1)} async-done(((bf16[16,2,128,256]{3,2,1,0:T(8,128)(2,1)}), bf16[16,2,128,256]{3,2,1,0:T(8,128)(2,1)}, u32[]{:S(2)}, u32[]{:S(2)}) %all-to-all-start.4) | async-done | bytes 2097184 | tf_op jit(solution)/shard_map/all_to_all | solution.py:35
  158.2 8.2 %collective-permute-start.9 = (bf16[2,128,256]{2,1,0:T(8,128)(2,1)S(1)}, bf16[2,128,256]{2,1,0:T(8,128)(2,1)S(1)}, u32[]{:S(2)}, u32[]{:S(2)}) collective-permute-start(bf16[2,128,256]{2,1,0:T(8,128)(2,1)S(1)} %convert_element_type.144), channel_id=1, source_target_pairs={{0,8},{8,0},{1,9},{9,1},{2,10},{10,2},{3,11},{11,3},{4,12},{12,4},... | collective-permute-start | bytes 393224 | tf_op jit(solution)/shard_map/ppermute | solution.py:47
  166.4 6.5 %collective-permute-done.9 = bf16[2,128,256]{2,1,0:T(8,128)(2,1)S(1)} collective-permute-done((bf16[2,128,256]{2,1,0:T(8,128)(2,1)S(1)}, bf16[2,128,256]{2,1,0:T(8,128)(2,1)S(1)}, u32[]{:S(2)}, u32[]{:S(2)}) %collective-permute-start.9) | collective-permute-done | bytes 131104 | tf_op jit(solution)/shard_map/ppermute | solution.py:47
  173.3 21.7 %all_to_all.35 = f32[32,3,256]{2,1,0:T(4,128)S(1)} all-to-all(f32[32,3,256]{2,1,0:T(4,128)S(1)} %broadcast_in_dim.15), channel_id=1, replica_groups=mesh['z2'=2,'z1'=2,'z0'=2,'x'=4,'zh'=2,'y1'=2,'y0'=2,'c'=2] {'z2','z1','..., dimensions={0} | all-to-all | bytes 196608 | tf_op jit(solution)/shard_map/all_to_all | solution.py:31
  195.2 14.8 %all_to_all.36 = bf16[4,256,256]{2,1,0:T(8,128)(2,1)S(1)} all-to-all(bf16[4,256,256]{2,1,0:T(8,128)(2,1)S(1)} %broadcast_in_dim.16), channel_id=1, replica_groups=mesh['z2'=2,'z1'=2,'z0'=2,'x'=4,'zh'=2,'y1'=2,'y0'=2,'c'=2] {'y1','y0'}, dimensions={0} | all-to-all | bytes 1048576 | tf_op jit(solution)/shard_map/all_to_all | solution.py:31
  210.0 6.6 %collective-permute-start.10 = (bf16[1,4,256,256]{3,2,1,0:T(8,128)(2,1)S(1)}, bf16[1,4,256,256]{3,2,1,0:T(8,128)(2,1)S(1)}, u32[]{:S(2)}, u32[]{:S(2)}) collective-permute-start(bf16[1,4,256,256]{3,2,1,0:T(8,128)(2,1)S(1)} %bitcast.193), channel_id=1, source_target_pairs={{0,1},{1,0},{2,3},{3,2},{4,5},{5,4},{6,7},{7,6},{8,9},{9,8},{10,11... | collective-permute-start | bytes 1572872 | tf_op jit(solution)/shard_map/ppermute | solution.py:25
  (75 shorter events, 31.0 us)
Async XLA Ops:
  0.6 94.0 %copy-start = (bf16[512,256]{1,0:T(8,128)(2,1)S(1)}, bf16[512,256]{1,0:T(8,128)(2,1)}, u32[]{:S(2)}) copy-start(bf16[512,256]{1,0:T(8,128)(2,1)} %param.8) | copy-start | bytes 786436
  0.6 7.8 %copy-start.3 = (bf16[64,512]{1,0:T(8,128)(2,1)S(1)}, bf16[64,512]{1,0:T(8,128)(2,1)}, u32[]{:S(2)}) copy-start(bf16[64,512]{1,0:T(8,128)(2,1)} %param.7) | copy-start | bytes 196612
  0.7 16.6 %copy-start.4 = (s32[128]{0:T(128)S(1)}, s32[128]{0:T(128)}, u32[]{:S(2)}) copy-start(s32[128]{0:T(128)} %param.9) | copy-start | bytes 1540
  3.6 24.4 %all-to-all-start = ((bf16[4,320,256]{2,1,0:T(8,128)(2,1)}), bf16[4,320,256]{2,1,0:T(8,128)(2,1)S(1)}, u32[]{:S(2)}, u32[]{:S(2)}) async-start(bf16[4,320,256]{2,1,0:T(8,128)(2,1)} %pad_maximum_fusion.3), calls=%async_computation | async-start | bytes 1310720 | tf_op jit(solution)/shard_map/all_to_all | solution.py:69
  8.4 19.5 %collective-permute-start = (bf16[64,512]{1,0:T(8,128)(2,1)S(1)}, bf16[64,512]{1,0:T(8,128)(2,1)S(1)}, u32[]{:S(2)}, u32[]{:S(2)}) collective-permute-start(bf16[64,512]{1,0:T(8,128)(2,1)S(1)} %copy-done.3), channel_id=1, source_target_pairs={{0,256},{256,0},{1,257},{257,1},{2,258},{258,2},{3,259},{259,3},{4... | collective-permute-start | bytes 196616 | tf_op jit(solution)/shard_map/ppermute | solution.py:25
  17.2 15.9 %collective-permute-start.3 = (s32[1,128]{1,0:T(1,128)S(1)}, s32[1,128]{1,0:T(1,128)S(1)}, u32[]{:S(2)}, u32[]{:S(2)}) collective-permute-start(s32[1,128]{1,0:T(1,128)S(1)} %bitcast.217), channel_id=1, source_target_pairs={{0,8},{8,0},{1,9},{9,1},{2,10},{10,2},{3,11},{11,3},{4,12},{12,4},... | collective-permute-start | bytes 1544 | tf_op jit(solution)/shard_map/ppermute | solution.py:25
  28.0 31.2 %copy-start.1 = (bf16[4,320,256]{2,1,0:T(8,128)(2,1)}, bf16[4,320,256]{2,1,0:T(8,128)(2,1)S(1)}, u32[]{:S(2)}) copy-start(bf16[4,320,256]{2,1,0:T(8,128)(2,1)S(1)} %all-to-all-done) | copy-start | bytes 1966084
  28.0 19.2 %collective-permute-start.2 = (bf16[256,256]{1,0:T(8,128)(2,1)S(1)}, bf16[256,256]{1,0:T(8,128)(2,1)S(1)}, u32[]{:S(2)}, u32[]{:S(2)}) collective-permute-start(bf16[256,256]{1,0:T(8,128)(2,1)S(1)} %bitcast.205), channel_id=1, source_target_pairs={{0,256},{256,0},{1,257},{257,1},{2,258},{258,2},{3,259},{259,3},{4... | collective-permute-start | bytes 393224 | tf_op jit(solution)/shard_map/ppermute | solution.py:25
  33.2 14.1 %collective-permute-start.1 = (bf16[128,512]{1,0:T(8,128)(2,1)S(1)}, bf16[128,512]{1,0:T(8,128)(2,1)S(1)}, u32[]{:S(2)}, u32[]{:S(2)}) collective-permute-start(bf16[128,512]{1,0:T(8,128)(2,1)S(1)} %bitcast.203), channel_id=1, source_target_pairs={{0,128},{128,0},{1,129},{129,1},{2,130},{130,2},{3,131},{131,3},{4... | collective-permute-start | bytes 393224 | tf_op jit(solution)/shard_map/ppermute | solution.py:25
  47.3 11.7 %collective-permute-start.4 = (bf16[256,512]{1,0:T(8,128)(2,1)S(1)}, bf16[256,512]{1,0:T(8,128)(2,1)S(1)}, u32[]{:S(2)}, u32[]{:S(2)}) collective-permute-start(bf16[256,512]{1,0:T(8,128)(2,1)S(1)} %bitcast.201), channel_id=1, source_target_pairs={{0,64},{64,0},{1,65},{65,1},{2,66},{66,2},{3,67},{67,3},{4,68},{68... | collective-permute-start | bytes 786440 | tf_op jit(solution)/shard_map/ppermute | solution.py:25
  49.3 19.9 %collective-permute-start.5 = (bf16[512,256]{1,0:T(8,128)(2,1)S(1)}, bf16[512,256]{1,0:T(8,128)(2,1)S(1)}, u32[]{:S(2)}, u32[]{:S(2)}) collective-permute-start(bf16[512,256]{1,0:T(8,128)(2,1)S(1)} %bitcast.199), channel_id=1, source_target_pairs={{0,128},{128,0},{1,129},{129,1},{2,130},{130,2},{3,131},{131,3},{4... | collective-permute-start | bytes 786440 | tf_op jit(solution)/shard_map/ppermute | solution.py:25
  52.7 11.0 %all-to-all-start.1 = ((s32[8,2,128]{2,1,0:T(2,128)}), s32[8,2,128]{2,1,0:T(2,128)S(1)}, u32[]{:S(2)}, u32[]{:S(2)}) async-start(s32[8,2,128]{2,1,0:T(2,128)} %broadcast_in_dim.13), calls=%async_computation.1 | async-start | bytes 16384 | tf_op jit(solution)/shard_map/all_to_all | solution.py:31
  65.2 29.4 %all-to-all-start.2 = ((bf16[4,512,512]{2,1,0:T(8,128)(2,1)}), bf16[4,512,512]{2,1,0:T(8,128)(2,1)S(1)}, u32[]{:S(2)}, u32[]{:S(2)}) async-start(bf16[4,512,512]{2,1,0:T(8,128)(2,1)} %broadcast_in_dim.14), calls=%async_computation.2 | async-start | bytes 4194304 | tf_op jit(solution)/shard_map/all_to_all | solution.py:31
  69.3 14.3 %collective-permute-start.6 = (bf16[1024,256]{1,0:T(8,128)(2,1)S(1)}, bf16[1024,256]{1,0:T(8,128)(2,1)S(1)}, u32[]{:S(2)}, u32[]{:S(2)}) collective-permute-start(bf16[1024,256]{1,0:T(8,128)(2,1)S(1)} %bitcast.194), channel_id=1, source_target_pairs={{0,64},{64,0},{1,65},{65,1},{2,66},{66,2},{3,67},{67,3},{4,68},{68... | collective-permute-start | bytes 1572872 | tf_op jit(solution)/shard_map/ppermute | solution.py:25
  96.4 1.1 copy-start.2
  100.3 12.9 %collective-permute-start.7 = (bf16[4,1024,256]{2,1,0:T(8,128)(2,1)}, bf16[4,1024,256]{2,1,0:T(8,128)(2,1)}, u32[]{:S(2)}, u32[]{:S(2)}) collective-permute-start(bf16[4,1024,256]{2,1,0:T(8,128)(2,1)} %pad_maximum_fusion), channel_id=1, source_target_pairs={{0,1},{1,0},{2,3},{3,2},{4,5},{5,4},{6,7},{7,6},{8,9},{9,8},{10,11... | collective-permute-start | bytes 6291464 | tf_op jit(solution)/shard_map/ppermute | solution.py:103
  104.1 19.4 %all-to-all-start.3 = ((bf16[8,2,128,256]{3,2,1,0:T(8,128)(2,1)}), bf16[8,2,128,256]{3,2,1,0:T(8,128)(2,1)}, u32[]{:S(2)}, u32[]{:S(2)}) async-start(bf16[8,2,128,256]{3,2,1,0:T(8,128)(2,1)} %bitcast.187), calls=%async_computation.3 | async-start | bytes 2097152 | tf_op jit(solution)/shard_map/all_to_all | solution.py:86
  123.5 32.7 %all-to-all-start.4 = ((bf16[16,2,128,256]{3,2,1,0:T(8,128)(2,1)}), bf16[16,2,128,256]{3,2,1,0:T(8,128)(2,1)}, u32[]{:S(2)}, u32[]{:S(2)}) async-start(bf16[16,2,128,256]{3,2,1,0:T(8,128)(2,1)} %bitcast.185), calls=%async_computation.4 | async-start | bytes 4194304 | tf_op jit(solution)/shard_map/all_to_all | solution.py:35
  129.4 14.8 %collective-permute-start.8 = (bf16[2,128,256]{2,1,0:T(8,128)(2,1)S(1)}, bf16[2,128,256]{2,1,0:T(8,128)(2,1)S(1)}, u32[]{:S(2)}, u32[]{:S(2)}) collective-permute-start(bf16[2,128,256]{2,1,0:T(8,128)(2,1)S(1)} %convert_element_type.142), channel_id=1, source_target_pairs={{0,8},{8,0},{1,9},{9,1},{2,10},{10,2},{3,11},{11,3},{4,12},{12,4},... | collective-permute-start | bytes 393224 | tf_op jit(solution)/shard_map/ppermute | solution.py:47
  158.2 14.7 %collective-permute-start.9 = (bf16[2,128,256]{2,1,0:T(8,128)(2,1)S(1)}, bf16[2,128,256]{2,1,0:T(8,128)(2,1)S(1)}, u32[]{:S(2)}, u32[]{:S(2)}) collective-permute-start(bf16[2,128,256]{2,1,0:T(8,128)(2,1)S(1)} %convert_element_type.144), channel_id=1, source_target_pairs={{0,8},{8,0},{1,9},{9,1},{2,10},{10,2},{3,11},{11,3},{4,12},{12,4},... | collective-permute-start | bytes 393224 | tf_op jit(solution)/shard_map/ppermute | solution.py:47
  210.0 8.1 %collective-permute-start.10 = (bf16[1,4,256,256]{3,2,1,0:T(8,128)(2,1)S(1)}, bf16[1,4,256,256]{3,2,1,0:T(8,128)(2,1)S(1)}, u32[]{:S(2)}, u32[]{:S(2)}) collective-permute-start(bf16[1,4,256,256]{3,2,1,0:T(8,128)(2,1)S(1)} %bitcast.193), channel_id=1, source_target_pairs={{0,1},{1,0},{2,3},{3,2},{4,5},{5,4},{6,7},{7,6},{8,9},{9,8},{10,11... | collective-permute-start | bytes 1572872 | tf_op jit(solution)/shard_map/ppermute | solution.py:25
